TPU v7x, 32 devices: a whole 2x2x4 slice. The times are simulated.
32 devices in a mesh: slab: 2 (over y), ex: 4 (over z), lay: 2 (over x), pb: 2 (over core).
Axes of the slice: x: 2, y: 2, z: 4, core: 2. Of those that a mesh axis runs over, the one named last changes fastest.
Arguments:
- store_grads: bfloat16 [2, 4096, 4096], P('lay', ('slab', 'ex')), parts along dimension 1, may hold values from -0.0625 to 0.0625
- query_grads: bfloat16 [2, 384, 4096], P('lay', ('pb', 'ex')), may hold values from -6 to 6
- query_block: int32 [384], replicated, may hold values from 0 to 3
- layer_slot: int32 [2], replicated, may hold values from 0 to 1, each once
- out_basis: bfloat16 [2, 64, 64], replicated, may hold values from -0.75 to 0.75
- in_basis: bfloat16 [2, 64, 64], replicated, may hold values from -0.75 to 0.75
- eigen_values: float32 [2, 64, 64], replicated, may hold values from 0.05 to 5
- damping: float32 [4], replicated, may hold values from 0.1 to 1
Outputs:
- scores: float32 [4096, 384], P(('slab', 'ex', 'lay'), 'pb'), parts along dimension 0
There are 2 independent parts, one for each index of `slab`. A program takes and returns all parts, laid end to end along the dimension named above; an argument that names none is the same for every part. Nothing has to cross between parts.
Inputs may be any that keep to these rules, and one draw needn't show every extreme that they name: `layer_slot`: a permutation of the 2 model layers.
All inputs are finite; a program needn't handle non-finite values.
Results may differ from a plain program's by a relative error of at most 0.003.
Values may be sent and summed in bfloat16 or wider, within the bound.
No kernel may reach another device: no remote copies, remote signals or barrier semaphores. Data moves between devices by JAX's collectives and lax.ppermute only.
A program may use at most 64 MiB of HBM per device.

v0:
```python
import jax
import jax.numpy as jnp
from jax import lax
from jax.sharding import PartitionSpec as P

OUT_RANK = 64
IN_RANK = 64
BLOCKS = 4


HIGHEST = lax.Precision.HIGHEST


def lookup_damping(block_ids, damping):
    hits = block_ids[:, None] == jnp.arange(BLOCKS, dtype=jnp.int32)[None, :]
    return jnp.sum(jnp.where(hits, damping[None, :], jnp.float32(0.0)), axis=1)


def rotate(block_rows, out_factor, in_factor, eigen_layer, damp_rows):
    count_rows = block_rows.shape[0]
    grid_rows = block_rows.astype(jnp.float32).reshape(count_rows, OUT_RANK, IN_RANK)
    left_side = jnp.einsum("ap,nai->npi", out_factor, grid_rows, precision=HIGHEST)
    middle = jnp.einsum("npi,iq->npq", left_side, in_factor, precision=HIGHEST)
    scaled = middle / (eigen_layer[None] + damp_rows[:, None, None])
    turned = jnp.einsum("ap,npq->naq", out_factor, scaled, precision=HIGHEST)
    result = jnp.einsum("naq,bq->nab", turned, in_factor, precision=HIGHEST)
    return result.reshape(count_rows, OUT_RANK * IN_RANK).astype(jnp.bfloat16)


def local(
    store_grads, query_grads, query_block, layer_slot, out_basis, in_basis, eigen_values, damping
):
    slots = store_grads.shape[0]
    local_count = query_grads.shape[1]
    members = lax.axis_size("ex")
    per_half = local_count * members
    half_start = lax.axis_index("pb") * per_half
    model_layer = layer_slot[lax.axis_index("lay") * slots + 0]
    factors = (
        out_basis[model_layer].astype(jnp.float32),
        in_basis[model_layer].astype(jnp.float32),
        eigen_values[model_layer],
    )
    count_rows = query_grads.shape[1]
    block_ids = lax.dynamic_slice_in_dim(
        query_block, half_start + lax.axis_index("ex") * local_count, count_rows
    )
    damp_rows = lookup_damping(block_ids, damping)
    sendable = jnp.stack([rotate(query_grads[0], factors[0], factors[1], factors[2], damp_rows)])
    rotated = lax.all_gather(sendable, "ex", axis=1, tiled=True)
    summed = jnp.einsum("ed,qd->eq", store_grads[0], rotated[0], preferred_element_type=jnp.float32)
    scores = lax.psum_scatter(summed, "lay", scatter_dimension=0, tiled=True)
    return scores


def solution(mesh):
    return jax.shard_map(
        local,
        mesh=mesh,
        in_specs=(
            P("lay", ("slab", "ex"), None),
            P("lay", ("pb", "ex"), None),
            P(),
            P(),
            P(),
            P(),
            P(),
            P(),
        ),
        out_specs=P(("slab", "ex", "lay"), "pb"),
        check_vma=False,
    )
```

profile of v0, /device:TPU:0, one launch (start us, length us, event | category | flops | bytes accessed | tf_op | source)
XLA Modules:
  0.0 82.5 jit_solution(11972059101755422913)
XLA Ops:
  6.5 0.0 copy-start
  6.5 0.0 all-gather.2.cloned.1.call-start
  6.5 1.3 %dynamic_slice.15 = s32[1]{0:T(128)} dynamic-slice(s32[2]{0:T(128)} %param.11, s32[]{:T(128)S(6)} %select_n.15), dynamic_slice_sizes={1} | dynamic-slice | bytes 12 | tf_op jit(solution)/shard_map/dynamic_slice | solution.py:38
  9.1 0.0 copy-start.1
  9.1 1.8 %reshape.19 = bf16[48,64,64]{2,1,0:T(8,128)(2,1)S(1)} reshape(bf16[1,48,4096]{2,1,0:T(8,128)(2,1)} %param.9) | data formatting | bytes 786432 | tf_op jit(solution)/shard_map/reshape | solution.py:21
  11.6 0.8 dynamic_slice.19
  12.3 0.7 select_reduce_fusion
  13.1 0.0 copy-done
  13.1 1.1 %fusion.23 = f32[64,48,64]{2,0,1:T(8,128)S(1)} fusion(bf16[48,64,64]{2,1,0:T(8,128)(2,1)S(1)} %reshape.19, bf16[2,64,64]{2,1,0:T(8,128)(2,1)} %param.12, s32[]{:T(128)S(6)} %select_n.16), kind=kOutput, calls=%fused_computation.18 | convolution fusion | flops 25165824 | bytes 1196036 | tf_op jit(solution)/shard_map/ap,nai->npi/dot_general | solution.py:22
  14.2 0.0 copy-done.1
  14.2 0.0 copy-start.2
  14.2 0.9 %fusion.5 = f32[48,64,64]{2,1,0:T(8,128)S(1)} fusion(f32[64,48,64]{2,0,1:T(8,128)S(1)} %fusion.23, bf16[2,64,64]{2,1,0:T(8,128)(2,1)S(1)} %copy-done.1, s32[]{:T(128)S(6)} %select_n.16), kind=kOutput, calls=%fused_computation.5 | convolution fusion | flops 150994944 | bytes 2375684 | tf_op jit(solution)/shard_map/npi,iq->npq/dot_general | solution.py:23
  15.1 0.0 copy-done.2
  15.1 1.2 %fusion.7 = f32[48,64,64]{1,2,0:T(8,128)S(1)} fusion(f32[48,64,64]{2,1,0:T(8,128)S(1)} %fusion.5, f32[48]{0:T(128)S(1)} %select_reduce_fusion, f32[64,64]{1,0:T(8,128)S(1)} %dynamic-slice_bitcast_fusion, bf16[2,64,64]{2,1,0:T(8,128)(2,1)S(1)} %copy-done.2, s32[]{:T(128)S(6)} %select_n.16), kind=kOutput, calls=%fused_computation.7 | convolution fusion | flops 151388160 | bytes 2408964 | tf_op jit(solution)/shard_map/ap,npq->naq/dot_general | solution.py:25
  16.3 0.9 %fusion.10 = bf16[48,64,64]{2,1,0:T(8,128)(2,1)S(1)} fusion(f32[48,64,64]{1,2,0:T(8,128)S(1)} %fusion.7, bf16[2,64,64]{2,1,0:T(8,128)(2,1)S(1)} %copy-done.1, s32[]{:T(128)S(6)} %select_n.16), kind=kOutput, calls=%fused_computation.10 | convolution fusion | flops 151191552 | bytes 1982468 | tf_op jit(solution)/shard_map/naq,bq->nab/dot_general | solution.py:26
  17.2 1.4 %convert_element_type.17 = bf16[1,48,4096]{2,1,0:T(8,128)(2,1)} reshape(bf16[48,64,64]{2,1,0:T(8,128)(2,1)S(1)} %fusion.10) | data formatting | bytes 786432 | tf_op jit(solution)/shard_map/convert_element_type | solution.py:27
  18.6 0.0 all-gather.2.cloned.1.call-update
  18.6 0.0 reduce-scatter.2.cloned.1.call-start
  18.7 39.9 %all-gather.2.cloned.1.call-done = bf16[1,192,4096]{2,1,0:T(8,128)(2,1)} async-done(((bf16[1,48,4096]{2,1,0:T(8,128)(2,1)}), bf16[1,192,4096]{2,1,0:T(8,128)(2,1)}) %all-gather.2.cloned.1.call-update) | async-done | bytes 1572880 | tf_op jit(solution)/shard_map/all_gather | solution.py:50
  58.5 4.9 %fusion.13 = f32[512,192]{0,1:T(8,128)} fusion(bf16[1,512,4096]{2,1,0:T(8,128)(2,1)} %param.8, bf16[1,192,4096]{2,1,0:T(8,128)(2,1)} %all-gather.2.cloned.1.call-done), kind=kOutput, calls=%fused_computation.11 | convolution fusion | flops 805306368 | bytes 6160384 | tf_op jit(solution)/shard_map/ed,qd->eq/dot_general | solution.py:51
  63.5 0.0 reduce-scatter.2.cloned.1.call-update
  63.5 12.1 %reduce-scatter.2.cloned.1.call-done = f32[256,192]{0,1:T(8,128)} async-done(((f32[512,192]{0,1:T(8,128)}), f32[256,192]{0,1:T(8,128)}) %reduce-scatter.2.cloned.1.call-update) | async-done | bytes 196624 | tf_op jit(solution)/shard_map/reduce_scatter | solution.py:52
  (1 shorter events, 0.0 us)
Async XLA Ops:
  6.5 6.5 %copy-start = (f32[2,64,64]{2,1,0:T(8,128)S(1)}, f32[2,64,64]{2,1,0:T(8,128)}, u32[]{:S(2)}) copy-start(f32[2,64,64]{2,1,0:T(8,128)} %param.14) | copy-start | bytes 98308
  6.5 52.0 %all-gather.2.cloned.1.call-start = ((), (), s32[]{:S(2)}) async-start(), calls=%async_computation.1 | async-start | bytes 1966080 | tf_op jit(solution)/shard_map/all_gather | solution.py:50
  9.1 5.1 %copy-start.1 = (bf16[2,64,64]{2,1,0:T(8,128)(2,1)S(1)}, bf16[2,64,64]{2,1,0:T(8,128)(2,1)}, u32[]{:S(2)}) copy-start(bf16[2,64,64]{2,1,0:T(8,128)(2,1)} %param.13) | copy-start | bytes 49156
  14.2 0.9 %copy-start.2 = (bf16[2,64,64]{2,1,0:T(8,128)(2,1)S(1)}, bf16[2,64,64]{2,1,0:T(8,128)(2,1)}, u32[]{:S(2)}) copy-start(bf16[2,64,64]{2,1,0:T(8,128)(2,1)} %param.12) | copy-start | bytes 49156
  18.6 57.0 %reduce-scatter.2.cloned.1.call-start = ((), (), s32[]{:S(2)}) async-start(), calls=%async_computation.2 | async-start | bytes 589824 | tf_op jit(solution)/shard_map/reduce_scatter | solution.py:52
Sparse Core Ops, SparseCore 0:
  18.7 39.7 all-gather.1
  63.6 11.9 reduce-scatter.1
where the time goes:
time: 82.8 us; the launch traced here: 82.5 us
  waiting for transfers between devices  52.1 us (63%)
  between operations  15.4 us (19%)
  matrix products  9.01 us (11%)
  local copies, waits for them, and re-layouts  5.2 us (6%)
    all_gather x1, waiting for transfers between devices, local(): rotated = lax.all_gather(sendable, 'ex', axis=1, tiled=True)  39.9 us
    reduce_scatter x1, waiting for transfers between devices, local(): scores = lax.psum_scatter(summed, 'lay', scatter_dimension=0, tiled=True)  12.1 us
    dot_general x1, matrix products, local(): jnp.einsum('ed,qd->eq', store_grads[0], rotated[0], preferred_element_typ...  4.95 us
    reshape x1, local copies, waits for them, and re-layouts, rotate(): block_rows.astype(jnp.float32).reshape(count_rows, OUT_RANK, IN_RANK)  1.76 us
  transfers between devices with their start and end apart: 2, of which 2 were waited for; matrix products, arithmetic and copies ran while one was open for 0% of the time, Pallas kernels for 0%

commit v1 on v0

v1 whole, which is shorter than its diff:
```python
import functools

import jax
import jax.numpy as jnp
from jax import lax
from jax.experimental import pallas as pl
from jax.experimental.pallas import tpu as pltpu
from jax.sharding import PartitionSpec as P

RANK = 64
BLOCKS = 4
F32 = jnp.float32
BF16 = jnp.bfloat16
NT = (((1,), (1,)), ((), ()))
RING = ("slab", "ex")


def split(x):
    hi = x.astype(BF16)
    return hi, (x - hi.astype(F32)).astype(BF16)


def rotate_kernel(
    half, lay_slots, block_ref, damping_ref, slot_ref, query_ref, out_ref, in_ref, eigen_ref,
    result_ref, rows_ref, basis_ref, turned_ref,
):
    pairs = RANK * RANK // 128
    local = query_ref.shape[1]
    slab = lax.axis_index("slab")
    first = (lax.axis_index("pb") * lax.axis_size("ex") + lax.axis_index("ex")) * local + slab * half
    model_layer = slot_ref[lax.axis_index("lay") * lay_slots]
    low_lanes = lax.broadcasted_iota(jnp.int32, (RANK // 2, 128), 1) < RANK

    for pair in range(pairs):
        block = query_ref[0, :, pair * 128:(pair + 1) * 128].astype(F32)
        rows_ref[pair * half:(pair + 1) * half, :] = jnp.where(slab == 0, block[:half], block[half:2 * half])

    basis_ref[:, :RANK] = out_ref[model_layer].astype(F32)
    out_rows = jnp.concatenate(
        [basis_ref[pl.ds(0, RANK // 2, stride=2), :], basis_ref[pl.ds(1, RANK // 2, stride=2), :]], axis=0
    )
    out_t = out_rows.T[:RANK].astype(BF16)
    out_rows = out_rows[:, :RANK].astype(BF16)
    out_twice = jnp.concatenate([out_rows, out_rows], axis=1)
    out_t_twice = jnp.concatenate([out_t, out_t], axis=1)

    in_wide = jnp.concatenate([in_ref[model_layer].astype(F32)] * 4, axis=1)
    in_tall = jnp.concatenate([in_wide] * 4, axis=0)
    row = lax.broadcasted_iota(jnp.int32, in_tall.shape, 0) // RANK
    col = lax.broadcasted_iota(jnp.int32, in_tall.shape, 1) // RANK
    in_diag = jnp.where(row == col, in_tall, F32(0.0)).astype(BF16)

    eigen = jnp.concatenate([eigen_ref[model_layer]] * 4, axis=1)
    lane = lax.broadcasted_iota(jnp.int32, (1, 4 * RANK), 1) // RANK

    for quad in range(half // 4):
        tops, bottoms = [], []
        for two in range(2):
            at = quad * 4 + two * 2
            a = rows_ref[pl.ds(at, pairs, stride=half), :]
            b = rows_ref[pl.ds(at + 1, pairs, stride=half), :]
            tops.append(jnp.where(low_lanes, a, pltpu.roll(b, RANK, 1)))
            bottoms.append(jnp.where(low_lanes, pltpu.roll(a, RANK, 1), b))
        grid = jnp.concatenate(
            [jnp.concatenate(tops, axis=1), jnp.concatenate(bottoms, axis=1)], axis=0
        ).astype(BF16)
        right = jnp.dot(grid, in_diag, preferred_element_type=F32)
        middle = jnp.dot(out_t_twice, jnp.concatenate(split(right), axis=0), preferred_element_type=F32)
        damp = jnp.zeros((1, 4 * RANK), F32)
        for one in range(4):
            block = block_ref[first + quad * 4 + one]
            value = F32(0.0)
            for k in range(BLOCKS):
                value = jnp.where(block == k, damping_ref[k], value)
            damp = jnp.where(lane == one, value, damp)
        scaled = middle / (eigen + damp)
        turned = jnp.dot(out_twice, jnp.concatenate(split(scaled), axis=0), preferred_element_type=F32)
        hi, lo = split(turned)
        result = lax.dot_general(hi, in_diag, NT, preferred_element_type=F32)
        result = result + lax.dot_general(lo, in_diag, NT, preferred_element_type=F32)
        for two in range(2):
            at = quad * 4 + two * 2
            top = result[:pairs, two * 128:(two + 1) * 128]
            bottom = result[pairs:, two * 128:(two + 1) * 128]
            turned_ref[pl.ds(at, pairs, stride=half), :] = jnp.where(low_lanes, top, pltpu.roll(bottom, RANK, 1))
            turned_ref[pl.ds(at + 1, pairs, stride=half), :] = jnp.where(low_lanes, pltpu.roll(top, RANK, 1), bottom)

    for pair in range(pairs):
        result_ref[:, pair * 128:(pair + 1) * 128] = turned_ref[pair * half:(pair + 1) * half, :].astype(BF16)


def rotate(query_grads, query_block, layer_slot, out_basis, in_basis, eigen_values, damping):
    half = query_grads.shape[1] // lax.axis_size("slab")
    dim = query_grads.shape[2]
    vmem = pl.BlockSpec(memory_space=pltpu.VMEM)
    smem = pl.BlockSpec(memory_space=pltpu.SMEM)
    return pl.pallas_call(
        functools.partial(rotate_kernel, half, 1),
        out_shape=jax.ShapeDtypeStruct((half, dim), BF16),
        in_specs=[smem, smem, smem, vmem, vmem, vmem, vmem],
        out_specs=vmem,
        scratch_shapes=[
            pltpu.VMEM((half * dim // 128, 128), F32),
            pltpu.VMEM((RANK, 128), F32),
            pltpu.VMEM((half * dim // 128, 128), F32),
        ],
        compiler_params=pltpu.CompilerParams(vmem_limit_bytes=16 << 20),
        cost_estimate=pl.CostEstimate(flops=8 * half * dim * 256, bytes_accessed=1 << 20, transcendentals=0),
        name="rotate",
    )(query_block, damping, layer_slot, query_grads, out_basis, in_basis, eigen_values)


def score_kernel(count, height, share, shares, *refs):
    pieces, store_ref = refs[:count], refs[count]
    keep_ref, sends, held = refs[count + 1], refs[count + 2:-1], refs[-1]
    half, width = pieces[0].shape
    dim = store_ref.shape[2]
    if width == dim:
        for k, piece in enumerate(pieces):
            held[k * height:k * height + half, :] = piece[...]
        whole = count
    else:
        for k, piece in enumerate(pieces):
            held[:half, k * width:(k + 1) * width] = piece[...]
        whole = 1
    lay = lax.axis_index("lay")
    for k in range(shares):
        owner = lax.rem(lay + k, shares)
        rows = pl.ds(pl.multiple_of(owner * share, share), share)
        block = lax.dot_general(held[...], store_ref[0, rows, :], NT, preferred_element_type=F32)
        target = keep_ref if k == 0 else sends[k - 1]
        for j in range(whole):
            target[j * half:(j + 1) * half, :] = block[j * height:j * height + half].astype(target.dtype)


def score(pieces, store):
    half, width = pieces[0].shape
    _, examples, dim = store.shape
    shares = lax.axis_size("lay")
    share = examples // shares
    whole = len(pieces) if width == dim else 1
    height = -(-half // 16) * 16
    vmem = pl.BlockSpec(memory_space=pltpu.VMEM)
    shape = (whole * half, share)
    out = pl.pallas_call(
        functools.partial(score_kernel, len(pieces), height, share, shares),
        out_shape=[jax.ShapeDtypeStruct(shape, F32)] + [jax.ShapeDtypeStruct(shape, BF16)] * (shares - 1),
        in_specs=[vmem] * (len(pieces) + 1),
        out_specs=[vmem] * shares,
        scratch_shapes=[pltpu.VMEM((whole * height, dim), BF16)],
        compiler_params=pltpu.CompilerParams(vmem_limit_bytes=24 << 20),
        cost_estimate=pl.CostEstimate(flops=2 * 256 * examples * dim, bytes_accessed=1 << 20, transcendentals=0),
        name="score",
    )(*pieces, store)
    return out[0], out[1:]


def swap_layers(sends):
    shares = lax.axis_size("lay")
    return [
        lax.ppermute(send, "lay", [(i, (i + k + 1) % shares) for i in range(shares)])
        for k, send in enumerate(sends)
    ]


def finish_kernel(half, members, sizes, *refs):
    out_ref = refs[-1]
    refs = refs[:-1]
    count = len(sizes)
    each = len(refs) // count
    slab, ex = lax.axis_index("slab"), lax.axis_index("ex")
    place = jnp.where(slab == 0, ex, 2 * members - 1 - ex)
    step = jnp.where(lax.rem(place, 2) == 0, 1, 2 * members - 1)
    at = 0
    for k, size in enumerate(sizes):
        keep, got = refs[k * each], refs[k * each + 1:(k + 1) * each]
        for j in range(size):
            rows = slice(j * half, (j + 1) * half)
            total = keep[rows, :]
            for g in got:
                total = total + g[rows, :].astype(F32)
            distance, side = (at + 1) // 2, (at + 1) % 2
            hops = distance if side == 0 else 2 * members - distance
            source = lax.rem(place + hops * step, 2 * members)
            block = jnp.where(source < members, 2 * source, 2 * (2 * members - 1 - source) + 1)
            out_ref[pl.ds(pl.multiple_of(block * half, 8), half), :] = total
            at += 1


def finish(half, parts):
    members = lax.axis_size("ex")
    vmem = pl.BlockSpec(memory_space=pltpu.VMEM)
    flat = [array for keep, got in parts for array in [keep, *got]]
    sizes = [keep.shape[0] // half for keep, _ in parts]
    return pl.pallas_call(
        functools.partial(finish_kernel, half, members, sizes),
        out_shape=jax.ShapeDtypeStruct((2 * members * half, flat[0].shape[1]), F32),
        in_specs=[vmem] * len(flat),
        out_specs=vmem,
        compiler_params=pltpu.CompilerParams(vmem_limit_bytes=16 << 20),
        name="finish",
    )(*flat)


def local(
    store_grads, query_grads, query_block, layer_slot, out_basis, in_basis, eigen_values, damping
):
    members = lax.axis_size("ex")
    ring = list(range(members)) + [members + i for i in reversed(range(members))]
    edges = [[], []]
    for i, a in enumerate(ring):
        b = ring[(i + 1) % len(ring)]
        edges[i % 2] += [(a, b), (b, a)]
    own = rotate(query_grads, query_block, layer_slot, out_basis, in_basis, eigen_values, damping)
    half, dim = own.shape
    even = odd = own
    batch, parts = [own], []
    for step in range(1, members + 1):
        if step == members:
            even, odd = even[:, dim // 2:], odd[:, :dim // 2]
        even, odd = lax.ppermute(odd, RING, edges[0]), lax.ppermute(even, RING, edges[1])
        if step < members:
            batch += [even, odd]
        if len(batch) >= 5 or step >= members - 1:
            if step == members:
                batch = [even, odd]
            keep, sends = score(batch, store_grads)
            parts.append((keep, swap_layers(sends)))
            batch = []
    return finish(half, parts).T


def solution(mesh):
    return jax.shard_map(
        local,
        mesh=mesh,
        in_specs=(
            P("lay", ("slab", "ex"), None),
            P("lay", ("pb", "ex"), None),
            P(),
            P(),
            P(),
            P(),
            P(),
            P(),
        ),
        out_specs=P(("slab", "ex", "lay"), "pb"),
        check_vma=False,
    )
```

time: 82.8 us -> 42.7 us (0.52)
  waiting for transfers between devices: 52.1 us -> 10.8 us
  starting transfers between devices: 0.04 us -> 16.1 us
  between operations: 15.4 us -> 0.05 us
  matrix products: 9.01 us -> 0 us
  Pallas kernels: 0 us -> 7.83 us
  local copies, waits for them, and re-layouts: 5.2 us -> 7.55 us
    all_gather x1 -> x0, waiting for transfers between devices: 39.9 us -> none  [local(): rotated = lax.all_gather(sendable, 'ex', axis=1, tiled=True)]
    ppermute x0 -> x11, starting transfers between devices: none -> 16.1 us  [the longest x4 7.58 us: local(): lax.ppermute(even, RING, edges[1])]
    reduce_scatter x1 -> x0, waiting for transfers between devices: 12.1 us -> none  [local(): scores = lax.psum_scatter(summed, 'lay', scatter_dimension=0, tiled=True)]
    ppermute x0 -> x11, waiting for transfers between devices: none -> 10.8 us  [the longest x4 4.7 us: local(): lax.ppermute(even, RING, edges[1])]
    dot_general x5 -> x0, matrix products: 9.01 us -> none  [the longest x1 4.95 us: local(): jnp.einsum('ed,qd->eq', store_grads[0], rotated[0], preferred_element_typ...]
    pallas_call x0 -> x5, Pallas kernels: none -> 7.83 us  [the longest x3 4.19 us: score(): pl.pallas_call(functools.partial(score_kernel, len(pieces), height, share...]
    unnamed x6 -> x18, local copies, waits for them, and re-layouts: 0.02 us -> 7.53 us
    dynamic_slice x2 -> x0, local copies, waits for them, and re-layouts: 2.03 us -> none  [the longest x1 1.27 us: local(): model_layer = layer_slot[lax.axis_index('lay') * slots + 0]]
  transfers between devices with their start and end apart: 2 -> 11, of which waited for: 2 -> 6; matrix products, arithmetic and copies ran while one was open for 0% -> 0% of each run, Pallas kernels for 0% -> 10%
where the time goes in v1:
time: 42.7 us; the launch traced here: 42.3 us
  starting transfers between devices  16.1 us (38%)
  waiting for transfers between devices  10.8 us (25%)
  Pallas kernels  7.83 us (18%)
  local copies, waits for them, and re-layouts  7.55 us (18%)
    ppermute x4, starting transfers between devices, local(): lax.ppermute(even, RING, edges[1])  7.58 us
    unnamed x18, local copies, waits for them, and re-layouts  7.53 us
    ppermute x4, starting transfers between devices, local(): lax.ppermute(odd, RING, edges[0])  5.91 us
    ppermute x4, waiting for transfers between devices, local(): lax.ppermute(even, RING, edges[1])  4.7 us
    pallas_call x3, Pallas kernels, score(): pl.pallas_call(functools.partial(score_kernel, len(pieces), height, share...  4.19 us
    ppermute x3, waiting for transfers between devices, swap_layers(): lax.ppermute(send, 'lay', [(i, (i + k + 1) % shares) for i in range(share...  3.28 us
    pallas_call x1, Pallas kernels, rotate(): pl.pallas_call(functools.partial(rotate_kernel, half, 1), out_shape=jax.S...  2.93 us
    ppermute x4, waiting for transfers between devices, local(): lax.ppermute(odd, RING, edges[0])  2.76 us
  transfers between devices with their start and end apart: 11, of which 6 were waited for; matrix products, arithmetic and copies ran while one was open for 0% of the time, Pallas kernels for 10%

profile of v1, /device:TPU:0, one launch (start us, length us, event | category | flops | bytes accessed | tf_op | source)
XLA Modules:
  0.0 42.3 jit_solution(7007157975516339634)
XLA Ops:
  0.0 1.0 %copy-done.2 = bf16[1,48,4096]{2,1,0:T(8,128)(2,1)S(1)} copy-done((bf16[1,48,4096]{2,1,0:T(8,128)(2,1)S(1)}, bf16[1,48,4096]{2,1,0:T(8,128)(2,1)}, u32[]{:S(2)}) %copy-start.2) | copy-done | bytes 393240
  1.0 0.8 %copy-done.3 = f32[2,64,64]{2,1,0:T(8,128)S(1)} copy-done((f32[2,64,64]{2,1,0:T(8,128)S(1)}, f32[2,64,64]{2,1,0:T(8,128)}, u32[]{:S(2)}) %copy-start.3) | copy-done | bytes 32792
  1.8 0.8 %copy-done.4 = bf16[2,64,64]{2,1,0:T(8,128)(2,1)S(1)} copy-done((bf16[2,64,64]{2,1,0:T(8,128)(2,1)S(1)}, bf16[2,64,64]{2,1,0:T(8,128)(2,1)}, u32[]{:S(2)}) %copy-start.4) | copy-done | bytes 16408
  2.6 0.8 %copy-done.5 = bf16[2,64,64]{2,1,0:T(8,128)(2,1)S(1)} copy-done((bf16[2,64,64]{2,1,0:T(8,128)(2,1)S(1)}, bf16[2,64,64]{2,1,0:T(8,128)(2,1)}, u32[]{:S(2)}) %copy-start.5) | copy-done | bytes 16408
  3.4 0.7 %copy-done.6 = s32[384]{0:T(512)S(1)} copy-done((s32[384]{0:T(512)S(1)}, s32[384]{0:T(512)}, u32[]{:S(2)}) %copy-start.6) | copy-done | bytes 1560
  4.0 0.7 %copy-done.7 = f32[4]{0:T(128)S(1)} copy-done((f32[4]{0:T(128)S(1)}, f32[4]{0:T(128)}, u32[]{:S(2)}) %copy-start.7) | copy-done | bytes 40
  4.7 0.7 %copy-done.8 = s32[2]{0:T(128)S(1)} copy-done((s32[2]{0:T(128)S(1)}, s32[2]{0:T(128)}, u32[]{:S(2)}) %copy-start.8) | copy-done | bytes 32
  5.3 2.9 %rotate.1.refs_0_ = bf16[24,4096]{1,0:T(8,128)(2,1)S(1)} custom-call(s32[384]{0:T(512)S(1)} %copy-done.6, f32[4]{0:T(128)S(1)} %copy-done.7, s32[2]{0:T(128)S(1)} %copy-done.8, bf16[1,48,4096]{2,1,0:T(8,128)(2,1)S(1)} %copy-done.2, bf16[2,64,64]{2,1,0:T(8,128)(2,1)S(1)} %copy-done.4, bf16[2,64,64]{2,1,0:T(8,128)(2,1)S(1)} %copy-done.5, ...), custom_call_target="tpu_custom_call" | custom-call | flops 201326592 | bytes 1048576 | tf_op jit(solution)/shard_map/rotate/pallas_call | solution.py:97
  8.3 3.0 %collective-permute-start.1 = (bf16[24,4096]{1,0:T(8,128)(2,1)S(1)}, bf16[24,4096]{1,0:T(8,128)(2,1)S(1)}, u32[]{:S(2)}, u32[]{:S(2)}) collective-permute-start(bf16[24,4096]{1,0:T(8,128)(2,1)S(1)} %rotate.1.refs_0_), channel_id=1, source_target_pairs={{4,8},{8,4},{12,28},{28,12},{24,20},{20,24},{16,0},{0,16},{5,9},{9... | collective-permute-start | bytes 589832 | tf_op jit(solution)/shard_map/ppermute | solution.py:221
  11.3 1.6 %collective-permute-start = (bf16[24,4096]{1,0:T(8,128)(2,1)S(1)}, bf16[24,4096]{1,0:T(8,128)(2,1)S(1)}, u32[]{:S(2)}, u32[]{:S(2)}) collective-permute-start(bf16[24,4096]{1,0:T(8,128)(2,1)S(1)} %rotate.1.refs_0_), channel_id=1, source_target_pairs={{0,4},{4,0},{8,12},{12,8},{28,24},{24,28},{20,16},{16,20},{1,5},{5... | collective-permute-start | bytes 589832 | tf_op jit(solution)/shard_map/ppermute | solution.py:221
  12.9 3.3 %collective-permute-done.1.refs_2_ = bf16[24,4096]{1,0:T(8,128)(2,1)S(1)} collective-permute-done((bf16[24,4096]{1,0:T(8,128)(2,1)S(1)}, bf16[24,4096]{1,0:T(8,128)(2,1)S(1)}, u32[]{:S(2)}, u32[]{:S(2)}) %collective-permute-start.1) | collective-permute-done | bytes 196640 | tf_op jit(solution)/shard_map/ppermute | solution.py:221
  16.2 1.8 %collective-permute-start.2 = (bf16[24,4096]{1,0:T(8,128)(2,1)S(1)}, bf16[24,4096]{1,0:T(8,128)(2,1)S(1)}, u32[]{:S(2)}, u32[]{:S(2)}) collective-permute-start(bf16[24,4096]{1,0:T(8,128)(2,1)S(1)} %collective-permute-done.1.refs_2_), channel_id=1, source_target_pairs={{0,4},{4,0},{8,12},{12,8},{28,24},{24,28},{20,16},{16,20},{1,5},{5... | collective-permute-start | bytes 589832 | tf_op jit(solution)/shard_map/ppermute | solution.py:221
  18.0 0.0 collective-permute-done.refs_1_
  18.0 1.5 %collective-permute-start.3 = (bf16[24,4096]{1,0:T(8,128)(2,1)S(1)}, bf16[24,4096]{1,0:T(8,128)(2,1)S(1)}, u32[]{:S(2)}, u32[]{:S(2)}) collective-permute-start(bf16[24,4096]{1,0:T(8,128)(2,1)S(1)} %collective-permute-done.refs_1_), channel_id=1, source_target_pairs={{4,8},{8,4},{12,28},{28,12},{24,20},{20,24},{16,0},{0,16},{5,9},{9... | collective-permute-start | bytes 589832 | tf_op jit(solution)/shard_map/ppermute | solution.py:221
  19.5 2.8 %collective-permute-done.2.refs_3_ = bf16[24,4096]{1,0:T(8,128)(2,1)S(1)} collective-permute-done((bf16[24,4096]{1,0:T(8,128)(2,1)S(1)}, bf16[24,4096]{1,0:T(8,128)(2,1)S(1)}, u32[]{:S(2)}, u32[]{:S(2)}) %collective-permute-start.2) | collective-permute-done | bytes 196640 | tf_op jit(solution)/shard_map/ppermute | solution.py:221
  22.3 1.4 %collective-permute-start.6 = (bf16[24,4096]{1,0:T(8,128)(2,1)S(1)}, bf16[24,4096]{1,0:T(8,128)(2,1)S(1)}, u32[]{:S(2)}, u32[]{:S(2)}) collective-permute-start(bf16[24,4096]{1,0:T(8,128)(2,1)S(1)} %collective-permute-done.2.refs_3_), channel_id=1, source_target_pairs={{4,8},{8,4},{12,28},{28,12},{24,20},{20,24},{16,0},{0,16},{5,9},{9... | collective-permute-start | bytes 589832 | tf_op jit(solution)/shard_map/ppermute | solution.py:221
  23.7 0.4 collective-permute-done.3.refs_4_
  24.1 1.4 %collective-permute-start.5 = (bf16[24,4096]{1,0:T(8,128)(2,1)S(1)}, bf16[24,4096]{1,0:T(8,128)(2,1)S(1)}, u32[]{:S(2)}, u32[]{:S(2)}) collective-permute-start(bf16[24,4096]{1,0:T(8,128)(2,1)S(1)} %collective-permute-done.3.refs_4_), channel_id=1, source_target_pairs={{0,4},{4,0},{8,12},{12,8},{28,24},{24,28},{20,16},{16,20},{1,5},{5... | collective-permute-start | bytes 589832 | tf_op jit(solution)/shard_map/ppermute | solution.py:221
  25.5 2.2 %copy-done = bf16[1,512,4096]{2,1,0:T(8,128)(2,1)S(1)} copy-done((bf16[1,512,4096]{2,1,0:T(8,128)(2,1)S(1)}, bf16[1,512,4096]{2,1,0:T(8,128)(2,1)}, u32[]{:S(2)}) %copy-start) | copy-done | bytes 4194328
  27.7 1.5 %score.3 = (f32[120,256]{1,0:T(8,128)S(1)}, bf16[120,256]{1,0:T(8,128)(2,1)S(1)}) custom-call(bf16[24,4096]{1,0:T(8,128)(2,1)S(1)} %rotate.1.refs_0_, bf16[24,4096]{1,0:T(8,128)(2,1)S(1)} %collective-permute-done.refs_1_, bf16[24,4096]{1,0:T(8,128)(2,1)S(1)} %collective-permute-done.1.refs_2_, bf16[24,4096]{1,0:T(8,128)(2,1)S(1)} %collective-permute-done.2.refs_3_, ...), custom_call_target="tpu_custom_call" | custom-call | flops 1073741824 | bytes 1048576 | tf_op jit(solution)/shard_map/score/pallas_call | solution.py:145
  29.2 1.6 %collective-permute-start.4 = (bf16[120,256]{1,0:T(8,128)(2,1)S(1)}, bf16[120,256]{1,0:T(8,128)(2,1)S(1)}, u32[]{:S(2)}, u32[]{:S(2)}) collective-permute-start(bf16[120,256]{1,0:T(8,128)(2,1)S(1)} %get-tuple-element.12), channel_id=1, source_target_pairs={{0,2},{2,0},{1,3},{3,1},{4,6},{6,4},{5,7},{7,5},{8,10},{10,8},{9,1... | collective-permute-start | bytes 184328 | tf_op jit(solution)/shard_map/ppermute | solution.py:161
  30.8 0.0 collective-permute-done.6.refs_1_
  30.8 1.1 %collective-permute-start.8 = (bf16[24,2048]{1,0:T(8,128)(2,1)S(1)}, bf16[24,2048]{1,0:T(8,128)(2,1)S(1)}, u32[]{:S(2)}, u32[]{:S(2)}) collective-permute-start(bf16[24,2048]{1,0:T(8,128)(2,1)S(1)} %slice.8), channel_id=1, source_target_pairs={{0,4},{4,0},{8,12},{12,8},{28,24},{24,28},{20,16},{16,20},{1,5},{5... | collective-permute-start | bytes 294920 | tf_op jit(solution)/shard_map/ppermute | solution.py:221
  31.9 1.6 %collective-permute-start.9 = (bf16[24,2048]{1,0:T(8,128)(2,1)S(1)}, bf16[24,2048]{1,0:T(8,128)(2,1)S(1)}, u32[]{:S(2)}, u32[]{:S(2)}) collective-permute-start(bf16[24,2048]{1,0:T(8,128)(2,1)S(1)} %slice.9), channel_id=1, source_target_pairs={{4,8},{8,4},{12,28},{28,12},{24,20},{20,24},{16,0},{0,16},{5,9},{9... | collective-permute-start | bytes 294920 | tf_op jit(solution)/shard_map/ppermute | solution.py:221
  33.5 1.4 %score.4 = (f32[48,256]{1,0:T(8,128)S(1)}, bf16[48,256]{1,0:T(8,128)(2,1)S(1)}) custom-call(bf16[24,4096]{1,0:T(8,128)(2,1)S(1)} %collective-permute-done.5.refs_0_, bf16[24,4096]{1,0:T(8,128)(2,1)S(1)} %collective-permute-done.6.refs_1_, bf16[1,512,4096]{2,1,0:T(8,128)(2,1)S(1)} %copy-done.1), custom_call_target="tpu_custom_call" | custom-call | flops 1073741824 | bytes 1048576 | tf_op jit(solution)/shard_map/score/pallas_call | solution.py:145
  34.9 0.6 %collective-permute-start.7 = (bf16[48,256]{1,0:T(8,128)(2,1)S(1)}, bf16[48,256]{1,0:T(8,128)(2,1)S(1)}, u32[]{:S(2)}, u32[]{:S(2)}) collective-permute-start(bf16[48,256]{1,0:T(8,128)(2,1)S(1)} %get-tuple-element.14), channel_id=1, source_target_pairs={{0,2},{2,0},{1,3},{3,1},{4,6},{6,4},{5,7},{7,5},{8,10},{10,8},{9,1... | collective-permute-start | bytes 73736 | tf_op jit(solution)/shard_map/ppermute | solution.py:161
  35.5 1.1 %collective-permute-done.9.refs_1_ = bf16[24,2048]{1,0:T(8,128)(2,1)S(1)} collective-permute-done((bf16[24,2048]{1,0:T(8,128)(2,1)S(1)}, bf16[24,2048]{1,0:T(8,128)(2,1)S(1)}, u32[]{:S(2)}, u32[]{:S(2)}) %collective-permute-start.9) | collective-permute-done | bytes 98336 | tf_op jit(solution)/shard_map/ppermute | solution.py:221
  36.6 1.3 %score.5 = (f32[24,256]{1,0:T(8,128)S(1)}, bf16[24,256]{1,0:T(8,128)(2,1)S(1)}) custom-call(bf16[24,2048]{1,0:T(8,128)(2,1)S(1)} %collective-permute-done.8.refs_0_, bf16[24,2048]{1,0:T(8,128)(2,1)S(1)} %collective-permute-done.9.refs_1_, bf16[1,512,4096]{2,1,0:T(8,128)(2,1)S(1)} %copy-done.1), custom_call_target="tpu_custom_call" | custom-call | flops 1073741824 | bytes 1048576 | tf_op jit(solution)/shard_map/score/pallas_call | solution.py:145
  37.9 0.5 %collective-permute-start.10 = (bf16[24,256]{1,0:T(8,128)(2,1)S(1)}, bf16[24,256]{1,0:T(8,128)(2,1)S(1)}, u32[]{:S(2)}, u32[]{:S(2)}) collective-permute-start(bf16[24,256]{1,0:T(8,128)(2,1)S(1)} %get-tuple-element.16), channel_id=1, source_target_pairs={{0,2},{2,0},{1,3},{3,1},{4,6},{6,4},{5,7},{7,5},{8,10},{10,8},{9,1... | collective-permute-start | bytes 36872 | tf_op jit(solution)/shard_map/ppermute | solution.py:161
  38.3 0.4 %collective-permute-done.7.refs_3_ = bf16[48,256]{1,0:T(8,128)(2,1)S(1)} collective-permute-done((bf16[48,256]{1,0:T(8,128)(2,1)S(1)}, bf16[48,256]{1,0:T(8,128)(2,1)S(1)}, u32[]{:S(2)}, u32[]{:S(2)}) %collective-permute-start.7) | collective-permute-done | bytes 24608 | tf_op jit(solution)/shard_map/ppermute | solution.py:161
  38.8 2.8 %collective-permute-done.10.refs_5_ = bf16[24,256]{1,0:T(8,128)(2,1)S(1)} collective-permute-done((bf16[24,256]{1,0:T(8,128)(2,1)S(1)}, bf16[24,256]{1,0:T(8,128)(2,1)S(1)}, u32[]{:S(2)}, u32[]{:S(2)}) %collective-permute-start.10) | collective-permute-done | bytes 12320 | tf_op jit(solution)/shard_map/ppermute | solution.py:161
  41.6 0.7 %finish.1 = f32[192,256]{1,0:T(8,128)} custom-call(f32[120,256]{1,0:T(8,128)S(1)} %get-tuple-element.11.refs_0_, bf16[120,256]{1,0:T(8,128)(2,1)S(1)} %collective-permute-done.4.refs_1_, f32[48,256]{1,0:T(8,128)S(1)} %get-tuple-element.13.refs_2_, bf16[48,256]{1,0:T(8,128)(2,1)S(1)} %collective-permute-done.7.refs_3_, ...), custom_call_target="tpu_custom_call" | custom-call | tf_op jit(solution)/shard_map/finish/pallas_call | solution.py:195
  (15 shorter events, 0.0 us)
Async XLA Ops:
  0.0 1.0 %copy-start.2 = (bf16[1,48,4096]{2,1,0:T(8,128)(2,1)S(1)}, bf16[1,48,4096]{2,1,0:T(8,128)(2,1)}, u32[]{:S(2)}) copy-start(bf16[1,48,4096]{2,1,0:T(8,128)(2,1)} %query_ref.1) | copy-start | bytes 1179652
  1.0 0.8 %copy-start.3 = (f32[2,64,64]{2,1,0:T(8,128)S(1)}, f32[2,64,64]{2,1,0:T(8,128)}, u32[]{:S(2)}) copy-start(f32[2,64,64]{2,1,0:T(8,128)} %eigen_ref.1) | copy-start | bytes 98308
  1.8 0.8 %copy-start.4 = (bf16[2,64,64]{2,1,0:T(8,128)(2,1)S(1)}, bf16[2,64,64]{2,1,0:T(8,128)(2,1)}, u32[]{:S(2)}) copy-start(bf16[2,64,64]{2,1,0:T(8,128)(2,1)} %out_ref.1) | copy-start | bytes 49156
  2.6 0.8 %copy-start.5 = (bf16[2,64,64]{2,1,0:T(8,128)(2,1)S(1)}, bf16[2,64,64]{2,1,0:T(8,128)(2,1)}, u32[]{:S(2)}) copy-start(bf16[2,64,64]{2,1,0:T(8,128)(2,1)} %in_ref.1) | copy-start | bytes 49156
  3.4 0.7 %copy-start.6 = (s32[384]{0:T(512)S(1)}, s32[384]{0:T(512)}, u32[]{:S(2)}) copy-start(s32[384]{0:T(512)} %block_ref.1) | copy-start | bytes 4612
  4.0 0.7 %copy-start.7 = (f32[4]{0:T(128)S(1)}, f32[4]{0:T(128)}, u32[]{:S(2)}) copy-start(f32[4]{0:T(128)} %damping_ref.1) | copy-start | bytes 52
  4.7 0.7 %copy-start.8 = (s32[2]{0:T(128)S(1)}, s32[2]{0:T(128)}, u32[]{:S(2)}) copy-start(s32[2]{0:T(128)} %slot_ref.1) | copy-start | bytes 28
  8.3 7.9 %collective-permute-start.1 = (bf16[24,4096]{1,0:T(8,128)(2,1)S(1)}, bf16[24,4096]{1,0:T(8,128)(2,1)S(1)}, u32[]{:S(2)}, u32[]{:S(2)}) collective-permute-start(bf16[24,4096]{1,0:T(8,128)(2,1)S(1)} %rotate.1.refs_0_), channel_id=1, source_target_pairs={{4,8},{8,4},{12,28},{28,12},{24,20},{20,24},{16,0},{0,16},{5,9},{9... | collective-permute-start | bytes 589832 | tf_op jit(solution)/shard_map/ppermute | solution.py:221
  11.3 6.7 %collective-permute-start = (bf16[24,4096]{1,0:T(8,128)(2,1)S(1)}, bf16[24,4096]{1,0:T(8,128)(2,1)S(1)}, u32[]{:S(2)}, u32[]{:S(2)}) collective-permute-start(bf16[24,4096]{1,0:T(8,128)(2,1)S(1)} %rotate.1.refs_0_), channel_id=1, source_target_pairs={{0,4},{4,0},{8,12},{12,8},{28,24},{24,28},{20,16},{16,20},{1,5},{5... | collective-permute-start | bytes 589832 | tf_op jit(solution)/shard_map/ppermute | solution.py:221
  16.2 6.1 %collective-permute-start.2 = (bf16[24,4096]{1,0:T(8,128)(2,1)S(1)}, bf16[24,4096]{1,0:T(8,128)(2,1)S(1)}, u32[]{:S(2)}, u32[]{:S(2)}) collective-permute-start(bf16[24,4096]{1,0:T(8,128)(2,1)S(1)} %collective-permute-done.1.refs_2_), channel_id=1, source_target_pairs={{0,4},{4,0},{8,12},{12,8},{28,24},{24,28},{20,16},{16,20},{1,5},{5... | collective-permute-start | bytes 589832 | tf_op jit(solution)/shard_map/ppermute | solution.py:221
  18.0 6.1 %collective-permute-start.3 = (bf16[24,4096]{1,0:T(8,128)(2,1)S(1)}, bf16[24,4096]{1,0:T(8,128)(2,1)S(1)}, u32[]{:S(2)}, u32[]{:S(2)}) collective-permute-start(bf16[24,4096]{1,0:T(8,128)(2,1)S(1)} %collective-permute-done.refs_1_), channel_id=1, source_target_pairs={{4,8},{8,4},{12,28},{28,12},{24,20},{20,24},{16,0},{0,16},{5,9},{9... | collective-permute-start | bytes 589832 | tf_op jit(solution)/shard_map/ppermute | solution.py:221
  22.3 8.5 %collective-permute-start.6 = (bf16[24,4096]{1,0:T(8,128)(2,1)S(1)}, bf16[24,4096]{1,0:T(8,128)(2,1)S(1)}, u32[]{:S(2)}, u32[]{:S(2)}) collective-permute-start(bf16[24,4096]{1,0:T(8,128)(2,1)S(1)} %collective-permute-done.2.refs_3_), channel_id=1, source_target_pairs={{4,8},{8,4},{12,28},{28,12},{24,20},{20,24},{16,0},{0,16},{5,9},{9... | collective-permute-start | bytes 589832 | tf_op jit(solution)/shard_map/ppermute | solution.py:221
  24.1 7.8 %collective-permute-start.5 = (bf16[24,4096]{1,0:T(8,128)(2,1)S(1)}, bf16[24,4096]{1,0:T(8,128)(2,1)S(1)}, u32[]{:S(2)}, u32[]{:S(2)}) collective-permute-start(bf16[24,4096]{1,0:T(8,128)(2,1)S(1)} %collective-permute-done.3.refs_4_), channel_id=1, source_target_pairs={{0,4},{4,0},{8,12},{12,8},{28,24},{24,28},{20,16},{16,20},{1,5},{5... | collective-permute-start | bytes 589832 | tf_op jit(solution)/shard_map/ppermute | solution.py:221
  25.5 2.2 %copy-start = (bf16[1,512,4096]{2,1,0:T(8,128)(2,1)S(1)}, bf16[1,512,4096]{2,1,0:T(8,128)(2,1)}, u32[]{:S(2)}) copy-start(bf16[1,512,4096]{2,1,0:T(8,128)(2,1)} %refs_2_.3) | copy-start | bytes 12582916
  27.7 5.8 %copy-start.1 = (bf16[1,512,4096]{2,1,0:T(8,128)(2,1)S(1)}, bf16[1,512,4096]{2,1,0:T(8,128)(2,1)}, u32[]{:S(2)}) copy-start(bf16[1,512,4096]{2,1,0:T(8,128)(2,1)} %refs_2_.3) | copy-start | bytes 12582916
  29.2 9.1 %collective-permute-start.4 = (bf16[120,256]{1,0:T(8,128)(2,1)S(1)}, bf16[120,256]{1,0:T(8,128)(2,1)S(1)}, u32[]{:S(2)}, u32[]{:S(2)}) collective-permute-start(bf16[120,256]{1,0:T(8,128)(2,1)S(1)} %get-tuple-element.12), channel_id=1, source_target_pairs={{0,2},{2,0},{1,3},{3,1},{4,6},{6,4},{5,7},{7,5},{8,10},{10,8},{9,1... | collective-permute-start | bytes 184328 | tf_op jit(solution)/shard_map/ppermute | solution.py:161
  30.8 4.7 %collective-permute-start.8 = (bf16[24,2048]{1,0:T(8,128)(2,1)S(1)}, bf16[24,2048]{1,0:T(8,128)(2,1)S(1)}, u32[]{:S(2)}, u32[]{:S(2)}) collective-permute-start(bf16[24,2048]{1,0:T(8,128)(2,1)S(1)} %slice.8), channel_id=1, source_target_pairs={{0,4},{4,0},{8,12},{12,8},{28,24},{24,28},{20,16},{16,20},{1,5},{5... | collective-permute-start | bytes 294920 | tf_op jit(solution)/shard_map/ppermute | solution.py:221
  31.9 4.7 %collective-permute-start.9 = (bf16[24,2048]{1,0:T(8,128)(2,1)S(1)}, bf16[24,2048]{1,0:T(8,128)(2,1)S(1)}, u32[]{:S(2)}, u32[]{:S(2)}) collective-permute-start(bf16[24,2048]{1,0:T(8,128)(2,1)S(1)} %slice.9), channel_id=1, source_target_pairs={{4,8},{8,4},{12,28},{28,12},{24,20},{20,24},{16,0},{0,16},{5,9},{9... | collective-permute-start | bytes 294920 | tf_op jit(solution)/shard_map/ppermute | solution.py:221
  34.9 3.9 %collective-permute-start.7 = (bf16[48,256]{1,0:T(8,128)(2,1)S(1)}, bf16[48,256]{1,0:T(8,128)(2,1)S(1)}, u32[]{:S(2)}, u32[]{:S(2)}) collective-permute-start(bf16[48,256]{1,0:T(8,128)(2,1)S(1)} %get-tuple-element.14), channel_id=1, source_target_pairs={{0,2},{2,0},{1,3},{3,1},{4,6},{6,4},{5,7},{7,5},{8,10},{10,8},{9,1... | collective-permute-start | bytes 73736 | tf_op jit(solution)/shard_map/ppermute | solution.py:161
  37.9 3.7 %collective-permute-start.10 = (bf16[24,256]{1,0:T(8,128)(2,1)S(1)}, bf16[24,256]{1,0:T(8,128)(2,1)S(1)}, u32[]{:S(2)}, u32[]{:S(2)}) collective-permute-start(bf16[24,256]{1,0:T(8,128)(2,1)S(1)} %get-tuple-element.16), channel_id=1, source_target_pairs={{0,2},{2,0},{1,3},{3,1},{4,6},{6,4},{5,7},{7,5},{8,10},{10,8},{9,1... | collective-permute-start | bytes 36872 | tf_op jit(solution)/shard_map/ppermute | solution.py:161

commit v2 on v1

v2 whole, which is shorter than its diff:
```python
import functools

import jax
import jax.numpy as jnp
from jax import lax
from jax.experimental import pallas as pl
from jax.experimental.pallas import tpu as pltpu
from jax.sharding import PartitionSpec as P

RANK = 64
BLOCKS = 4
F32 = jnp.float32
BF16 = jnp.bfloat16
NT = (((1,), (1,)), ((), ()))
RING = ("slab", "ex")


def in_hbm(x):
    return pltpu.with_memory_space_constraint(x, pltpu.HBM)


def split(x):
    hi = x.astype(BF16)
    return hi, (x - hi.astype(F32)).astype(BF16)


def rotate_kernel(
    half, lay_slots, query_hbm, block_hbm, damping_hbm, slot_hbm, out_hbm, in_hbm, eigen_hbm,
    result_ref, query_ref, block_ref, damping_ref, slot_ref, out_ref, in_ref, eigen_ref,
    rows_ref, basis_ref, turned_ref, sems,
):
    pairs = RANK * RANK // 128
    local = query_ref.shape[1]
    copies = [
        pltpu.make_async_copy(source, target, sems.at[k])
        for k, (source, target) in enumerate([
            (slot_hbm, slot_ref), (query_hbm, query_ref), (block_hbm, block_ref), (damping_hbm, damping_ref),
            (out_hbm, out_ref), (in_hbm, in_ref), (eigen_hbm, eigen_ref),
        ])
    ]
    for copy in copies:
        copy.start()
    slab = lax.axis_index("slab")
    first = (lax.axis_index("pb") * lax.axis_size("ex") + lax.axis_index("ex")) * local + slab * half
    low_lanes = lax.broadcasted_iota(jnp.int32, (RANK // 2, 128), 1) < RANK
    row = lax.broadcasted_iota(jnp.int32, (4 * RANK, 4 * RANK), 0) // RANK
    col = lax.broadcasted_iota(jnp.int32, (4 * RANK, 4 * RANK), 1) // RANK
    lane = lax.broadcasted_iota(jnp.int32, (1, 4 * RANK), 1) // RANK
    for copy in copies:
        copy.wait()
    model_layer = slot_ref[lax.axis_index("lay") * lay_slots]

    for pair in range(pairs):
        block = query_ref[0, :, pair * 128:(pair + 1) * 128].astype(F32)
        rows_ref[pair * half:(pair + 1) * half, :] = jnp.where(slab == 0, block[:half], block[half:2 * half])

    basis_ref[:, :RANK] = out_ref[model_layer].astype(F32)
    out_rows = jnp.concatenate(
        [basis_ref[pl.ds(0, RANK // 2, stride=2), :], basis_ref[pl.ds(1, RANK // 2, stride=2), :]], axis=0
    )
    out_t = out_rows.T[:RANK].astype(BF16)
    out_rows = out_rows[:, :RANK].astype(BF16)
    out_twice = jnp.concatenate([out_rows, out_rows], axis=1)
    out_t_twice = jnp.concatenate([out_t, out_t], axis=1)

    in_wide = jnp.concatenate([in_ref[model_layer].astype(F32)] * 4, axis=1)
    in_tall = jnp.concatenate([in_wide] * 4, axis=0)
    in_diag = jnp.where(row == col, in_tall, F32(0.0)).astype(BF16)
    eigen = jnp.concatenate([eigen_ref[model_layer]] * 4, axis=1)

    quads = range(half // 4)
    grids = []
    for quad in quads:
        tops, bottoms = [], []
        for two in range(2):
            at = quad * 4 + two * 2
            a = rows_ref[pl.ds(at, pairs, stride=half), :]
            b = rows_ref[pl.ds(at + 1, pairs, stride=half), :]
            tops.append(jnp.where(low_lanes, a, pltpu.roll(b, RANK, 1)))
            bottoms.append(jnp.where(low_lanes, pltpu.roll(a, RANK, 1), b))
        grids += [jnp.concatenate(tops, axis=1), jnp.concatenate(bottoms, axis=1)]
    right = jnp.dot(jnp.concatenate(grids, axis=0).astype(BF16), in_diag, preferred_element_type=F32)
    turned = []
    for quad in quads:
        part = right[quad * RANK:(quad + 1) * RANK]
        middle = jnp.dot(out_t_twice, jnp.concatenate(split(part), axis=0), preferred_element_type=F32)
        damp = jnp.zeros((1, 4 * RANK), F32)
        for one in range(4):
            block = block_ref[first + quad * 4 + one]
            value = F32(0.0)
            for k in range(BLOCKS):
                value = jnp.where(block == k, damping_ref[k], value)
            damp = jnp.where(lane == one, value, damp)
        scaled = middle / (eigen + damp)
        turned.append(jnp.dot(out_twice, jnp.concatenate(split(scaled), axis=0), preferred_element_type=F32))
    hi, lo = split(jnp.concatenate(turned, axis=0))
    result = lax.dot_general(hi, in_diag, NT, preferred_element_type=F32)
    result = result + lax.dot_general(lo, in_diag, NT, preferred_element_type=F32)
    for quad in quads:
        for two in range(2):
            at = quad * 4 + two * 2
            top = result[quad * RANK:quad * RANK + pairs, two * 128:(two + 1) * 128]
            bottom = result[quad * RANK + pairs:(quad + 1) * RANK, two * 128:(two + 1) * 128]
            turned_ref[pl.ds(at, pairs, stride=half), :] = jnp.where(low_lanes, top, pltpu.roll(bottom, RANK, 1))
            turned_ref[pl.ds(at + 1, pairs, stride=half), :] = jnp.where(low_lanes, pltpu.roll(top, RANK, 1), bottom)

    for pair in range(pairs):
        result_ref[:, pair * 128:(pair + 1) * 128] = turned_ref[pair * half:(pair + 1) * half, :].astype(BF16)


def rotate(query_grads, query_block, layer_slot, out_basis, in_basis, eigen_values, damping):
    half = query_grads.shape[1] // lax.axis_size("slab")
    dim = query_grads.shape[2]
    operands = (query_grads, query_block, damping, layer_slot, out_basis, in_basis, eigen_values)
    homes = (pltpu.VMEM, pltpu.SMEM, pltpu.SMEM, pltpu.SMEM, pltpu.VMEM, pltpu.VMEM, pltpu.VMEM)
    return pl.pallas_call(
        functools.partial(rotate_kernel, half, 1),
        out_shape=jax.ShapeDtypeStruct((half, dim), BF16),
        in_specs=[pl.BlockSpec(memory_space=pltpu.HBM)] * len(operands),
        out_specs=pl.BlockSpec(memory_space=pltpu.VMEM),
        scratch_shapes=[home(x.shape, x.dtype) for home, x in zip(homes, operands)] + [
            pltpu.VMEM((half * dim // 128, 128), F32),
            pltpu.VMEM((RANK, 128), F32),
            pltpu.VMEM((half * dim // 128, 128), F32),
            pltpu.SemaphoreType.DMA((len(operands),)),
        ],
        compiler_params=pltpu.CompilerParams(vmem_limit_bytes=16 << 20),
        cost_estimate=pl.CostEstimate(flops=8 * half * dim * 256, bytes_accessed=1 << 20, transcendentals=0),
        name="rotate",
    )(*map(in_hbm, operands))


def fetch_kernel(after_ref, store_hbm, store_ref, sems):
    del after_ref
    parts = sems.shape[0]
    rows = store_ref.shape[1] // parts
    copies = [
        pltpu.make_async_copy(
            store_hbm.at[:, pl.ds(k * rows, rows)], store_ref.at[:, pl.ds(k * rows, rows)], sems.at[k]
        )
        for k in range(parts)
    ]
    for copy in copies:
        copy.start()
    for copy in copies:
        copy.wait()


def fetch(after, store):
    return pl.pallas_call(
        fetch_kernel,
        out_shape=jax.ShapeDtypeStruct(store.shape, store.dtype),
        in_specs=[pl.BlockSpec(memory_space=pltpu.VMEM), pl.BlockSpec(memory_space=pltpu.HBM)],
        out_specs=pl.BlockSpec(memory_space=pltpu.VMEM),
        scratch_shapes=[pltpu.SemaphoreType.DMA((4,))],
        compiler_params=pltpu.CompilerParams(vmem_limit_bytes=8 << 20),
        cost_estimate=pl.CostEstimate(flops=0, bytes_accessed=2 * store.size * 2, transcendentals=0),
        name="fetch",
    )(after, in_hbm(store))


def score_kernel(count, height, share, shares, owners, *refs):
    outs, held = refs[-1 - len(owners):-1], refs[-1]
    pieces, store_ref = refs[:-2 - len(owners)], refs[-2 - len(owners)]
    half = pieces[0].shape[0]
    for k, piece in enumerate(pieces[:count]):
        held[k * height:k * height + half, :] = piece[...]
    for k, piece in enumerate(pieces[count:]):
        width = piece.shape[1]
        held[count * height:count * height + half, k * width:(k + 1) * width] = piece[...]
    lay = lax.axis_index("lay")
    for out, owner in zip(outs, owners):
        rows = pl.ds(pl.multiple_of(lax.rem(lay + owner, shares) * share, share), share)
        block = lax.dot_general(held[...], store_ref[0, rows, :], NT, preferred_element_type=F32)
        for j in range(out.shape[0] // half):
            out[j * half:(j + 1) * half, :] = block[j * height:j * height + half].astype(out.dtype)


def score(pieces, parts, store, owners):
    half = (pieces + parts)[0].shape[0]
    _, examples, dim = store.shape
    shares = lax.axis_size("lay")
    share = examples // shares
    whole = len(pieces) + (1 if parts else 0)
    height = -(-half // 16) * 16
    vmem = pl.BlockSpec(memory_space=pltpu.VMEM)
    return pl.pallas_call(
        functools.partial(score_kernel, len(pieces), height, share, shares, tuple(owners)),
        out_shape=[jax.ShapeDtypeStruct((whole * half, share), BF16 if owner else F32) for owner in owners],
        in_specs=[vmem] * (len(pieces) + len(parts) + 1),
        out_specs=[vmem] * len(owners),
        scratch_shapes=[pltpu.VMEM((whole * height, dim), BF16)],
        compiler_params=pltpu.CompilerParams(vmem_limit_bytes=24 << 20),
        cost_estimate=pl.CostEstimate(
            flops=2 * 256 * share * len(owners) * dim, bytes_accessed=1 << 20, transcendentals=0
        ),
        name="score",
    )(*pieces, *parts, store)


def swap_layers(sends):
    shares = lax.axis_size("lay")
    return [
        lax.ppermute(send, "lay", [(i, (i + k + 1) % shares) for i in range(shares)])
        for k, send in enumerate(sends)
    ]


def finish_kernel(half, members, sizes, *refs):
    out_ref = refs[-1]
    refs = refs[:-1]
    count = len(sizes)
    each = len(refs) // count
    slab, ex = lax.axis_index("slab"), lax.axis_index("ex")
    place = jnp.where(slab == 0, ex, 2 * members - 1 - ex)
    at = 0
    for k, size in enumerate(sizes):
        keep, got = refs[k * each], refs[k * each + 1:(k + 1) * each]
        for j in range(size):
            rows = slice(j * half, (j + 1) * half)
            total = keep[rows, :]
            for g in got:
                total = total + g[rows, :].astype(F32)
            distance = (at + 1) // 2
            hops = 2 * members - distance if at % 2 == 1 else distance
            source = lax.rem(place + hops, 2 * members)
            block = jnp.where(source < members, 2 * source, 2 * (2 * members - 1 - source) + 1)
            out_ref[pl.ds(pl.multiple_of(block * half, 8), half), :] = total
            at += 1


def finish(half, parts):
    members = lax.axis_size("ex")
    vmem = pl.BlockSpec(memory_space=pltpu.VMEM)
    flat = [array for keep, got in parts for array in [keep, *got]]
    sizes = [keep.shape[0] // half for keep, _ in parts]
    return pl.pallas_call(
        functools.partial(finish_kernel, half, members, sizes),
        out_shape=jax.ShapeDtypeStruct((2 * members * half, flat[0].shape[1]), F32),
        in_specs=[vmem] * len(flat),
        out_specs=vmem,
        compiler_params=pltpu.CompilerParams(vmem_limit_bytes=16 << 20),
        name="finish",
    )(*flat)


def local(
    store_grads, query_grads, query_block, layer_slot, out_basis, in_basis, eigen_values, damping
):
    members = lax.axis_size("ex")
    ring = list(range(members)) + [members + i for i in reversed(range(members))]
    forth = [(a, ring[(i + 1) % len(ring)]) for i, a in enumerate(ring)]
    back = [(b, a) for a, b in forth]
    own = rotate(query_grads, query_block, layer_slot, out_basis, in_basis, eigen_values, damping)
    store = fetch(own, store_grads)
    half, dim = own.shape
    others = range(1, lax.axis_size("lay"))
    one = two = own
    batch, sums, hidden = [own], [], store
    for step in range(1, members):
        one, two = lax.ppermute(one, RING, forth), lax.ppermute(two, RING, back)
        one, two, hidden = lax.optimization_barrier((one, two, hidden))
        if step == 1:
            store = hidden
        elif hidden:
            sums.append((keep, swap_layers(hidden)))
        hidden = []
        batch += [one, two]
        if len(batch) >= 5 and step < members - 1:
            keep, *hidden = score(batch, [], store, [0, *others])
            batch = []
    parts = [lax.ppermute(one[:, :dim // 2], RING, forth), lax.ppermute(two[:, dim // 2:], RING, back)]
    got = swap_layers(score(batch, parts, store, others))
    sums.append((*score(batch, parts, store, [0]), got))
    return finish(half, sums).T


def solution(mesh):
    return jax.shard_map(
        local,
        mesh=mesh,
        in_specs=(
            P("lay", ("slab", "ex"), None),
            P("lay", ("pb", "ex"), None),
            P(),
            P(),
            P(),
            P(),
            P(),
            P(),
        ),
        out_specs=P(("slab", "ex", "lay"), "pb"),
        check_vma=False,
    )
```

time: 42.7 us -> 36.8 us (0.86)
  local copies, waits for them, and re-layouts: 7.55 us -> 0.02 us
  waiting for transfers between devices: 10.8 us -> 15.6 us
  starting transfers between devices: 16.1 us -> 12.6 us
  Pallas kernels: 7.83 us -> 8.38 us
    unnamed x18 -> x0, local copies, waits for them, and re-layouts: 7.53 us -> none
    ppermute x8, waiting for transfers between devices: 7.47 us -> 14.1 us  [the longest x6 12.6 us: local(): one, two = (lax.ppermute(one, RING, forth), lax.ppermute(two, RING, back))]
    ppermute x8, starting transfers between devices: 13.5 us -> 9.27 us  [the longest x6 7.19 us: local(): one, two = (lax.ppermute(one, RING, forth), lax.ppermute(two, RING, back))]
    pallas_call x0 -> x1, Pallas kernels: none -> 2.2 us  [fetch(): pl.pallas_call(fetch_kernel, out_shape=jax.ShapeDtypeStruct(store.shape,...]
    ppermute x3 -> x2, waiting for transfers between devices: 3.28 us -> 1.44 us  [swap_layers(): lax.ppermute(send, 'lay', [(i, (i + k + 1) % shares) for i in range(share...]
    pallas_call x3, Pallas kernels: 4.19 us -> 3.05 us  [score(): pl.pallas_call(functools.partial(score_kernel, len(pieces), height, share...]
    ppermute x3 -> x2, starting transfers between devices: 2.65 us -> 3.3 us  [swap_layers(): lax.ppermute(send, 'lay', [(i, (i + k + 1) % shares) for i in range(share...]
    pallas_call x1, Pallas kernels: 2.93 us -> 2.41 us  [rotate(): pl.pallas_call(functools.partial(rotate_kernel, half, 1), out_shape=jax.S...]
  transfers between devices with their start and end apart: 11 -> 10, of which waited for: 6 -> 9; matrix products, arithmetic and copies ran while one was open for 0% -> 0% of each run, Pallas kernels for 10% -> 14%
where the time goes in v2:
time: 36.8 us; the launch traced here: 36.6 us
  waiting for transfers between devices  15.6 us (42%)
  starting transfers between devices  12.6 us (34%)
  Pallas kernels  8.38 us (23%)
    ppermute x6, waiting for transfers between devices, local(): one, two = (lax.ppermute(one, RING, forth), lax.ppermute(two, RING, back))  12.6 us
    ppermute x6, starting transfers between devices, local(): one, two = (lax.ppermute(one, RING, forth), lax.ppermute(two, RING, back))  7.19 us
    ppermute x2, starting transfers between devices, swap_layers(): lax.ppermute(send, 'lay', [(i, (i + k + 1) % shares) for i in range(share...  3.3 us
    pallas_call x3, Pallas kernels, score(): pl.pallas_call(functools.partial(score_kernel, len(pieces), height, share...  3.05 us
    pallas_call x1, Pallas kernels, rotate(): pl.pallas_call(functools.partial(rotate_kernel, half, 1), out_shape=jax.S...  2.41 us
    pallas_call x1, Pallas kernels, fetch(): pl.pallas_call(fetch_kernel, out_shape=jax.ShapeDtypeStruct(store.shape,...  2.2 us
    ppermute x1, starting transfers between devices, local(): lax.ppermute(one[:, :dim // 2], RING, forth)  1.61 us
    ppermute x2, waiting for transfers between devices, swap_layers(): lax.ppermute(send, 'lay', [(i, (i + k + 1) % shares) for i in range(share...  1.44 us
  transfers between devices with their start and end apart: 10, of which 9 were waited for; matrix products, arithmetic and copies ran while one was open for 0% of the time, Pallas kernels for 14%

profile of v2, /device:TPU:0, one launch (start us, length us, event | category | flops | bytes accessed | tf_op | source)
XLA Modules:
  0.0 36.6 jit_solution(2519047839793973154)
XLA Ops:
  0.0 2.4 %rotate.1.after_ref.refs_0_ = bf16[24,4096]{1,0:T(8,128)(2,1)S(1)} custom-call(bf16[1,48,4096]{2,1,0:T(8,128)(2,1)} %query_hbm.1, s32[384]{0:T(512)} %block_hbm.1, f32[4]{0:T(128)} %damping_hbm.1, s32[2]{0:T(128)} %slot_hbm.1, bf16[2,64,64]{2,1,0:T(8,128)(2,1)} %out_hbm.1, bf16[2,64,64]{2,1,0:T(8,128)(2,1)} %in_hbm.1, f32[2,64,64]{2,1,0:T(8,128)} %eigen_hbm.1), custom_call_target="tpu_custom_call" | custom-call | flops 201326592 | bytes 1048576 | tf_op jit(solution)/shard_map/rotate/pallas_call | solution.py:116
  2.4 3.0 %collective-permute-start.1 = (bf16[24,4096]{1,0:T(8,128)(2,1)S(1)}, bf16[24,4096]{1,0:T(8,128)(2,1)S(1)}, u32[]{:S(2)}, u32[]{:S(2)}) collective-permute-start(bf16[24,4096]{1,0:T(8,128)(2,1)S(1)} %rotate.1.after_ref.refs_0_), channel_id=1, source_target_pairs={{4,0},{8,4},{12,8},{28,12},{24,28},{20,24},{16,20},{0,16},{5,1},{9... | collective-permute-start | bytes 589832 | tf_op jit(solution)/shard_map/ppermute | solution.py:261
  5.4 0.1 collective-permute-start
  5.6 2.2 %fetch.1.refs_5_.refs_4_ = bf16[1,512,4096]{2,1,0:T(8,128)(2,1)S(1)} custom-call(bf16[24,4096]{1,0:T(8,128)(2,1)S(1)} %rotate.1.after_ref.refs_0_, bf16[1,512,4096]{2,1,0:T(8,128)(2,1)} %store_hbm.1), custom_call_target="tpu_custom_call" | custom-call | bytes 8388608 | tf_op jit(solution)/shard_map/fetch/pallas_call | solution.py:150
  7.8 2.6 %collective-permute-done.1.refs_2_ = bf16[24,4096]{1,0:T(8,128)(2,1)S(1)} collective-permute-done((bf16[24,4096]{1,0:T(8,128)(2,1)S(1)}, bf16[24,4096]{1,0:T(8,128)(2,1)S(1)}, u32[]{:S(2)}, u32[]{:S(2)}) %collective-permute-start.1) | collective-permute-done | bytes 196640 | tf_op jit(solution)/shard_map/ppermute | solution.py:261
  10.4 1.4 %collective-permute-done.refs_1_ = bf16[24,4096]{1,0:T(8,128)(2,1)S(1)} collective-permute-done((bf16[24,4096]{1,0:T(8,128)(2,1)S(1)}, bf16[24,4096]{1,0:T(8,128)(2,1)S(1)}, u32[]{:S(2)}, u32[]{:S(2)}) %collective-permute-start) | collective-permute-done | bytes 196640 | tf_op jit(solution)/shard_map/ppermute | solution.py:261
  11.8 0.4 %collective-permute-start.2 = (bf16[24,4096]{1,0:T(8,128)(2,1)S(1)}, bf16[24,4096]{1,0:T(8,128)(2,1)S(1)}, u32[]{:S(2)}, u32[]{:S(2)}) collective-permute-start(bf16[24,4096]{1,0:T(8,128)(2,1)S(1)} %collective-permute-done.refs_1_), channel_id=1, source_target_pairs={{0,4},{4,8},{8,12},{12,28},{28,24},{24,20},{20,16},{16,0},{1,5},{5... | collective-permute-start | bytes 589832 | tf_op jit(solution)/shard_map/ppermute | solution.py:261
  12.2 1.6 %collective-permute-start.3 = (bf16[24,4096]{1,0:T(8,128)(2,1)S(1)}, bf16[24,4096]{1,0:T(8,128)(2,1)S(1)}, u32[]{:S(2)}, u32[]{:S(2)}) collective-permute-start(bf16[24,4096]{1,0:T(8,128)(2,1)S(1)} %collective-permute-done.1.refs_2_), channel_id=1, source_target_pairs={{4,0},{8,4},{12,8},{28,12},{24,28},{20,24},{16,20},{0,16},{5,1},{9... | collective-permute-start | bytes 589832 | tf_op jit(solution)/shard_map/ppermute | solution.py:261
  13.8 3.6 %collective-permute-done.2.refs_3_ = bf16[24,4096]{1,0:T(8,128)(2,1)S(1)} collective-permute-done((bf16[24,4096]{1,0:T(8,128)(2,1)S(1)}, bf16[24,4096]{1,0:T(8,128)(2,1)S(1)}, u32[]{:S(2)}, u32[]{:S(2)}) %collective-permute-start.2) | collective-permute-done | bytes 196640 | tf_op jit(solution)/shard_map/ppermute | solution.py:261
  17.5 0.4 %collective-permute-done.3.refs_4_ = bf16[24,4096]{1,0:T(8,128)(2,1)S(1)} collective-permute-done((bf16[24,4096]{1,0:T(8,128)(2,1)S(1)}, bf16[24,4096]{1,0:T(8,128)(2,1)S(1)}, u32[]{:S(2)}, u32[]{:S(2)}) %collective-permute-start.3) | collective-permute-done | bytes 196640 | tf_op jit(solution)/shard_map/ppermute | solution.py:261
  17.9 1.7 %collective-permute-start.4 = (bf16[24,4096]{1,0:T(8,128)(2,1)S(1)}, bf16[24,4096]{1,0:T(8,128)(2,1)S(1)}, u32[]{:S(2)}, u32[]{:S(2)}) collective-permute-start(bf16[24,4096]{1,0:T(8,128)(2,1)S(1)} %collective-permute-done.2.refs_3_), channel_id=1, source_target_pairs={{0,4},{4,8},{8,12},{12,28},{28,24},{24,20},{20,16},{16,0},{1,5},{5... | collective-permute-start | bytes 589832 | tf_op jit(solution)/shard_map/ppermute | solution.py:261
  19.6 0.3 collective-permute-start.5
  19.9 1.5 %score.3 = (f32[120,256]{1,0:T(8,128)S(1)}, bf16[120,256]{1,0:T(8,128)(2,1)S(1)}) custom-call(bf16[24,4096]{1,0:T(8,128)(2,1)S(1)} %rotate.1.after_ref.refs_0_, bf16[24,4096]{1,0:T(8,128)(2,1)S(1)} %collective-permute-done.refs_1_, bf16[24,4096]{1,0:T(8,128)(2,1)S(1)} %collective-permute-done.1.refs_2_, bf16[24,4096]{1,0:T(8,128)(2,1)S(1)} %collective-permute-done.2.refs_3_, ...), custom_call_target="tpu_custom_call" | custom-call | flops 1073741824 | bytes 1048576 | tf_op jit(solution)/shard_map/score/pallas_call | solution.py:187
  21.4 2.1 %collective-permute-done.4.refs_0_ = bf16[24,4096]{1,0:T(8,128)(2,1)S(1)} collective-permute-done((bf16[24,4096]{1,0:T(8,128)(2,1)S(1)}, bf16[24,4096]{1,0:T(8,128)(2,1)S(1)}, u32[]{:S(2)}, u32[]{:S(2)}) %collective-permute-start.4) | collective-permute-done | bytes 196640 | tf_op jit(solution)/shard_map/ppermute | solution.py:261
  23.5 2.4 %collective-permute-done.5.refs_1_ = bf16[24,4096]{1,0:T(8,128)(2,1)S(1)} collective-permute-done((bf16[24,4096]{1,0:T(8,128)(2,1)S(1)}, bf16[24,4096]{1,0:T(8,128)(2,1)S(1)}, u32[]{:S(2)}, u32[]{:S(2)}) %collective-permute-start.5) | collective-permute-done | bytes 196640 | tf_op jit(solution)/shard_map/ppermute | solution.py:261
  26.0 0.5 %collective-permute-start.8 = (bf16[24,2048]{1,0:T(8,128)(2,1)S(1)}, bf16[24,2048]{1,0:T(8,128)(2,1)S(1)}, u32[]{:S(2)}, u32[]{:S(2)}) collective-permute-start(bf16[24,2048]{1,0:T(8,128)(2,1)S(1)} %slice.7), channel_id=1, source_target_pairs={{4,0},{8,4},{12,8},{28,12},{24,28},{20,24},{16,20},{0,16},{5,1},{9... | collective-permute-start | bytes 294920 | tf_op jit(solution)/shard_map/ppermute | solution.py:272
  26.5 1.6 %collective-permute-start.7 = (bf16[24,2048]{1,0:T(8,128)(2,1)S(1)}, bf16[24,2048]{1,0:T(8,128)(2,1)S(1)}, u32[]{:S(2)}, u32[]{:S(2)}) collective-permute-start(bf16[24,2048]{1,0:T(8,128)(2,1)S(1)} %slice.6), channel_id=1, source_target_pairs={{0,4},{4,8},{8,12},{12,28},{28,24},{24,20},{20,16},{16,0},{1,5},{5... | collective-permute-start | bytes 294920 | tf_op jit(solution)/shard_map/ppermute | solution.py:272
  28.1 1.5 %collective-permute-start.6 = (bf16[120,256]{1,0:T(8,128)(2,1)S(1)}, bf16[120,256]{1,0:T(8,128)(2,1)S(1)}, u32[]{:S(2)}, u32[]{:S(2)}) collective-permute-start(bf16[120,256]{1,0:T(8,128)(2,1)S(1)} %get-tuple-element.22), channel_id=1, source_target_pairs={{0,2},{2,0},{1,3},{3,1},{4,6},{6,4},{5,7},{7,5},{8,10},{10,8},{9,1... | collective-permute-start | bytes 184328 | tf_op jit(solution)/shard_map/ppermute | solution.py:204
  29.6 1.1 %collective-permute-done.8.refs_3_ = bf16[24,2048]{1,0:T(8,128)(2,1)S(1)} collective-permute-done((bf16[24,2048]{1,0:T(8,128)(2,1)S(1)}, bf16[24,2048]{1,0:T(8,128)(2,1)S(1)}, u32[]{:S(2)}, u32[]{:S(2)}) %collective-permute-start.8) | collective-permute-done | bytes 98336 | tf_op jit(solution)/shard_map/ppermute | solution.py:272
  30.7 0.4 %collective-permute-done.7.refs_2_ = bf16[24,2048]{1,0:T(8,128)(2,1)S(1)} collective-permute-done((bf16[24,2048]{1,0:T(8,128)(2,1)S(1)}, bf16[24,2048]{1,0:T(8,128)(2,1)S(1)}, u32[]{:S(2)}, u32[]{:S(2)}) %collective-permute-start.7) | collective-permute-done | bytes 98336 | tf_op jit(solution)/shard_map/ppermute | solution.py:272
  31.1 0.8 %score.5 = bf16[72,256]{1,0:T(8,128)(2,1)S(1)} custom-call(bf16[24,4096]{1,0:T(8,128)(2,1)S(1)} %collective-permute-done.4.refs_0_, bf16[24,4096]{1,0:T(8,128)(2,1)S(1)} %collective-permute-done.5.refs_1_, bf16[24,2048]{1,0:T(8,128)(2,1)S(1)} %collective-permute-done.7.refs_2_, bf16[24,2048]{1,0:T(8,128)(2,1)S(1)} %collective-permute-done.8.refs_3_, ...), custom_call_target="tpu_custom_call" | custom-call | flops 536870912 | bytes 1048576 | tf_op jit(solution)/shard_map/score/pallas_call | solution.py:187
  31.9 1.8 %collective-permute-start.9 = (bf16[72,256]{1,0:T(8,128)(2,1)S(1)}, bf16[72,256]{1,0:T(8,128)(2,1)S(1)}, u32[]{:S(2)}, u32[]{:S(2)}) collective-permute-start(bf16[72,256]{1,0:T(8,128)(2,1)S(1)} %score.5), channel_id=1, source_target_pairs={{0,2},{2,0},{1,3},{3,1},{4,6},{6,4},{5,7},{7,5},{8,10},{10,8},{9,1... | collective-permute-start | bytes 110600 | tf_op jit(solution)/shard_map/ppermute | solution.py:204
  33.7 0.8 %score.4.refs_2_ = f32[72,256]{1,0:T(8,128)S(1)} custom-call(bf16[24,4096]{1,0:T(8,128)(2,1)S(1)} %collective-permute-done.4.refs_0_, bf16[24,4096]{1,0:T(8,128)(2,1)S(1)} %collective-permute-done.5.refs_1_, bf16[24,2048]{1,0:T(8,128)(2,1)S(1)} %collective-permute-done.7.refs_2_, bf16[24,2048]{1,0:T(8,128)(2,1)S(1)} %collective-permute-done.8.refs_3_, ...), custom_call_target="tpu_custom_call" | custom-call | flops 536870912 | bytes 1048576 | tf_op jit(solution)/shard_map/score/pallas_call | solution.py:187
  34.4 0.0 collective-permute-done.6.refs_1_
  34.5 1.4 %collective-permute-done.9.refs_3_ = bf16[72,256]{1,0:T(8,128)(2,1)S(1)} collective-permute-done((bf16[72,256]{1,0:T(8,128)(2,1)S(1)}, bf16[72,256]{1,0:T(8,128)(2,1)S(1)}, u32[]{:S(2)}, u32[]{:S(2)}) %collective-permute-start.9) | collective-permute-done | bytes 36896 | tf_op jit(solution)/shard_map/ppermute | solution.py:204
  35.9 0.7 %finish.1 = f32[192,256]{1,0:T(8,128)} custom-call(f32[120,256]{1,0:T(8,128)S(1)} %get-tuple-element.20.refs_0_, bf16[120,256]{1,0:T(8,128)(2,1)S(1)} %collective-permute-done.6.refs_1_, f32[72,256]{1,0:T(8,128)S(1)} %score.4.refs_2_, bf16[72,256]{1,0:T(8,128)(2,1)S(1)} %collective-permute-done.9.refs_3_), custom_call_target="tpu_custom_call" | custom-call | tf_op jit(solution)/shard_map/finish/pallas_call | solution.py:237
  (2 shorter events, 0.0 us)
Async XLA Ops:
  2.4 8.0 %collective-permute-start.1 = (bf16[24,4096]{1,0:T(8,128)(2,1)S(1)}, bf16[24,4096]{1,0:T(8,128)(2,1)S(1)}, u32[]{:S(2)}, u32[]{:S(2)}) collective-permute-start(bf16[24,4096]{1,0:T(8,128)(2,1)S(1)} %rotate.1.after_ref.refs_0_), channel_id=1, source_target_pairs={{4,0},{8,4},{12,8},{28,12},{24,28},{20,24},{16,20},{0,16},{5,1},{9... | collective-permute-start | bytes 589832 | tf_op jit(solution)/shard_map/ppermute | solution.py:261
  5.4 6.4 %collective-permute-start = (bf16[24,4096]{1,0:T(8,128)(2,1)S(1)}, bf16[24,4096]{1,0:T(8,128)(2,1)S(1)}, u32[]{:S(2)}, u32[]{:S(2)}) collective-permute-start(bf16[24,4096]{1,0:T(8,128)(2,1)S(1)} %rotate.1.after_ref.refs_0_), channel_id=1, source_target_pairs={{0,4},{4,8},{8,12},{12,28},{28,24},{24,20},{20,16},{16,0},{1,5},{5... | collective-permute-start | bytes 589832 | tf_op jit(solution)/shard_map/ppermute | solution.py:261
  11.8 5.7 %collective-permute-start.2 = (bf16[24,4096]{1,0:T(8,128)(2,1)S(1)}, bf16[24,4096]{1,0:T(8,128)(2,1)S(1)}, u32[]{:S(2)}, u32[]{:S(2)}) collective-permute-start(bf16[24,4096]{1,0:T(8,128)(2,1)S(1)} %collective-permute-done.refs_1_), channel_id=1, source_target_pairs={{0,4},{4,8},{8,12},{12,28},{28,24},{24,20},{20,16},{16,0},{1,5},{5... | collective-permute-start | bytes 589832 | tf_op jit(solution)/shard_map/ppermute | solution.py:261
  12.2 5.7 %collective-permute-start.3 = (bf16[24,4096]{1,0:T(8,128)(2,1)S(1)}, bf16[24,4096]{1,0:T(8,128)(2,1)S(1)}, u32[]{:S(2)}, u32[]{:S(2)}) collective-permute-start(bf16[24,4096]{1,0:T(8,128)(2,1)S(1)} %collective-permute-done.1.refs_2_), channel_id=1, source_target_pairs={{4,0},{8,4},{12,8},{28,12},{24,28},{20,24},{16,20},{0,16},{5,1},{9... | collective-permute-start | bytes 589832 | tf_op jit(solution)/shard_map/ppermute | solution.py:261
  17.9 5.7 %collective-permute-start.4 = (bf16[24,4096]{1,0:T(8,128)(2,1)S(1)}, bf16[24,4096]{1,0:T(8,128)(2,1)S(1)}, u32[]{:S(2)}, u32[]{:S(2)}) collective-permute-start(bf16[24,4096]{1,0:T(8,128)(2,1)S(1)} %collective-permute-done.2.refs_3_), channel_id=1, source_target_pairs={{0,4},{4,8},{8,12},{12,28},{28,24},{24,20},{20,16},{16,0},{1,5},{5... | collective-permute-start | bytes 589832 | tf_op jit(solution)/shard_map/ppermute | solution.py:261
  19.6 6.4 %collective-permute-start.5 = (bf16[24,4096]{1,0:T(8,128)(2,1)S(1)}, bf16[24,4096]{1,0:T(8,128)(2,1)S(1)}, u32[]{:S(2)}, u32[]{:S(2)}) collective-permute-start(bf16[24,4096]{1,0:T(8,128)(2,1)S(1)} %collective-permute-done.3.refs_4_), channel_id=1, source_target_pairs={{4,0},{8,4},{12,8},{28,12},{24,28},{20,24},{16,20},{0,16},{5,1},{9... | collective-permute-start | bytes 589832 | tf_op jit(solution)/shard_map/ppermute | solution.py:261
  26.0 4.7 %collective-permute-start.8 = (bf16[24,2048]{1,0:T(8,128)(2,1)S(1)}, bf16[24,2048]{1,0:T(8,128)(2,1)S(1)}, u32[]{:S(2)}, u32[]{:S(2)}) collective-permute-start(bf16[24,2048]{1,0:T(8,128)(2,1)S(1)} %slice.7), channel_id=1, source_target_pairs={{4,0},{8,4},{12,8},{28,12},{24,28},{20,24},{16,20},{0,16},{5,1},{9... | collective-permute-start | bytes 294920 | tf_op jit(solution)/shard_map/ppermute | solution.py:272
  26.5 4.6 %collective-permute-start.7 = (bf16[24,2048]{1,0:T(8,128)(2,1)S(1)}, bf16[24,2048]{1,0:T(8,128)(2,1)S(1)}, u32[]{:S(2)}, u32[]{:S(2)}) collective-permute-start(bf16[24,2048]{1,0:T(8,128)(2,1)S(1)} %slice.6), channel_id=1, source_target_pairs={{0,4},{4,8},{8,12},{12,28},{28,24},{24,20},{20,16},{16,0},{1,5},{5... | collective-permute-start | bytes 294920 | tf_op jit(solution)/shard_map/ppermute | solution.py:272
  28.1 6.4 %collective-permute-start.6 = (bf16[120,256]{1,0:T(8,128)(2,1)S(1)}, bf16[120,256]{1,0:T(8,128)(2,1)S(1)}, u32[]{:S(2)}, u32[]{:S(2)}) collective-permute-start(bf16[120,256]{1,0:T(8,128)(2,1)S(1)} %get-tuple-element.22), channel_id=1, source_target_pairs={{0,2},{2,0},{1,3},{3,1},{4,6},{6,4},{5,7},{7,5},{8,10},{10,8},{9,1... | collective-permute-start | bytes 184328 | tf_op jit(solution)/shard_map/ppermute | solution.py:204
  31.9 4.0 %collective-permute-start.9 = (bf16[72,256]{1,0:T(8,128)(2,1)S(1)}, bf16[72,256]{1,0:T(8,128)(2,1)S(1)}, u32[]{:S(2)}, u32[]{:S(2)}) collective-permute-start(bf16[72,256]{1,0:T(8,128)(2,1)S(1)} %score.5), channel_id=1, source_target_pairs={{0,2},{2,0},{1,3},{3,1},{4,6},{6,4},{5,7},{7,5},{8,10},{10,8},{9,1... | collective-permute-start | bytes 110600 | tf_op jit(solution)/shard_map/ppermute | solution.py:204

commit v3 on v2

--- a/solution.py
+++ b/solution.py
@@ -25,9 +25,9 @@
 
 
 def rotate_kernel(
-    half, lay_slots, query_hbm, block_hbm, damping_hbm, slot_hbm, out_hbm, in_hbm, eigen_hbm,
-    result_ref, query_ref, block_ref, damping_ref, slot_ref, out_ref, in_ref, eigen_ref,
-    rows_ref, basis_ref, turned_ref, sems,
+    half, lay_slots, query_hbm, block_hbm, damping_hbm, slot_hbm, out_hbm, in_hbm, eigen_hbm, store_hbm,
+    result_ref, store_ref, query_ref, block_ref, damping_ref, slot_ref, out_ref, in_ref, eigen_ref,
+    rows_ref, basis_ref, turned_ref, sems, store_sems,
 ):
     pairs = RANK * RANK // 128
     local = query_ref.shape[1]
@@ -38,7 +38,14 @@
             (out_hbm, out_ref), (in_hbm, in_ref), (eigen_hbm, eigen_ref),
         ])
     ]
-    for copy in copies:
+    stretch = store_ref.shape[1] // store_sems.shape[0]
+    store_copies = [
+        pltpu.make_async_copy(
+            store_hbm.at[:, pl.ds(k * stretch, stretch)], store_ref.at[:, pl.ds(k * stretch, stretch)], store_sems.at[k]
+        )
+        for k in range(store_sems.shape[0])
+    ]
+    for copy in copies + store_copies:
         copy.start()
     slab = lax.axis_index("slab")
     first = (lax.axis_index("pb") * lax.axis_size("ex") + lax.axis_index("ex")) * local + slab * half
@@ -106,57 +113,31 @@
 
     for pair in range(pairs):
         result_ref[:, pair * 128:(pair + 1) * 128] = turned_ref[pair * half:(pair + 1) * half, :].astype(BF16)
-
-
-def rotate(query_grads, query_block, layer_slot, out_basis, in_basis, eigen_values, damping):
+    for copy in store_copies:
+        copy.wait()
+
+
+def rotate(query_grads, query_block, layer_slot, out_basis, in_basis, eigen_values, damping, store):
     half = query_grads.shape[1] // lax.axis_size("slab")
     dim = query_grads.shape[2]
     operands = (query_grads, query_block, damping, layer_slot, out_basis, in_basis, eigen_values)
     homes = (pltpu.VMEM, pltpu.SMEM, pltpu.SMEM, pltpu.SMEM, pltpu.VMEM, pltpu.VMEM, pltpu.VMEM)
     return pl.pallas_call(
         functools.partial(rotate_kernel, half, 1),
-        out_shape=jax.ShapeDtypeStruct((half, dim), BF16),
-        in_specs=[pl.BlockSpec(memory_space=pltpu.HBM)] * len(operands),
-        out_specs=pl.BlockSpec(memory_space=pltpu.VMEM),
+        out_shape=[jax.ShapeDtypeStruct((half, dim), BF16), jax.ShapeDtypeStruct(store.shape, store.dtype)],
+        in_specs=[pl.BlockSpec(memory_space=pltpu.HBM)] * (len(operands) + 1),
+        out_specs=[pl.BlockSpec(memory_space=pltpu.VMEM)] * 2,
         scratch_shapes=[home(x.shape, x.dtype) for home, x in zip(homes, operands)] + [
             pltpu.VMEM((half * dim // 128, 128), F32),
             pltpu.VMEM((RANK, 128), F32),
             pltpu.VMEM((half * dim // 128, 128), F32),
             pltpu.SemaphoreType.DMA((len(operands),)),
+            pltpu.SemaphoreType.DMA((4,)),
         ],
         compiler_params=pltpu.CompilerParams(vmem_limit_bytes=16 << 20),
         cost_estimate=pl.CostEstimate(flops=8 * half * dim * 256, bytes_accessed=1 << 20, transcendentals=0),
         name="rotate",
-    )(*map(in_hbm, operands))
-
-
-def fetch_kernel(after_ref, store_hbm, store_ref, sems):
-    del after_ref
-    parts = sems.shape[0]
-    rows = store_ref.shape[1] // parts
-    copies = [
-        pltpu.make_async_copy(
-            store_hbm.at[:, pl.ds(k * rows, rows)], store_ref.at[:, pl.ds(k * rows, rows)], sems.at[k]
-        )
-        for k in range(parts)
-    ]
-    for copy in copies:
-        copy.start()
-    for copy in copies:
-        copy.wait()
-
-
-def fetch(after, store):
-    return pl.pallas_call(
-        fetch_kernel,
-        out_shape=jax.ShapeDtypeStruct(store.shape, store.dtype),
-        in_specs=[pl.BlockSpec(memory_space=pltpu.VMEM), pl.BlockSpec(memory_space=pltpu.HBM)],
-        out_specs=pl.BlockSpec(memory_space=pltpu.VMEM),
-        scratch_shapes=[pltpu.SemaphoreType.DMA((4,))],
-        compiler_params=pltpu.CompilerParams(vmem_limit_bytes=8 << 20),
-        cost_estimate=pl.CostEstimate(flops=0, bytes_accessed=2 * store.size * 2, transcendentals=0),
-        name="fetch",
-    )(after, in_hbm(store))
+    )(*map(in_hbm, operands), in_hbm(store))
 
 
 def score_kernel(count, height, share, shares, owners, *refs):
@@ -251,20 +232,19 @@
     ring = list(range(members)) + [members + i for i in reversed(range(members))]
     forth = [(a, ring[(i + 1) % len(ring)]) for i, a in enumerate(ring)]
     back = [(b, a) for a, b in forth]
-    own = rotate(query_grads, query_block, layer_slot, out_basis, in_basis, eigen_values, damping)
-    store = fetch(own, store_grads)
+    own, store = rotate(
+        query_grads, query_block, layer_slot, out_basis, in_basis, eigen_values, damping, store_grads
+    )
     half, dim = own.shape
     others = range(1, lax.axis_size("lay"))
     one = two = own
-    batch, sums, hidden = [own], [], store
+    batch, sums, hidden = [own], [], []
     for step in range(1, members):
         one, two = lax.ppermute(one, RING, forth), lax.ppermute(two, RING, back)
-        one, two, hidden = lax.optimization_barrier((one, two, hidden))
-        if step == 1:
-            store = hidden
-        elif hidden:
+        if hidden:
+            two, hidden = lax.optimization_barrier((two, hidden))
             sums.append((keep, swap_layers(hidden)))
-        hidden = []
+            hidden = []
         batch += [one, two]
         if len(batch) >= 5 and step < members - 1:
             keep, *hidden = score(batch, [], store, [0, *others])

time: 36.8 us -> 35.3 us (0.959)
  Pallas kernels: 8.38 us -> 7.14 us
  waiting for transfers between devices: 15.6 us -> 15.2 us
    ppermute x6, waiting for transfers between devices: 12.6 us -> 11.1 us  [local(): one, two = (lax.ppermute(one, RING, forth), lax.ppermute(two, RING, back))]
    ppermute x1, waiting for transfers between devices: 0.41 us -> 1.75 us  [local(): lax.ppermute(one[:, :dim // 2], RING, forth)]
    ppermute x1, starting transfers between devices: 0.46 us -> 1.74 us  [local(): lax.ppermute(two[:, dim // 2:], RING, back)]
    pallas_call x2 -> x1, Pallas kernels: 4.62 us -> 3.37 us  [rotate(): pl.pallas_call(functools.partial(rotate_kernel, half, 1), out_shape=[jax....]
    ppermute x1, starting transfers between devices: 1.61 us -> 0.54 us  [local(): lax.ppermute(one[:, :dim // 2], RING, forth)]
  transfers between devices with their start and end apart: 10 -> 10, of which waited for: 9 -> 6; matrix products, arithmetic and copies ran while one was open for 0% -> 0% of each run, Pallas kernels for 14% -> 9%
where the time goes in v3:
time: 35.3 us; the launch traced here: 35.1 us
  waiting for transfers between devices  15.2 us (43%)
  starting transfers between devices  12.7 us (36%)
  Pallas kernels  7.14 us (20%)
    ppermute x6, waiting for transfers between devices, local(): one, two = (lax.ppermute(one, RING, forth), lax.ppermute(two, RING, back))  11.1 us
    ppermute x6, starting transfers between devices, local(): one, two = (lax.ppermute(one, RING, forth), lax.ppermute(two, RING, back))  7.19 us
    pallas_call x1, Pallas kernels, rotate(): pl.pallas_call(functools.partial(rotate_kernel, half, 1), out_shape=[jax....  3.37 us
    ppermute x2, starting transfers between devices, swap_layers(): lax.ppermute(send, 'lay', [(i, (i + k + 1) % shares) for i in range(share...  3.21 us
    pallas_call x3, Pallas kernels, score(): pl.pallas_call(functools.partial(score_kernel, len(pieces), height, share...  3.05 us
    ppermute x1, waiting for transfers between devices, local(): lax.ppermute(one[:, :dim // 2], RING, forth)  1.75 us
    ppermute x1, starting transfers between devices, local(): lax.ppermute(two[:, dim // 2:], RING, back)  1.74 us
    ppermute x2, waiting for transfers between devices, swap_layers(): lax.ppermute(send, 'lay', [(i, (i + k + 1) % shares) for i in range(share...  1.68 us
  transfers between devices with their start and end apart: 10, of which 6 were waited for; matrix products, arithmetic and copies ran while one was open for 0% of the time, Pallas kernels for 9%

profile of v3, /device:TPU:0, one launch (start us, length us, event | category | flops | bytes accessed | tf_op | source)
XLA Modules:
  0.0 35.1 jit_solution(7350795333208380298)
XLA Ops:
  0.0 3.4 %rotate.1 = (bf16[24,4096]{1,0:T(8,128)(2,1)S(1)}, bf16[1,512,4096]{2,1,0:T(8,128)(2,1)S(1)}) custom-call(bf16[1,48,4096]{2,1,0:T(8,128)(2,1)} %query_hbm.1, s32[384]{0:T(512)} %block_hbm.1, f32[4]{0:T(128)} %damping_hbm.1, s32[2]{0:T(128)} %slot_hbm.1, bf16[2,64,64]{2,1,0:T(8,128)(2,1)} %out_hbm.1, bf16[2,64,64]{2,1,0:T(8,128)(2,1)} %in_hbm.1, ...), custom_call_target="tpu_custom_call" | custom-call | flops 201326592 | bytes 1048576 | tf_op jit(solution)/shard_map/rotate/pallas_call | solution.py:125
  3.4 3.0 %collective-permute-start.1 = (bf16[24,4096]{1,0:T(8,128)(2,1)S(1)}, bf16[24,4096]{1,0:T(8,128)(2,1)S(1)}, u32[]{:S(2)}, u32[]{:S(2)}) collective-permute-start(bf16[24,4096]{1,0:T(8,128)(2,1)S(1)} %get-tuple-element.11.refs_0_), channel_id=1, source_target_pairs={{4,0},{8,4},{12,8},{28,12},{24,28},{20,24},{16,20},{0,16},{5,1},{9... | collective-permute-start | bytes 589832 | tf_op jit(solution)/shard_map/ppermute | solution.py:243
  6.4 0.1 collective-permute-start
  6.5 4.8 %collective-permute-done.1.refs_2_ = bf16[24,4096]{1,0:T(8,128)(2,1)S(1)} collective-permute-done((bf16[24,4096]{1,0:T(8,128)(2,1)S(1)}, bf16[24,4096]{1,0:T(8,128)(2,1)S(1)}, u32[]{:S(2)}, u32[]{:S(2)}) %collective-permute-start.1) | collective-permute-done | bytes 196640 | tf_op jit(solution)/shard_map/ppermute | solution.py:243
  11.4 1.7 %collective-permute-start.3 = (bf16[24,4096]{1,0:T(8,128)(2,1)S(1)}, bf16[24,4096]{1,0:T(8,128)(2,1)S(1)}, u32[]{:S(2)}, u32[]{:S(2)}) collective-permute-start(bf16[24,4096]{1,0:T(8,128)(2,1)S(1)} %collective-permute-done.1.refs_2_), channel_id=1, source_target_pairs={{4,0},{8,4},{12,8},{28,12},{24,28},{20,24},{16,20},{0,16},{5,1},{9... | collective-permute-start | bytes 589832 | tf_op jit(solution)/shard_map/ppermute | solution.py:243
  13.0 0.0 collective-permute-done.refs_1_
  13.0 0.3 collective-permute-start.2
  13.4 4.1 %collective-permute-done.3.refs_4_ = bf16[24,4096]{1,0:T(8,128)(2,1)S(1)} collective-permute-done((bf16[24,4096]{1,0:T(8,128)(2,1)S(1)}, bf16[24,4096]{1,0:T(8,128)(2,1)S(1)}, u32[]{:S(2)}, u32[]{:S(2)}) %collective-permute-start.3) | collective-permute-done | bytes 196640 | tf_op jit(solution)/shard_map/ppermute | solution.py:243
  17.4 1.4 %collective-permute-start.4 = (bf16[24,4096]{1,0:T(8,128)(2,1)S(1)}, bf16[24,4096]{1,0:T(8,128)(2,1)S(1)}, u32[]{:S(2)}, u32[]{:S(2)}) collective-permute-start(bf16[24,4096]{1,0:T(8,128)(2,1)S(1)} %collective-permute-done.3.refs_4_), channel_id=1, source_target_pairs={{4,0},{8,4},{12,8},{28,12},{24,28},{20,24},{16,20},{0,16},{5,1},{9... | collective-permute-start | bytes 589832 | tf_op jit(solution)/shard_map/ppermute | solution.py:243
  18.8 0.0 collective-permute-done.2.refs_3_
  18.8 0.7 %collective-permute-start.6 = (bf16[24,4096]{1,0:T(8,128)(2,1)S(1)}, bf16[24,4096]{1,0:T(8,128)(2,1)S(1)}, u32[]{:S(2)}, u32[]{:S(2)}) collective-permute-start(bf16[24,4096]{1,0:T(8,128)(2,1)S(1)} %collective-permute-done.2.refs_3_), channel_id=1, source_target_pairs={{0,4},{4,8},{8,12},{12,28},{28,24},{24,20},{20,16},{16,0},{1,5},{5... | collective-permute-start | bytes 589832 | tf_op jit(solution)/shard_map/ppermute | solution.py:243
  19.5 1.5 %score.3 = (f32[120,256]{1,0:T(8,128)S(1)}, bf16[120,256]{1,0:T(8,128)(2,1)S(1)}) custom-call(bf16[24,4096]{1,0:T(8,128)(2,1)S(1)} %get-tuple-element.11.refs_0_, bf16[24,4096]{1,0:T(8,128)(2,1)S(1)} %collective-permute-done.refs_1_, bf16[24,4096]{1,0:T(8,128)(2,1)S(1)} %collective-permute-done.1.refs_2_, ...), custom_call_target="tpu_custom_call" | custom-call | flops 1073741824 | bytes 1048576 | tf_op jit(solution)/shard_map/score/pallas_call | solution.py:168
  21.0 2.2 %collective-permute-done.4.refs_1_ = bf16[24,4096]{1,0:T(8,128)(2,1)S(1)} collective-permute-done((bf16[24,4096]{1,0:T(8,128)(2,1)S(1)}, bf16[24,4096]{1,0:T(8,128)(2,1)S(1)}, u32[]{:S(2)}, u32[]{:S(2)}) %collective-permute-start.4) | collective-permute-done | bytes 196640 | tf_op jit(solution)/shard_map/ppermute | solution.py:243
  23.2 1.7 %collective-permute-start.8 = (bf16[24,2048]{1,0:T(8,128)(2,1)S(1)}, bf16[24,2048]{1,0:T(8,128)(2,1)S(1)}, u32[]{:S(2)}, u32[]{:S(2)}) collective-permute-start(bf16[24,2048]{1,0:T(8,128)(2,1)S(1)} %slice.7), channel_id=1, source_target_pairs={{4,0},{8,4},{12,8},{28,12},{24,28},{20,24},{16,20},{0,16},{5,1},{9... | collective-permute-start | bytes 294920 | tf_op jit(solution)/shard_map/ppermute | solution.py:252
  24.9 0.0 collective-permute-done.6.refs_0_
  24.9 0.5 %collective-permute-start.7 = (bf16[24,2048]{1,0:T(8,128)(2,1)S(1)}, bf16[24,2048]{1,0:T(8,128)(2,1)S(1)}, u32[]{:S(2)}, u32[]{:S(2)}) collective-permute-start(bf16[24,2048]{1,0:T(8,128)(2,1)S(1)} %slice.8), channel_id=1, source_target_pairs={{0,4},{4,8},{8,12},{12,28},{28,24},{24,20},{20,16},{16,0},{1,5},{5... | collective-permute-start | bytes 294920 | tf_op jit(solution)/shard_map/ppermute | solution.py:252
  25.5 1.7 %collective-permute-start.5 = (bf16[120,256]{1,0:T(8,128)(2,1)S(1)}, bf16[120,256]{1,0:T(8,128)(2,1)S(1)}, u32[]{:S(2)}, u32[]{:S(2)}) collective-permute-start(bf16[120,256]{1,0:T(8,128)(2,1)S(1)} %get-tuple-element.15), channel_id=1, source_target_pairs={{0,2},{2,0},{1,3},{3,1},{4,6},{6,4},{5,7},{7,5},{8,10},{10,8},{9,1... | collective-permute-start | bytes 184328 | tf_op jit(solution)/shard_map/ppermute | solution.py:185
  27.1 0.7 %collective-permute-done.8.refs_3_ = bf16[24,2048]{1,0:T(8,128)(2,1)S(1)} collective-permute-done((bf16[24,2048]{1,0:T(8,128)(2,1)S(1)}, bf16[24,2048]{1,0:T(8,128)(2,1)S(1)}, u32[]{:S(2)}, u32[]{:S(2)}) %collective-permute-start.8) | collective-permute-done | bytes 98336 | tf_op jit(solution)/shard_map/ppermute | solution.py:252
  27.9 1.8 %collective-permute-done.7.refs_2_ = bf16[24,2048]{1,0:T(8,128)(2,1)S(1)} collective-permute-done((bf16[24,2048]{1,0:T(8,128)(2,1)S(1)}, bf16[24,2048]{1,0:T(8,128)(2,1)S(1)}, u32[]{:S(2)}, u32[]{:S(2)}) %collective-permute-start.7) | collective-permute-done | bytes 98336 | tf_op jit(solution)/shard_map/ppermute | solution.py:252
  29.6 0.8 %score.5 = bf16[72,256]{1,0:T(8,128)(2,1)S(1)} custom-call(bf16[24,4096]{1,0:T(8,128)(2,1)S(1)} %collective-permute-done.6.refs_0_, bf16[24,4096]{1,0:T(8,128)(2,1)S(1)} %collective-permute-done.4.refs_1_, bf16[24,2048]{1,0:T(8,128)(2,1)S(1)} %collective-permute-done.7.refs_2_, bf16[24,2048]{1,0:T(8,128)(2,1)S(1)} %collective-permute-done.8.refs_3_, ...), custom_call_target="tpu_custom_call" | custom-call | flops 536870912 | bytes 1048576 | tf_op jit(solution)/shard_map/score/pallas_call | solution.py:168
  30.4 1.6 %collective-permute-start.9 = (bf16[72,256]{1,0:T(8,128)(2,1)S(1)}, bf16[72,256]{1,0:T(8,128)(2,1)S(1)}, u32[]{:S(2)}, u32[]{:S(2)}) collective-permute-start(bf16[72,256]{1,0:T(8,128)(2,1)S(1)} %score.5), channel_id=1, source_target_pairs={{0,2},{2,0},{1,3},{3,1},{4,6},{6,4},{5,7},{7,5},{8,10},{10,8},{9,1... | collective-permute-start | bytes 110600 | tf_op jit(solution)/shard_map/ppermute | solution.py:185
  32.0 0.8 %score.4.refs_2_ = f32[72,256]{1,0:T(8,128)S(1)} custom-call(bf16[24,4096]{1,0:T(8,128)(2,1)S(1)} %collective-permute-done.6.refs_0_, bf16[24,4096]{1,0:T(8,128)(2,1)S(1)} %collective-permute-done.4.refs_1_, bf16[24,2048]{1,0:T(8,128)(2,1)S(1)} %collective-permute-done.7.refs_2_, bf16[24,2048]{1,0:T(8,128)(2,1)S(1)} %collective-permute-done.8.refs_3_, ...), custom_call_target="tpu_custom_call" | custom-call | flops 536870912 | bytes 1048576 | tf_op jit(solution)/shard_map/score/pallas_call | solution.py:168
  32.7 0.0 collective-permute-done.5.refs_1_
  32.7 1.7 %collective-permute-done.9.refs_3_ = bf16[72,256]{1,0:T(8,128)(2,1)S(1)} collective-permute-done((bf16[72,256]{1,0:T(8,128)(2,1)S(1)}, bf16[72,256]{1,0:T(8,128)(2,1)S(1)}, u32[]{:S(2)}, u32[]{:S(2)}) %collective-permute-start.9) | collective-permute-done | bytes 36896 | tf_op jit(solution)/shard_map/ppermute | solution.py:185
  34.4 0.7 %finish.1 = f32[192,256]{1,0:T(8,128)} custom-call(f32[120,256]{1,0:T(8,128)S(1)} %get-tuple-element.13.refs_0_, bf16[120,256]{1,0:T(8,128)(2,1)S(1)} %collective-permute-done.5.refs_1_, f32[72,256]{1,0:T(8,128)S(1)} %score.4.refs_2_, bf16[72,256]{1,0:T(8,128)(2,1)S(1)} %collective-permute-done.9.refs_3_), custom_call_target="tpu_custom_call" | custom-call | tf_op jit(solution)/shard_map/finish/pallas_call | solution.py:218
  (2 shorter events, 0.0 us)
Async XLA Ops:
  3.4 8.0 %collective-permute-start.1 = (bf16[24,4096]{1,0:T(8,128)(2,1)S(1)}, bf16[24,4096]{1,0:T(8,128)(2,1)S(1)}, u32[]{:S(2)}, u32[]{:S(2)}) collective-permute-start(bf16[24,4096]{1,0:T(8,128)(2,1)S(1)} %get-tuple-element.11.refs_0_), channel_id=1, source_target_pairs={{4,0},{8,4},{12,8},{28,12},{24,28},{20,24},{16,20},{0,16},{5,1},{9... | collective-permute-start | bytes 589832 | tf_op jit(solution)/shard_map/ppermute | solution.py:243
  6.4 6.6 %collective-permute-start = (bf16[24,4096]{1,0:T(8,128)(2,1)S(1)}, bf16[24,4096]{1,0:T(8,128)(2,1)S(1)}, u32[]{:S(2)}, u32[]{:S(2)}) collective-permute-start(bf16[24,4096]{1,0:T(8,128)(2,1)S(1)} %get-tuple-element.11.refs_0_), channel_id=1, source_target_pairs={{0,4},{4,8},{8,12},{12,28},{28,24},{24,20},{20,16},{16,0},{1,5},{5... | collective-permute-start | bytes 589832 | tf_op jit(solution)/shard_map/ppermute | solution.py:243
  11.4 6.1 %collective-permute-start.3 = (bf16[24,4096]{1,0:T(8,128)(2,1)S(1)}, bf16[24,4096]{1,0:T(8,128)(2,1)S(1)}, u32[]{:S(2)}, u32[]{:S(2)}) collective-permute-start(bf16[24,4096]{1,0:T(8,128)(2,1)S(1)} %collective-permute-done.1.refs_2_), channel_id=1, source_target_pairs={{4,0},{8,4},{12,8},{28,12},{24,28},{20,24},{16,20},{0,16},{5,1},{9... | collective-permute-start | bytes 589832 | tf_op jit(solution)/shard_map/ppermute | solution.py:243
  13.0 5.8 %collective-permute-start.2 = (bf16[24,4096]{1,0:T(8,128)(2,1)S(1)}, bf16[24,4096]{1,0:T(8,128)(2,1)S(1)}, u32[]{:S(2)}, u32[]{:S(2)}) collective-permute-start(bf16[24,4096]{1,0:T(8,128)(2,1)S(1)} %collective-permute-done.refs_1_), channel_id=1, source_target_pairs={{0,4},{4,8},{8,12},{12,28},{28,24},{24,20},{20,16},{16,0},{1,5},{5... | collective-permute-start | bytes 589832 | tf_op jit(solution)/shard_map/ppermute | solution.py:243
  17.4 5.7 %collective-permute-start.4 = (bf16[24,4096]{1,0:T(8,128)(2,1)S(1)}, bf16[24,4096]{1,0:T(8,128)(2,1)S(1)}, u32[]{:S(2)}, u32[]{:S(2)}) collective-permute-start(bf16[24,4096]{1,0:T(8,128)(2,1)S(1)} %collective-permute-done.3.refs_4_), channel_id=1, source_target_pairs={{4,0},{8,4},{12,8},{28,12},{24,28},{20,24},{16,20},{0,16},{5,1},{9... | collective-permute-start | bytes 589832 | tf_op jit(solution)/shard_map/ppermute | solution.py:243
  18.8 6.1 %collective-permute-start.6 = (bf16[24,4096]{1,0:T(8,128)(2,1)S(1)}, bf16[24,4096]{1,0:T(8,128)(2,1)S(1)}, u32[]{:S(2)}, u32[]{:S(2)}) collective-permute-start(bf16[24,4096]{1,0:T(8,128)(2,1)S(1)} %collective-permute-done.2.refs_3_), channel_id=1, source_target_pairs={{0,4},{4,8},{8,12},{12,28},{28,24},{24,20},{20,16},{16,0},{1,5},{5... | collective-permute-start | bytes 589832 | tf_op jit(solution)/shard_map/ppermute | solution.py:243
  23.2 4.7 %collective-permute-start.8 = (bf16[24,2048]{1,0:T(8,128)(2,1)S(1)}, bf16[24,2048]{1,0:T(8,128)(2,1)S(1)}, u32[]{:S(2)}, u32[]{:S(2)}) collective-permute-start(bf16[24,2048]{1,0:T(8,128)(2,1)S(1)} %slice.7), channel_id=1, source_target_pairs={{4,0},{8,4},{12,8},{28,12},{24,28},{20,24},{16,20},{0,16},{5,1},{9... | collective-permute-start | bytes 294920 | tf_op jit(solution)/shard_map/ppermute | solution.py:252
  24.9 4.7 %collective-permute-start.7 = (bf16[24,2048]{1,0:T(8,128)(2,1)S(1)}, bf16[24,2048]{1,0:T(8,128)(2,1)S(1)}, u32[]{:S(2)}, u32[]{:S(2)}) collective-permute-start(bf16[24,2048]{1,0:T(8,128)(2,1)S(1)} %slice.8), channel_id=1, source_target_pairs={{0,4},{4,8},{8,12},{12,28},{28,24},{24,20},{20,16},{16,0},{1,5},{5... | collective-permute-start | bytes 294920 | tf_op jit(solution)/shard_map/ppermute | solution.py:252
  25.5 7.2 %collective-permute-start.5 = (bf16[120,256]{1,0:T(8,128)(2,1)S(1)}, bf16[120,256]{1,0:T(8,128)(2,1)S(1)}, u32[]{:S(2)}, u32[]{:S(2)}) collective-permute-start(bf16[120,256]{1,0:T(8,128)(2,1)S(1)} %get-tuple-element.15), channel_id=1, source_target_pairs={{0,2},{2,0},{1,3},{3,1},{4,6},{6,4},{5,7},{7,5},{8,10},{10,8},{9,1... | collective-permute-start | bytes 184328 | tf_op jit(solution)/shard_map/ppermute | solution.py:185
  30.4 4.0 %collective-permute-start.9 = (bf16[72,256]{1,0:T(8,128)(2,1)S(1)}, bf16[72,256]{1,0:T(8,128)(2,1)S(1)}, u32[]{:S(2)}, u32[]{:S(2)}) collective-permute-start(bf16[72,256]{1,0:T(8,128)(2,1)S(1)} %score.5), channel_id=1, source_target_pairs={{0,2},{2,0},{1,3},{3,1},{4,6},{6,4},{5,7},{7,5},{8,10},{10,8},{9,1... | collective-permute-start | bytes 110600 | tf_op jit(solution)/shard_map/ppermute | solution.py:185

commit v4 on v2

--- a/solution.py
+++ b/solution.py
@@ -160,42 +160,42 @@
 
 
 def score_kernel(count, height, share, shares, owners, *refs):
-    outs, held = refs[-1 - len(owners):-1], refs[-1]
-    pieces, store_ref = refs[:-2 - len(owners)], refs[-2 - len(owners)]
+    pieces, store_ref, held = refs[:count], refs[count], refs[-1]
+    before, outs = refs[count + 1:-1 - len(owners)], refs[-1 - len(owners):-1]
     half = pieces[0].shape[0]
-    for k, piece in enumerate(pieces[:count]):
+    for k, piece in enumerate(pieces):
         held[k * height:k * height + half, :] = piece[...]
-    for k, piece in enumerate(pieces[count:]):
-        width = piece.shape[1]
-        held[count * height:count * height + half, k * width:(k + 1) * width] = piece[...]
     lay = lax.axis_index("lay")
-    for out, owner in zip(outs, owners):
+    for i, (out, owner) in enumerate(zip(outs, owners)):
         rows = pl.ds(pl.multiple_of(lax.rem(lay + owner, shares) * share, share), share)
         block = lax.dot_general(held[...], store_ref[0, rows, :], NT, preferred_element_type=F32)
-        for j in range(out.shape[0] // half):
-            out[j * half:(j + 1) * half, :] = block[j * height:j * height + half].astype(out.dtype)
-
-
-def score(pieces, parts, store, owners):
-    half = (pieces + parts)[0].shape[0]
-    _, examples, dim = store.shape
+        start = out.shape[0] - count * half
+        if start:
+            out[:start, :] = before[i][...]
+        for j in range(count):
+            out[start + j * half:start + (j + 1) * half, :] = block[j * height:j * height + half].astype(out.dtype)
+
+
+def score(pieces, store, owners, before=()):
+    half, dim = pieces[0].shape
     shares = lax.axis_size("lay")
-    share = examples // shares
-    whole = len(pieces) + (1 if parts else 0)
+    share = store.shape[1] // shares
+    count = len(pieces)
     height = -(-half // 16) * 16
+    rows = count * half + (before[0].shape[0] if before else 0)
     vmem = pl.BlockSpec(memory_space=pltpu.VMEM)
     return pl.pallas_call(
-        functools.partial(score_kernel, len(pieces), height, share, shares, tuple(owners)),
-        out_shape=[jax.ShapeDtypeStruct((whole * half, share), BF16 if owner else F32) for owner in owners],
-        in_specs=[vmem] * (len(pieces) + len(parts) + 1),
+        functools.partial(score_kernel, count, height, share, shares, tuple(owners)),
+        out_shape=[jax.ShapeDtypeStruct((rows, share), BF16 if owner else F32) for owner in owners],
+        in_specs=[vmem] * (count + 1 + len(before)),
         out_specs=[vmem] * len(owners),
-        scratch_shapes=[pltpu.VMEM((whole * height, dim), BF16)],
+        scratch_shapes=[pltpu.VMEM((count * height, dim), BF16)],
         compiler_params=pltpu.CompilerParams(vmem_limit_bytes=24 << 20),
         cost_estimate=pl.CostEstimate(
             flops=2 * 256 * share * len(owners) * dim, bytes_accessed=1 << 20, transcendentals=0
         ),
         name="score",
-    )(*pieces, *parts, store)
+    )(*pieces, store, *before)
 
 
 def swap_layers(sends):
@@ -253,25 +253,29 @@
     back = [(b, a) for a, b in forth]
     own = rotate(query_grads, query_block, layer_slot, out_basis, in_basis, eigen_values, damping)
     store = fetch(own, store_grads)
-    half, dim = own.shape
+    half, _ = own.shape
     others = range(1, lax.axis_size("lay"))
     one = two = own
-    batch, sums, hidden = [own], [], store
+    batch, sums, hidden = [own], [], [store]
     for step in range(1, members):
         one, two = lax.ppermute(one, RING, forth), lax.ppermute(two, RING, back)
-        one, two, hidden = lax.optimization_barrier((one, two, hidden))
+        one, hidden = lax.optimization_barrier((one, hidden))
         if step == 1:
-            store = hidden
-        elif hidden:
-            sums.append((keep, swap_layers(hidden)))
-        hidden = []
+            store, = hidden
+            hidden = []
         batch += [one, two]
-        if len(batch) >= 5 and step < members - 1:
-            keep, *hidden = score(batch, [], store, [0, *others])
+        if len(batch) >= 5 or step == members - 1:
+            if hidden and step < members - 1:
+                keep, *sends = hidden
+                sums.append((keep, swap_layers(sends)))
+                hidden = []
+            hidden = score(batch, store, [0, *others], hidden)
             batch = []
-    parts = [lax.ppermute(one[:, :dim // 2], RING, forth), lax.ppermute(two[:, dim // 2:], RING, back)]
-    got = swap_layers(score(batch, parts, store, others))
-    sums.append((*score(batch, parts, store, [0]), got))
+    keep, *sends = hidden
+    sums.append((keep, swap_layers(sends)))
+    last = [lax.ppermute(one, RING, forth)]
+    got = swap_layers(score(last, store, others))
+    sums.append((*score(last, store, [0]), got))
     return finish(half, sums).T
 
 

time: 36.8 us -> 33.2 us (0.902)
  waiting for transfers between devices: 15.6 us -> 11.1 us
  Pallas kernels: 8.38 us -> 9.63 us
  starting transfers between devices: 12.6 us -> 12.2 us
    ppermute x6, waiting for transfers between devices: 12.6 us -> 8.94 us  [local(): one, two = (lax.ppermute(one, RING, forth), lax.ppermute(two, RING, back))]
    pallas_call x3 -> x4, Pallas kernels: 3.05 us -> 4.3 us  [score(): pl.pallas_call(functools.partial(score_kernel, count, height, share, shar...]
    ppermute x2 -> x1, waiting for transfers between devices: 1.5 us -> 0.93 us  [local(): last = [lax.ppermute(one, RING, forth)]]
    ppermute x2 -> x1, starting transfers between devices: 2.08 us -> 1.79 us  [local(): last = [lax.ppermute(one, RING, forth)]]
  transfers between devices with their start and end apart: 10 -> 9, of which waited for: 9 -> 5; matrix products, arithmetic and copies ran while one was open for 0% -> 0% of each run, Pallas kernels for 14% -> 20%
where the time goes in v4:
time: 33.2 us; the launch traced here: 33 us
  starting transfers between devices  12.2 us (37%)
  waiting for transfers between devices  11.1 us (33%)
  Pallas kernels  9.63 us (29%)
    ppermute x6, waiting for transfers between devices, local(): one, two = (lax.ppermute(one, RING, forth), lax.ppermute(two, RING, back))  8.94 us
    ppermute x6, starting transfers between devices, local(): one, two = (lax.ppermute(one, RING, forth), lax.ppermute(two, RING, back))  7.14 us
    pallas_call x4, Pallas kernels, score(): pl.pallas_call(functools.partial(score_kernel, count, height, share, shar...  4.3 us
    ppermute x2, starting transfers between devices, swap_layers(): lax.ppermute(send, 'lay', [(i, (i + k + 1) % shares) for i in range(share...  3.29 us
    pallas_call x1, Pallas kernels, rotate(): pl.pallas_call(functools.partial(rotate_kernel, half, 1), out_shape=jax.S...  2.41 us
    pallas_call x1, Pallas kernels, fetch(): pl.pallas_call(fetch_kernel, out_shape=jax.ShapeDtypeStruct(store.shape,...  2.2 us
    ppermute x1, starting transfers between devices, local(): last = [lax.ppermute(one, RING, forth)]  1.79 us
    ppermute x2, waiting for transfers between devices, swap_layers(): lax.ppermute(send, 'lay', [(i, (i + k + 1) % shares) for i in range(share...  1.27 us
  transfers between devices with their start and end apart: 9, of which 5 were waited for; matrix products, arithmetic and copies ran while one was open for 0% of the time, Pallas kernels for 20%

profile of v4, /device:TPU:0, one launch (start us, length us, event | category | flops | bytes accessed | tf_op | source)
XLA Modules:
  0.0 33.0 jit_solution(14204211012556984570)
XLA Ops:
  0.0 2.4 %rotate.1.after_ref.refs_0_ = bf16[24,4096]{1,0:T(8,128)(2,1)S(1)} custom-call(bf16[1,48,4096]{2,1,0:T(8,128)(2,1)} %query_hbm.1, s32[384]{0:T(512)} %block_hbm.1, f32[4]{0:T(128)} %damping_hbm.1, s32[2]{0:T(128)} %slot_hbm.1, bf16[2,64,64]{2,1,0:T(8,128)(2,1)} %out_hbm.1, bf16[2,64,64]{2,1,0:T(8,128)(2,1)} %in_hbm.1, f32[2,64,64]{2,1,0:T(8,128)} %eigen_hbm.1), custom_call_target="tpu_custom_call" | custom-call | flops 201326592 | bytes 1048576 | tf_op jit(solution)/shard_map/rotate/pallas_call | solution.py:116
  2.4 3.1 %collective-permute-start = (bf16[24,4096]{1,0:T(8,128)(2,1)S(1)}, bf16[24,4096]{1,0:T(8,128)(2,1)S(1)}, u32[]{:S(2)}, u32[]{:S(2)}) collective-permute-start(bf16[24,4096]{1,0:T(8,128)(2,1)S(1)} %rotate.1.after_ref.refs_0_), channel_id=1, source_target_pairs={{0,4},{4,8},{8,12},{12,28},{28,24},{24,20},{20,16},{16,0},{1,5},{5... | collective-permute-start | bytes 589832 | tf_op jit(solution)/shard_map/ppermute | solution.py:261
  5.5 0.0 collective-permute-start.3
  5.5 2.2 %fetch.1.refs_5_.refs_2_.refs_1_ = bf16[1,512,4096]{2,1,0:T(8,128)(2,1)S(1)} custom-call(bf16[24,4096]{1,0:T(8,128)(2,1)S(1)} %rotate.1.after_ref.refs_0_, bf16[1,512,4096]{2,1,0:T(8,128)(2,1)} %store_hbm.1), custom_call_target="tpu_custom_call" | custom-call | bytes 8388608 | tf_op jit(solution)/shard_map/fetch/pallas_call | solution.py:150
  7.7 2.6 %collective-permute-done.refs_1_ = bf16[24,4096]{1,0:T(8,128)(2,1)S(1)} collective-permute-done((bf16[24,4096]{1,0:T(8,128)(2,1)S(1)}, bf16[24,4096]{1,0:T(8,128)(2,1)S(1)}, u32[]{:S(2)}, u32[]{:S(2)}) %collective-permute-start) | collective-permute-done | bytes 196640 | tf_op jit(solution)/shard_map/ppermute | solution.py:261
  10.3 1.8 %collective-permute-start.1 = (bf16[24,4096]{1,0:T(8,128)(2,1)S(1)}, bf16[24,4096]{1,0:T(8,128)(2,1)S(1)}, u32[]{:S(2)}, u32[]{:S(2)}) collective-permute-start(bf16[24,4096]{1,0:T(8,128)(2,1)S(1)} %collective-permute-done.refs_1_), channel_id=1, source_target_pairs={{0,4},{4,8},{8,12},{12,28},{28,24},{24,20},{20,16},{16,0},{1,5},{5... | collective-permute-start | bytes 589832 | tf_op jit(solution)/shard_map/ppermute | solution.py:261
  12.1 0.0 collective-permute-done.3.refs_2_
  12.1 0.2 collective-permute-start.4
  12.4 4.1 %collective-permute-done.1.refs_3_ = bf16[24,4096]{1,0:T(8,128)(2,1)S(1)} collective-permute-done((bf16[24,4096]{1,0:T(8,128)(2,1)S(1)}, bf16[24,4096]{1,0:T(8,128)(2,1)S(1)}, u32[]{:S(2)}, u32[]{:S(2)}) %collective-permute-start.1) | collective-permute-done | bytes 196640 | tf_op jit(solution)/shard_map/ppermute | solution.py:261
  16.4 1.5 %collective-permute-start.2 = (bf16[24,4096]{1,0:T(8,128)(2,1)S(1)}, bf16[24,4096]{1,0:T(8,128)(2,1)S(1)}, u32[]{:S(2)}, u32[]{:S(2)}) collective-permute-start(bf16[24,4096]{1,0:T(8,128)(2,1)S(1)} %collective-permute-done.1.refs_3_), channel_id=1, source_target_pairs={{0,4},{4,8},{8,12},{12,28},{28,24},{24,20},{20,16},{16,0},{1,5},{5... | collective-permute-start | bytes 589832 | tf_op jit(solution)/shard_map/ppermute | solution.py:261
  17.9 0.0 collective-permute-done.4.refs_4_
  17.9 0.6 %collective-permute-start.5 = (bf16[24,4096]{1,0:T(8,128)(2,1)S(1)}, bf16[24,4096]{1,0:T(8,128)(2,1)S(1)}, u32[]{:S(2)}, u32[]{:S(2)}) collective-permute-start(bf16[24,4096]{1,0:T(8,128)(2,1)S(1)} %collective-permute-done.4.refs_4_), channel_id=1, source_target_pairs={{4,0},{8,4},{12,8},{28,12},{24,28},{20,24},{16,20},{0,16},{5,1},{9... | collective-permute-start | bytes 589832 | tf_op jit(solution)/shard_map/ppermute | solution.py:261
  18.5 1.5 %score.4 = (f32[120,256]{1,0:T(8,128)S(1)}, bf16[120,256]{1,0:T(8,128)(2,1)S(1)}) custom-call(bf16[24,4096]{1,0:T(8,128)(2,1)S(1)} %rotate.1.after_ref.refs_0_, bf16[24,4096]{1,0:T(8,128)(2,1)S(1)} %collective-permute-done.refs_1_, bf16[24,4096]{1,0:T(8,128)(2,1)S(1)} %collective-permute-done.3.refs_2_, bf16[24,4096]{1,0:T(8,128)(2,1)S(1)} %collective-permute-done.1.refs_3_, ...), custom_call_target="tpu_custom_call" | custom-call | flops 1073741824 | bytes 1048576 | tf_op jit(solution)/shard_map/score/pallas_call | solution.py:187
  20.0 2.3 %collective-permute-done.2.refs_0_ = bf16[24,4096]{1,0:T(8,128)(2,1)S(1)} collective-permute-done((bf16[24,4096]{1,0:T(8,128)(2,1)S(1)}, bf16[24,4096]{1,0:T(8,128)(2,1)S(1)}, u32[]{:S(2)}, u32[]{:S(2)}) %collective-permute-start.2) | collective-permute-done | bytes 196640 | tf_op jit(solution)/shard_map/ppermute | solution.py:261
  22.2 1.8 %collective-permute-start.7 = (bf16[24,4096]{1,0:T(8,128)(2,1)S(1)}, bf16[24,4096]{1,0:T(8,128)(2,1)S(1)}, u32[]{:S(2)}, u32[]{:S(2)}) collective-permute-start(bf16[24,4096]{1,0:T(8,128)(2,1)S(1)} %collective-permute-done.2.refs_0_), channel_id=1, source_target_pairs={{0,4},{4,8},{8,12},{12,28},{28,24},{24,20},{20,16},{16,0},{1,5},{5... | collective-permute-start | bytes 589832 | tf_op jit(solution)/shard_map/ppermute | solution.py:276
  24.0 0.0 collective-permute-done.5.refs_1_
  24.0 1.4 %score.5 = (f32[168,256]{1,0:T(8,128)S(1)}, bf16[168,256]{1,0:T(8,128)(2,1)S(1)}) custom-call(bf16[24,4096]{1,0:T(8,128)(2,1)S(1)} %collective-permute-done.2.refs_0_, bf16[24,4096]{1,0:T(8,128)(2,1)S(1)} %collective-permute-done.5.refs_1_, bf16[1,512,4096]{2,1,0:T(8,128)(2,1)S(1)} %fetch.1.refs_5_.refs_2_.refs_1_, ...), custom_call_target="tpu_custom_call" | custom-call | flops 1073741824 | bytes 1048576 | tf_op jit(solution)/shard_map/score/pallas_call | solution.py:187
  25.4 1.6 %collective-permute-start.6 = (bf16[168,256]{1,0:T(8,128)(2,1)S(1)}, bf16[168,256]{1,0:T(8,128)(2,1)S(1)}, u32[]{:S(2)}, u32[]{:S(2)}) collective-permute-start(bf16[168,256]{1,0:T(8,128)(2,1)S(1)} %get-tuple-element.22), channel_id=1, source_target_pairs={{0,2},{2,0},{1,3},{3,1},{4,6},{6,4},{5,7},{7,5},{8,10},{10,8},{9,1... | collective-permute-start | bytes 258056 | tf_op jit(solution)/shard_map/ppermute | solution.py:204
  27.0 0.9 %collective-permute-done.7.refs_0_ = bf16[24,4096]{1,0:T(8,128)(2,1)S(1)} collective-permute-done((bf16[24,4096]{1,0:T(8,128)(2,1)S(1)}, bf16[24,4096]{1,0:T(8,128)(2,1)S(1)}, u32[]{:S(2)}, u32[]{:S(2)}) %collective-permute-start.7) | collective-permute-done | bytes 196640 | tf_op jit(solution)/shard_map/ppermute | solution.py:276
  27.9 0.7 %score.7 = bf16[24,256]{1,0:T(8,128)(2,1)S(1)} custom-call(bf16[24,4096]{1,0:T(8,128)(2,1)S(1)} %collective-permute-done.7.refs_0_, bf16[1,512,4096]{2,1,0:T(8,128)(2,1)S(1)} %fetch.1.refs_5_.refs_2_.refs_1_), custom_call_target="tpu_custom_call" | custom-call | flops 536870912 | bytes 1048576 | tf_op jit(solution)/shard_map/score/pallas_call | solution.py:187
  28.6 1.7 %collective-permute-start.8 = (bf16[24,256]{1,0:T(8,128)(2,1)S(1)}, bf16[24,256]{1,0:T(8,128)(2,1)S(1)}, u32[]{:S(2)}, u32[]{:S(2)}) collective-permute-start(bf16[24,256]{1,0:T(8,128)(2,1)S(1)} %score.7), channel_id=1, source_target_pairs={{0,2},{2,0},{1,3},{3,1},{4,6},{6,4},{5,7},{7,5},{8,10},{10,8},{9,1... | collective-permute-start | bytes 36872 | tf_op jit(solution)/shard_map/ppermute | solution.py:204
  30.3 0.7 %score.6.refs_2_ = f32[24,256]{1,0:T(8,128)S(1)} custom-call(bf16[24,4096]{1,0:T(8,128)(2,1)S(1)} %collective-permute-done.7.refs_0_, bf16[1,512,4096]{2,1,0:T(8,128)(2,1)S(1)} %fetch.1.refs_5_.refs_2_.refs_1_), custom_call_target="tpu_custom_call" | custom-call | flops 536870912 | bytes 1048576 | tf_op jit(solution)/shard_map/score/pallas_call | solution.py:187
  31.1 0.0 collective-permute-done.6.refs_1_
  31.1 1.3 %collective-permute-done.8.refs_3_ = bf16[24,256]{1,0:T(8,128)(2,1)S(1)} collective-permute-done((bf16[24,256]{1,0:T(8,128)(2,1)S(1)}, bf16[24,256]{1,0:T(8,128)(2,1)S(1)}, u32[]{:S(2)}, u32[]{:S(2)}) %collective-permute-start.8) | collective-permute-done | bytes 12320 | tf_op jit(solution)/shard_map/ppermute | solution.py:204
  32.3 0.7 %finish.1 = f32[192,256]{1,0:T(8,128)} custom-call(f32[168,256]{1,0:T(8,128)S(1)} %get-tuple-element.21.refs_0_, bf16[168,256]{1,0:T(8,128)(2,1)S(1)} %collective-permute-done.6.refs_1_, f32[24,256]{1,0:T(8,128)S(1)} %score.6.refs_2_, bf16[24,256]{1,0:T(8,128)(2,1)S(1)} %collective-permute-done.8.refs_3_), custom_call_target="tpu_custom_call" | custom-call | tf_op jit(solution)/shard_map/finish/pallas_call | solution.py:237
Async XLA Ops:
  2.4 7.9 %collective-permute-start = (bf16[24,4096]{1,0:T(8,128)(2,1)S(1)}, bf16[24,4096]{1,0:T(8,128)(2,1)S(1)}, u32[]{:S(2)}, u32[]{:S(2)}) collective-permute-start(bf16[24,4096]{1,0:T(8,128)(2,1)S(1)} %rotate.1.after_ref.refs_0_), channel_id=1, source_target_pairs={{0,4},{4,8},{8,12},{12,28},{28,24},{24,20},{20,16},{16,0},{1,5},{5... | collective-permute-start | bytes 589832 | tf_op jit(solution)/shard_map/ppermute | solution.py:261
  5.5 6.6 %collective-permute-start.3 = (bf16[24,4096]{1,0:T(8,128)(2,1)S(1)}, bf16[24,4096]{1,0:T(8,128)(2,1)S(1)}, u32[]{:S(2)}, u32[]{:S(2)}) collective-permute-start(bf16[24,4096]{1,0:T(8,128)(2,1)S(1)} %rotate.1.after_ref.refs_0_), channel_id=1, source_target_pairs={{4,0},{8,4},{12,8},{28,12},{24,28},{20,24},{16,20},{0,16},{5,1},{9... | collective-permute-start | bytes 589832 | tf_op jit(solution)/shard_map/ppermute | solution.py:261
  10.3 6.1 %collective-permute-start.1 = (bf16[24,4096]{1,0:T(8,128)(2,1)S(1)}, bf16[24,4096]{1,0:T(8,128)(2,1)S(1)}, u32[]{:S(2)}, u32[]{:S(2)}) collective-permute-start(bf16[24,4096]{1,0:T(8,128)(2,1)S(1)} %collective-permute-done.refs_1_), channel_id=1, source_target_pairs={{0,4},{4,8},{8,12},{12,28},{28,24},{24,20},{20,16},{16,0},{1,5},{5... | collective-permute-start | bytes 589832 | tf_op jit(solution)/shard_map/ppermute | solution.py:261
  12.1 5.8 %collective-permute-start.4 = (bf16[24,4096]{1,0:T(8,128)(2,1)S(1)}, bf16[24,4096]{1,0:T(8,128)(2,1)S(1)}, u32[]{:S(2)}, u32[]{:S(2)}) collective-permute-start(bf16[24,4096]{1,0:T(8,128)(2,1)S(1)} %collective-permute-done.3.refs_2_), channel_id=1, source_target_pairs={{4,0},{8,4},{12,8},{28,12},{24,28},{20,24},{16,20},{0,16},{5,1},{9... | collective-permute-start | bytes 589832 | tf_op jit(solution)/shard_map/ppermute | solution.py:261
  16.4 5.8 %collective-permute-start.2 = (bf16[24,4096]{1,0:T(8,128)(2,1)S(1)}, bf16[24,4096]{1,0:T(8,128)(2,1)S(1)}, u32[]{:S(2)}, u32[]{:S(2)}) collective-permute-start(bf16[24,4096]{1,0:T(8,128)(2,1)S(1)} %collective-permute-done.1.refs_3_), channel_id=1, source_target_pairs={{0,4},{4,8},{8,12},{12,28},{28,24},{24,20},{20,16},{16,0},{1,5},{5... | collective-permute-start | bytes 589832 | tf_op jit(solution)/shard_map/ppermute | solution.py:261
  17.9 6.1 %collective-permute-start.5 = (bf16[24,4096]{1,0:T(8,128)(2,1)S(1)}, bf16[24,4096]{1,0:T(8,128)(2,1)S(1)}, u32[]{:S(2)}, u32[]{:S(2)}) collective-permute-start(bf16[24,4096]{1,0:T(8,128)(2,1)S(1)} %collective-permute-done.4.refs_4_), channel_id=1, source_target_pairs={{4,0},{8,4},{12,8},{28,12},{24,28},{20,24},{16,20},{0,16},{5,1},{9... | collective-permute-start | bytes 589832 | tf_op jit(solution)/shard_map/ppermute | solution.py:261
  22.2 5.7 %collective-permute-start.7 = (bf16[24,4096]{1,0:T(8,128)(2,1)S(1)}, bf16[24,4096]{1,0:T(8,128)(2,1)S(1)}, u32[]{:S(2)}, u32[]{:S(2)}) collective-permute-start(bf16[24,4096]{1,0:T(8,128)(2,1)S(1)} %collective-permute-done.2.refs_0_), channel_id=1, source_target_pairs={{0,4},{4,8},{8,12},{12,28},{28,24},{24,20},{20,16},{16,0},{1,5},{5... | collective-permute-start | bytes 589832 | tf_op jit(solution)/shard_map/ppermute | solution.py:276
  25.4 5.7 %collective-permute-start.6 = (bf16[168,256]{1,0:T(8,128)(2,1)S(1)}, bf16[168,256]{1,0:T(8,128)(2,1)S(1)}, u32[]{:S(2)}, u32[]{:S(2)}) collective-permute-start(bf16[168,256]{1,0:T(8,128)(2,1)S(1)} %get-tuple-element.22), channel_id=1, source_target_pairs={{0,2},{2,0},{1,3},{3,1},{4,6},{6,4},{5,7},{7,5},{8,10},{10,8},{9,1... | collective-permute-start | bytes 258056 | tf_op jit(solution)/shard_map/ppermute | solution.py:204
  28.6 3.7 %collective-permute-start.8 = (bf16[24,256]{1,0:T(8,128)(2,1)S(1)}, bf16[24,256]{1,0:T(8,128)(2,1)S(1)}, u32[]{:S(2)}, u32[]{:S(2)}) collective-permute-start(bf16[24,256]{1,0:T(8,128)(2,1)S(1)} %score.7), channel_id=1, source_target_pairs={{0,2},{2,0},{1,3},{3,1},{4,6},{6,4},{5,7},{7,5},{8,10},{10,8},{9,1... | collective-permute-start | bytes 36872 | tf_op jit(solution)/shard_map/ppermute | solution.py:204

commit v5 on v2

--- a/solution.py
+++ b/solution.py
@@ -80,10 +80,15 @@
             bottoms.append(jnp.where(low_lanes, pltpu.roll(a, RANK, 1), b))
         grids += [jnp.concatenate(tops, axis=1), jnp.concatenate(bottoms, axis=1)]
     right = jnp.dot(jnp.concatenate(grids, axis=0).astype(BF16), in_diag, preferred_element_type=F32)
-    turned = []
+    middles = [
+        jnp.dot(
+            out_t_twice, jnp.concatenate(split(right[quad * RANK:(quad + 1) * RANK]), axis=0),
+            preferred_element_type=F32,
+        )
+        for quad in quads
+    ]
+    scaled = []
     for quad in quads:
-        part = right[quad * RANK:(quad + 1) * RANK]
-        middle = jnp.dot(out_t_twice, jnp.concatenate(split(part), axis=0), preferred_element_type=F32)
         damp = jnp.zeros((1, 4 * RANK), F32)
         for one in range(4):
             block = block_ref[first + quad * 4 + one]
@@ -91,8 +96,10 @@
             for k in range(BLOCKS):
                 value = jnp.where(block == k, damping_ref[k], value)
             damp = jnp.where(lane == one, value, damp)
-        scaled = middle / (eigen + damp)
-        turned.append(jnp.dot(out_twice, jnp.concatenate(split(scaled), axis=0), preferred_element_type=F32))
+        scaled.append(middles[quad] / (eigen + damp))
+    turned = [
+        jnp.dot(out_twice, jnp.concatenate(split(block), axis=0), preferred_element_type=F32) for block in scaled
+    ]
     hi, lo = split(jnp.concatenate(turned, axis=0))
     result = lax.dot_general(hi, in_diag, NT, preferred_element_type=F32)
     result = result + lax.dot_general(lo, in_diag, NT, preferred_element_type=F32)
@@ -165,9 +172,10 @@
     half = pieces[0].shape[0]
     for k, piece in enumerate(pieces[:count]):
         held[k * height:k * height + half, :] = piece[...]
-    for k, piece in enumerate(pieces[count:]):
-        width = piece.shape[1]
-        held[count * height:count * height + half, k * width:(k + 1) * width] = piece[...]
+    column = 0
+    for piece in pieces[count:]:
+        held[count * height:count * height + half, column:column + piece.shape[1]] = piece[...]
+        column += piece.shape[1]
     lay = lax.axis_index("lay")
     for out, owner in zip(outs, owners):
         rows = pl.ds(pl.multiple_of(lax.rem(lay + owner, shares) * share, share), share)
@@ -249,27 +257,34 @@
 ):
     members = lax.axis_size("ex")
     ring = list(range(members)) + [members + i for i in reversed(range(members))]
-    forth = [(a, ring[(i + 1) % len(ring)]) for i, a in enumerate(ring)]
-    back = [(b, a) for a, b in forth]
+    def hop(piece, steps):
+        return lax.ppermute(piece, RING, [(a, ring[(i + steps) % len(ring)]) for i, a in enumerate(ring)])
+
     own = rotate(query_grads, query_block, layer_slot, out_basis, in_basis, eigen_values, damping)
     store = fetch(own, store_grads)
     half, dim = own.shape
     others = range(1, lax.axis_size("lay"))
     one = two = own
-    batch, sums, hidden = [own], [], store
+    batch, sums, hidden = [own], [], [store]
     for step in range(1, members):
-        one, two = lax.ppermute(one, RING, forth), lax.ppermute(two, RING, back)
-        one, two, hidden = lax.optimization_barrier((one, two, hidden))
+        if step == members - 1:
+            cut = dim // 8 * 5 // 128 * 128
+            parts = [one[:, :cut], two[:, cut:]]
+        one, two = hop(one, 1), hop(two, -1)
+        if step == members - 1:
+            parts = [hop(parts[0], 2), hop(parts[1], -2)]
+        if step < members - 1:
+            one, hidden = lax.optimization_barrier((one, hidden))
         if step == 1:
-            store = hidden
+            store, = hidden
         elif hidden:
-            sums.append((keep, swap_layers(hidden)))
+            keep, *sends = hidden
+            sums.append((keep, swap_layers(sends)))
         hidden = []
         batch += [one, two]
         if len(batch) >= 5 and step < members - 1:
-            keep, *hidden = score(batch, [], store, [0, *others])
+            hidden = score(batch, [], store, [0, *others])
             batch = []
-    parts = [lax.ppermute(one[:, :dim // 2], RING, forth), lax.ppermute(two[:, dim // 2:], RING, back)]
     got = swap_layers(score(batch, parts, store, others))
     sums.append((*score(batch, parts, store, [0]), got))
     return finish(half, sums).T

time: 36.8 us -> 31.9 us (0.87)
  waiting for transfers between devices: 15.6 us -> 10.6 us
  starting transfers between devices: 12.6 us -> 13.1 us
  Pallas kernels: 8.38 us -> 7.98 us
    ppermute x8, waiting for transfers between devices: 14.1 us -> 8.92 us  [hop(): lax.ppermute(piece, RING, [(a, ring[(i + steps) % len(ring)]) for i, a in...]
    ppermute x8, starting transfers between devices: 9.27 us -> 10.1 us  [hop(): lax.ppermute(piece, RING, [(a, ring[(i + steps) % len(ring)]) for i, a in...]
    pallas_call x1, Pallas kernels: 2.41 us -> 2 us  [rotate(): pl.pallas_call(functools.partial(rotate_kernel, half, 1), out_shape=jax.S...]
  transfers between devices with their start and end apart: 10 -> 10, of which waited for: 9 -> 5; matrix products, arithmetic and copies ran while one was open for 0% -> 0% of each run, Pallas kernels for 14% -> 17%
where the time goes in v5:
time: 31.9 us; the launch traced here: 31.8 us
  starting transfers between devices  13.1 us (41%)
  waiting for transfers between devices  10.6 us (33%)
  Pallas kernels  7.98 us (25%)
    ppermute x8, starting transfers between devices, hop(): lax.ppermute(piece, RING, [(a, ring[(i + steps) % len(ring)]) for i, a in...  10.1 us
    ppermute x8, waiting for transfers between devices, hop(): lax.ppermute(piece, RING, [(a, ring[(i + steps) % len(ring)]) for i, a in...  8.92 us
    pallas_call x3, Pallas kernels, score(): pl.pallas_call(functools.partial(score_kernel, len(pieces), height, share...  3.06 us
    ppermute x2, starting transfers between devices, swap_layers(): lax.ppermute(send, 'lay', [(i, (i + k + 1) % shares) for i in range(share...  3.03 us
    pallas_call x1, Pallas kernels, fetch(): pl.pallas_call(fetch_kernel, out_shape=jax.ShapeDtypeStruct(store.shape,...  2.2 us
    pallas_call x1, Pallas kernels, rotate(): pl.pallas_call(functools.partial(rotate_kernel, half, 1), out_shape=jax.S...  2 us
    ppermute x2, waiting for transfers between devices, swap_layers(): lax.ppermute(send, 'lay', [(i, (i + k + 1) % shares) for i in range(share...  1.67 us
    pallas_call x1, Pallas kernels, finish(): pl.pallas_call(functools.partial(finish_kernel, half, members, sizes), ou...  0.71 us
  transfers between devices with their start and end apart: 10, of which 5 were waited for; matrix products, arithmetic and copies ran while one was open for 0% of the time, Pallas kernels for 17%

profile of v5, /device:TPU:0, one launch (start us, length us, event | category | flops | bytes accessed | tf_op | source)
XLA Modules:
  0.0 31.8 jit_solution(11655025142432437689)
XLA Ops:
  0.0 2.0 %rotate.1.after_ref.refs_0_ = bf16[24,4096]{1,0:T(8,128)(2,1)S(1)} custom-call(bf16[1,48,4096]{2,1,0:T(8,128)(2,1)} %query_hbm.1, s32[384]{0:T(512)} %block_hbm.1, f32[4]{0:T(128)} %damping_hbm.1, s32[2]{0:T(128)} %slot_hbm.1, bf16[2,64,64]{2,1,0:T(8,128)(2,1)} %out_hbm.1, bf16[2,64,64]{2,1,0:T(8,128)(2,1)} %in_hbm.1, f32[2,64,64]{2,1,0:T(8,128)} %eigen_hbm.1), custom_call_target="tpu_custom_call" | custom-call | flops 201326592 | bytes 1048576 | tf_op jit(solution)/shard_map/rotate/pallas_call | solution.py:123
  2.0 3.1 %collective-permute-start = (bf16[24,4096]{1,0:T(8,128)(2,1)S(1)}, bf16[24,4096]{1,0:T(8,128)(2,1)S(1)}, u32[]{:S(2)}, u32[]{:S(2)}) collective-permute-start(bf16[24,4096]{1,0:T(8,128)(2,1)S(1)} %rotate.1.after_ref.refs_0_), channel_id=1, source_target_pairs={{0,4},{4,8},{8,12},{12,28},{28,24},{24,20},{20,16},{16,0},{1,5},{5... | collective-permute-start | bytes 589832 | tf_op jit(solution)/shard_map/ppermute | solution.py:261
  5.1 0.0 collective-permute-start.1
  5.1 2.2 %fetch.1.refs_5_.refs_4_ = bf16[1,512,4096]{2,1,0:T(8,128)(2,1)S(1)} custom-call(bf16[24,4096]{1,0:T(8,128)(2,1)S(1)} %rotate.1.after_ref.refs_0_, bf16[1,512,4096]{2,1,0:T(8,128)(2,1)} %store_hbm.1), custom_call_target="tpu_custom_call" | custom-call | bytes 8388608 | tf_op jit(solution)/shard_map/fetch/pallas_call | solution.py:157
  7.3 2.6 %collective-permute-done.refs_1_ = bf16[24,4096]{1,0:T(8,128)(2,1)S(1)} collective-permute-done((bf16[24,4096]{1,0:T(8,128)(2,1)S(1)}, bf16[24,4096]{1,0:T(8,128)(2,1)S(1)}, u32[]{:S(2)}, u32[]{:S(2)}) %collective-permute-start) | collective-permute-done | bytes 196640 | tf_op jit(solution)/shard_map/ppermute | solution.py:261
  9.9 1.8 %collective-permute-start.2 = (bf16[24,4096]{1,0:T(8,128)(2,1)S(1)}, bf16[24,4096]{1,0:T(8,128)(2,1)S(1)}, u32[]{:S(2)}, u32[]{:S(2)}) collective-permute-start(bf16[24,4096]{1,0:T(8,128)(2,1)S(1)} %collective-permute-done.refs_1_), channel_id=1, source_target_pairs={{0,4},{4,8},{8,12},{12,28},{28,24},{24,20},{20,16},{16,0},{1,5},{5... | collective-permute-start | bytes 589832 | tf_op jit(solution)/shard_map/ppermute | solution.py:261
  11.7 0.0 collective-permute-done.1.refs_2_
  11.7 0.2 collective-permute-start.3
  12.0 4.1 %collective-permute-done.2.refs_3_ = bf16[24,4096]{1,0:T(8,128)(2,1)S(1)} collective-permute-done((bf16[24,4096]{1,0:T(8,128)(2,1)S(1)}, bf16[24,4096]{1,0:T(8,128)(2,1)S(1)}, u32[]{:S(2)}, u32[]{:S(2)}) %collective-permute-start.2) | collective-permute-done | bytes 196640 | tf_op jit(solution)/shard_map/ppermute | solution.py:261
  16.0 1.5 %collective-permute-start.5 = (bf16[24,4096]{1,0:T(8,128)(2,1)S(1)}, bf16[24,4096]{1,0:T(8,128)(2,1)S(1)}, u32[]{:S(2)}, u32[]{:S(2)}) collective-permute-start(bf16[24,4096]{1,0:T(8,128)(2,1)S(1)} %collective-permute-done.2.refs_3_), channel_id=1, source_target_pairs={{0,4},{4,8},{8,12},{12,28},{28,24},{24,20},{20,16},{16,0},{1,5},{5... | collective-permute-start | bytes 589832 | tf_op jit(solution)/shard_map/ppermute | solution.py:261
  17.5 0.0 collective-permute-done.3.refs_4_
  17.5 0.6 %collective-permute-start.6 = (bf16[24,4096]{1,0:T(8,128)(2,1)S(1)}, bf16[24,4096]{1,0:T(8,128)(2,1)S(1)}, u32[]{:S(2)}, u32[]{:S(2)}) collective-permute-start(bf16[24,4096]{1,0:T(8,128)(2,1)S(1)} %collective-permute-done.3.refs_4_), channel_id=1, source_target_pairs={{0,16},{4,0},{8,4},{12,8},{28,12},{24,28},{20,24},{16,20},{1,17},{... | collective-permute-start | bytes 589832 | tf_op jit(solution)/shard_map/ppermute | solution.py:261
  18.1 2.5 %collective-permute-start.7 = (bf16[24,2560]{1,0:T(8,128)(2,1)S(1)}, bf16[24,2560]{1,0:T(8,128)(2,1)S(1)}, u32[]{:S(2)}, u32[]{:S(2)}) collective-permute-start(bf16[24,2560]{1,0:T(8,128)(2,1)S(1)} %slice.8), channel_id=1, source_target_pairs={{0,8},{4,12},{8,28},{12,24},{28,20},{24,16},{20,0},{16,4},{1,9},{5... | collective-permute-start | bytes 368648 | tf_op jit(solution)/shard_map/ppermute | solution.py:261
  20.6 0.4 %collective-permute-start.8 = (bf16[24,1536]{1,0:T(8,128)(2,1)S(1)}, bf16[24,1536]{1,0:T(8,128)(2,1)S(1)}, u32[]{:S(2)}, u32[]{:S(2)}) collective-permute-start(bf16[24,1536]{1,0:T(8,128)(2,1)S(1)} %slice.9), channel_id=1, source_target_pairs={{0,20},{4,16},{8,0},{12,4},{28,8},{24,12},{20,28},{16,24},{1,21},{... | collective-permute-start | bytes 221192 | tf_op jit(solution)/shard_map/ppermute | solution.py:261
  21.1 1.5 %score.3 = (f32[120,256]{1,0:T(8,128)S(1)}, bf16[120,256]{1,0:T(8,128)(2,1)S(1)}) custom-call(bf16[24,4096]{1,0:T(8,128)(2,1)S(1)} %rotate.1.after_ref.refs_0_, bf16[24,4096]{1,0:T(8,128)(2,1)S(1)} %collective-permute-done.refs_1_, bf16[24,4096]{1,0:T(8,128)(2,1)S(1)} %collective-permute-done.1.refs_2_, bf16[24,4096]{1,0:T(8,128)(2,1)S(1)} %collective-permute-done.2.refs_3_, ...), custom_call_target="tpu_custom_call" | custom-call | flops 1073741824 | bytes 1048576 | tf_op jit(solution)/shard_map/score/pallas_call | solution.py:195
  22.6 1.5 %collective-permute-start.4 = (bf16[120,256]{1,0:T(8,128)(2,1)S(1)}, bf16[120,256]{1,0:T(8,128)(2,1)S(1)}, u32[]{:S(2)}, u32[]{:S(2)}) collective-permute-start(bf16[120,256]{1,0:T(8,128)(2,1)S(1)} %get-tuple-element.12), channel_id=1, source_target_pairs={{0,2},{2,0},{1,3},{3,1},{4,6},{6,4},{5,7},{7,5},{8,10},{10,8},{9,1... | collective-permute-start | bytes 184328 | tf_op jit(solution)/shard_map/ppermute | solution.py:212
  24.0 1.8 %collective-permute-done.8.refs_3_ = bf16[24,1536]{1,0:T(8,128)(2,1)S(1)} collective-permute-done((bf16[24,1536]{1,0:T(8,128)(2,1)S(1)}, bf16[24,1536]{1,0:T(8,128)(2,1)S(1)}, u32[]{:S(2)}, u32[]{:S(2)}) %collective-permute-start.8) | collective-permute-done | bytes 73760 | tf_op jit(solution)/shard_map/ppermute | solution.py:261
  25.9 0.4 %collective-permute-done.7.refs_2_ = bf16[24,2560]{1,0:T(8,128)(2,1)S(1)} collective-permute-done((bf16[24,2560]{1,0:T(8,128)(2,1)S(1)}, bf16[24,2560]{1,0:T(8,128)(2,1)S(1)}, u32[]{:S(2)}, u32[]{:S(2)}) %collective-permute-start.7) | collective-permute-done | bytes 122912 | tf_op jit(solution)/shard_map/ppermute | solution.py:261
  26.3 0.0 collective-permute-done.5.refs_0_
  26.3 0.0 collective-permute-done.6.refs_1_
  26.3 0.8 %score.5 = bf16[72,256]{1,0:T(8,128)(2,1)S(1)} custom-call(bf16[24,4096]{1,0:T(8,128)(2,1)S(1)} %collective-permute-done.5.refs_0_, bf16[24,4096]{1,0:T(8,128)(2,1)S(1)} %collective-permute-done.6.refs_1_, bf16[24,2560]{1,0:T(8,128)(2,1)S(1)} %collective-permute-done.7.refs_2_, bf16[24,1536]{1,0:T(8,128)(2,1)S(1)} %collective-permute-done.8.refs_3_, ...), custom_call_target="tpu_custom_call" | custom-call | flops 536870912 | bytes 1048576 | tf_op jit(solution)/shard_map/score/pallas_call | solution.py:195
  27.0 1.6 %collective-permute-start.9 = (bf16[72,256]{1,0:T(8,128)(2,1)S(1)}, bf16[72,256]{1,0:T(8,128)(2,1)S(1)}, u32[]{:S(2)}, u32[]{:S(2)}) collective-permute-start(bf16[72,256]{1,0:T(8,128)(2,1)S(1)} %score.5), channel_id=1, source_target_pairs={{0,2},{2,0},{1,3},{3,1},{4,6},{6,4},{5,7},{7,5},{8,10},{10,8},{9,1... | collective-permute-start | bytes 110600 | tf_op jit(solution)/shard_map/ppermute | solution.py:212
  28.6 0.8 %score.4.refs_2_ = f32[72,256]{1,0:T(8,128)S(1)} custom-call(bf16[24,4096]{1,0:T(8,128)(2,1)S(1)} %collective-permute-done.5.refs_0_, bf16[24,4096]{1,0:T(8,128)(2,1)S(1)} %collective-permute-done.6.refs_1_, bf16[24,2560]{1,0:T(8,128)(2,1)S(1)} %collective-permute-done.7.refs_2_, bf16[24,1536]{1,0:T(8,128)(2,1)S(1)} %collective-permute-done.8.refs_3_, ...), custom_call_target="tpu_custom_call" | custom-call | flops 536870912 | bytes 1048576 | tf_op jit(solution)/shard_map/score/pallas_call | solution.py:195
  29.4 0.0 collective-permute-done.4.refs_1_
  29.4 1.7 %collective-permute-done.9.refs_3_ = bf16[72,256]{1,0:T(8,128)(2,1)S(1)} collective-permute-done((bf16[72,256]{1,0:T(8,128)(2,1)S(1)}, bf16[72,256]{1,0:T(8,128)(2,1)S(1)}, u32[]{:S(2)}, u32[]{:S(2)}) %collective-permute-start.9) | collective-permute-done | bytes 36896 | tf_op jit(solution)/shard_map/ppermute | solution.py:212
  31.1 0.7 %finish.1 = f32[192,256]{1,0:T(8,128)} custom-call(f32[120,256]{1,0:T(8,128)S(1)} %get-tuple-element.11.refs_0_, bf16[120,256]{1,0:T(8,128)(2,1)S(1)} %collective-permute-done.4.refs_1_, f32[72,256]{1,0:T(8,128)S(1)} %score.4.refs_2_, bf16[72,256]{1,0:T(8,128)(2,1)S(1)} %collective-permute-done.9.refs_3_), custom_call_target="tpu_custom_call" | custom-call | tf_op jit(solution)/shard_map/finish/pallas_call | solution.py:245
  (2 shorter events, 0.0 us)
Async XLA Ops:
  2.0 7.9 %collective-permute-start = (bf16[24,4096]{1,0:T(8,128)(2,1)S(1)}, bf16[24,4096]{1,0:T(8,128)(2,1)S(1)}, u32[]{:S(2)}, u32[]{:S(2)}) collective-permute-start(bf16[24,4096]{1,0:T(8,128)(2,1)S(1)} %rotate.1.after_ref.refs_0_), channel_id=1, source_target_pairs={{0,4},{4,8},{8,12},{12,28},{28,24},{24,20},{20,16},{16,0},{1,5},{5... | collective-permute-start | bytes 589832 | tf_op jit(solution)/shard_map/ppermute | solution.py:261
  5.1 6.6 %collective-permute-start.1 = (bf16[24,4096]{1,0:T(8,128)(2,1)S(1)}, bf16[24,4096]{1,0:T(8,128)(2,1)S(1)}, u32[]{:S(2)}, u32[]{:S(2)}) collective-permute-start(bf16[24,4096]{1,0:T(8,128)(2,1)S(1)} %rotate.1.after_ref.refs_0_), channel_id=1, source_target_pairs={{0,16},{4,0},{8,4},{12,8},{28,12},{24,28},{20,24},{16,20},{1,17},{... | collective-permute-start | bytes 589832 | tf_op jit(solution)/shard_map/ppermute | solution.py:261
  9.9 6.1 %collective-permute-start.2 = (bf16[24,4096]{1,0:T(8,128)(2,1)S(1)}, bf16[24,4096]{1,0:T(8,128)(2,1)S(1)}, u32[]{:S(2)}, u32[]{:S(2)}) collective-permute-start(bf16[24,4096]{1,0:T(8,128)(2,1)S(1)} %collective-permute-done.refs_1_), channel_id=1, source_target_pairs={{0,4},{4,8},{8,12},{12,28},{28,24},{24,20},{20,16},{16,0},{1,5},{5... | collective-permute-start | bytes 589832 | tf_op jit(solution)/shard_map/ppermute | solution.py:261
  11.7 5.8 %collective-permute-start.3 = (bf16[24,4096]{1,0:T(8,128)(2,1)S(1)}, bf16[24,4096]{1,0:T(8,128)(2,1)S(1)}, u32[]{:S(2)}, u32[]{:S(2)}) collective-permute-start(bf16[24,4096]{1,0:T(8,128)(2,1)S(1)} %collective-permute-done.1.refs_2_), channel_id=1, source_target_pairs={{0,16},{4,0},{8,4},{12,8},{28,12},{24,28},{20,24},{16,20},{1,17},{... | collective-permute-start | bytes 589832 | tf_op jit(solution)/shard_map/ppermute | solution.py:261
  16.0 10.2 %collective-permute-start.5 = (bf16[24,4096]{1,0:T(8,128)(2,1)S(1)}, bf16[24,4096]{1,0:T(8,128)(2,1)S(1)}, u32[]{:S(2)}, u32[]{:S(2)}) collective-permute-start(bf16[24,4096]{1,0:T(8,128)(2,1)S(1)} %collective-permute-done.2.refs_3_), channel_id=1, source_target_pairs={{0,4},{4,8},{8,12},{12,28},{28,24},{24,20},{20,16},{16,0},{1,5},{5... | collective-permute-start | bytes 589832 | tf_op jit(solution)/shard_map/ppermute | solution.py:261
  17.5 8.8 %collective-permute-start.6 = (bf16[24,4096]{1,0:T(8,128)(2,1)S(1)}, bf16[24,4096]{1,0:T(8,128)(2,1)S(1)}, u32[]{:S(2)}, u32[]{:S(2)}) collective-permute-start(bf16[24,4096]{1,0:T(8,128)(2,1)S(1)} %collective-permute-done.3.refs_4_), channel_id=1, source_target_pairs={{0,16},{4,0},{8,4},{12,8},{28,12},{24,28},{20,24},{16,20},{1,17},{... | collective-permute-start | bytes 589832 | tf_op jit(solution)/shard_map/ppermute | solution.py:261
  18.1 8.2 %collective-permute-start.7 = (bf16[24,2560]{1,0:T(8,128)(2,1)S(1)}, bf16[24,2560]{1,0:T(8,128)(2,1)S(1)}, u32[]{:S(2)}, u32[]{:S(2)}) collective-permute-start(bf16[24,2560]{1,0:T(8,128)(2,1)S(1)} %slice.8), channel_id=1, source_target_pairs={{0,8},{4,12},{8,28},{12,24},{28,20},{24,16},{20,0},{16,4},{1,9},{5... | collective-permute-start | bytes 368648 | tf_op jit(solution)/shard_map/ppermute | solution.py:261
  20.6 5.3 %collective-permute-start.8 = (bf16[24,1536]{1,0:T(8,128)(2,1)S(1)}, bf16[24,1536]{1,0:T(8,128)(2,1)S(1)}, u32[]{:S(2)}, u32[]{:S(2)}) collective-permute-start(bf16[24,1536]{1,0:T(8,128)(2,1)S(1)} %slice.9), channel_id=1, source_target_pairs={{0,20},{4,16},{8,0},{12,4},{28,8},{24,12},{20,28},{16,24},{1,21},{... | collective-permute-start | bytes 221192 | tf_op jit(solution)/shard_map/ppermute | solution.py:261
  22.6 6.8 %collective-permute-start.4 = (bf16[120,256]{1,0:T(8,128)(2,1)S(1)}, bf16[120,256]{1,0:T(8,128)(2,1)S(1)}, u32[]{:S(2)}, u32[]{:S(2)}) collective-permute-start(bf16[120,256]{1,0:T(8,128)(2,1)S(1)} %get-tuple-element.12), channel_id=1, source_target_pairs={{0,2},{2,0},{1,3},{3,1},{4,6},{6,4},{5,7},{7,5},{8,10},{10,8},{9,1... | collective-permute-start | bytes 184328 | tf_op jit(solution)/shard_map/ppermute | solution.py:212
  27.0 4.0 %collective-permute-start.9 = (bf16[72,256]{1,0:T(8,128)(2,1)S(1)}, bf16[72,256]{1,0:T(8,128)(2,1)S(1)}, u32[]{:S(2)}, u32[]{:S(2)}) collective-permute-start(bf16[72,256]{1,0:T(8,128)(2,1)S(1)} %score.5), channel_id=1, source_target_pairs={{0,2},{2,0},{1,3},{3,1},{4,6},{6,4},{5,7},{7,5},{8,10},{10,8},{9,1... | collective-permute-start | bytes 110600 | tf_op jit(solution)/shard_map/ppermute | solution.py:212

commit v6 on v5

--- a/solution.py
+++ b/solution.py
@@ -137,7 +137,7 @@
     )(*map(in_hbm, operands))
 
 
-def fetch_kernel(after_ref, store_hbm, store_ref, sems):
+def fetch_kernel(shares, after_ref, store_hbm, store_ref, turned_ref, sems):
     del after_ref
     parts = sems.shape[0]
     rows = store_ref.shape[1] // parts
@@ -151,22 +151,33 @@
         copy.start()
     for copy in copies:
         copy.wait()
+    lay = lax.axis_index("lay")
+    for k in range(shares - 1):
+        share = turned_ref.shape[2]
+        owned = pl.ds(pl.multiple_of(lax.rem(lay + k + 1, shares) * share, share), share)
+        turned_ref[k] = store_ref[0, owned, :].T
 
 
 def fetch(after, store):
+    shares = lax.axis_size("lay")
+    _, examples, dim = store.shape
+    vmem = pl.BlockSpec(memory_space=pltpu.VMEM)
     return pl.pallas_call(
-        fetch_kernel,
-        out_shape=jax.ShapeDtypeStruct(store.shape, store.dtype),
-        in_specs=[pl.BlockSpec(memory_space=pltpu.VMEM), pl.BlockSpec(memory_space=pltpu.HBM)],
-        out_specs=pl.BlockSpec(memory_space=pltpu.VMEM),
+        functools.partial(fetch_kernel, shares),
+        out_shape=[
+            jax.ShapeDtypeStruct(store.shape, store.dtype),
+            jax.ShapeDtypeStruct((shares - 1, dim, examples // shares), store.dtype),
+        ],
+        in_specs=[vmem, pl.BlockSpec(memory_space=pltpu.HBM)],
+        out_specs=[vmem] * 2,
         scratch_shapes=[pltpu.SemaphoreType.DMA((4,))],
-        compiler_params=pltpu.CompilerParams(vmem_limit_bytes=8 << 20),
+        compiler_params=pltpu.CompilerParams(vmem_limit_bytes=24 << 20),
         cost_estimate=pl.CostEstimate(flops=0, bytes_accessed=2 * store.size * 2, transcendentals=0),
         name="fetch",
     )(after, in_hbm(store))
 
 
-def score_kernel(count, height, share, shares, owners, *refs):
+def score_kernel(count, height, share, shares, owners, turned, *refs):
     outs, held = refs[-1 - len(owners):-1], refs[-1]
     pieces, store_ref = refs[:-2 - len(owners)], refs[-2 - len(owners)]
     half = pieces[0].shape[0]
@@ -178,22 +189,24 @@
         column += piece.shape[1]
     lay = lax.axis_index("lay")
     for out, owner in zip(outs, owners):
-        rows = pl.ds(pl.multiple_of(lax.rem(lay + owner, shares) * share, share), share)
-        block = lax.dot_general(held[...], store_ref[0, rows, :], NT, preferred_element_type=F32)
+        if not turned:
+            rows = pl.ds(pl.multiple_of(lax.rem(lay + owner, shares) * share, share), share)
+            block = lax.dot_general(held[...], store_ref[0, rows, :], NT, preferred_element_type=F32)
+        else:
+            block = jnp.dot(held[...], store_ref[owner - 1], preferred_element_type=F32)
         for j in range(out.shape[0] // half):
             out[j * half:(j + 1) * half, :] = block[j * height:j * height + half].astype(out.dtype)
 
 
-def score(pieces, parts, store, owners):
-    half = (pieces + parts)[0].shape[0]
-    _, examples, dim = store.shape
+def score(pieces, parts, store, owners, turned=False):
+    half, dim = pieces[0].shape
     shares = lax.axis_size("lay")
-    share = examples // shares
+    share = store.shape[2] if turned else store.shape[1] // shares
     whole = len(pieces) + (1 if parts else 0)
     height = -(-half // 16) * 16
     vmem = pl.BlockSpec(memory_space=pltpu.VMEM)
     return pl.pallas_call(
-        functools.partial(score_kernel, len(pieces), height, share, shares, tuple(owners)),
+        functools.partial(score_kernel, len(pieces), height, share, shares, tuple(owners), turned),
         out_shape=[jax.ShapeDtypeStruct((whole * half, share), BF16 if owner else F32) for owner in owners],
         in_specs=[vmem] * (len(pieces) + len(parts) + 1),
         out_specs=[vmem] * len(owners),
@@ -261,11 +274,11 @@
         return lax.ppermute(piece, RING, [(a, ring[(i + steps) % len(ring)]) for i, a in enumerate(ring)])
 
     own = rotate(query_grads, query_block, layer_slot, out_basis, in_basis, eigen_values, damping)
-    store = fetch(own, store_grads)
+    store, turned = fetch(own, store_grads)
     half, dim = own.shape
     others = range(1, lax.axis_size("lay"))
     one = two = own
-    batch, sums, hidden = [own], [], [store]
+    batch, sums, hidden = [own], [], [store, turned]
     for step in range(1, members):
         if step == members - 1:
             cut = dim // 8 * 5 // 128 * 128
@@ -276,7 +289,7 @@
         if step < members - 1:
             one, hidden = lax.optimization_barrier((one, hidden))
         if step == 1:
-            store, = hidden
+            store, turned = hidden
         elif hidden:
             keep, *sends = hidden
             sums.append((keep, swap_layers(sends)))
@@ -285,7 +298,7 @@
         if len(batch) >= 5 and step < members - 1:
             hidden = score(batch, [], store, [0, *others])
             batch = []
-    got = swap_layers(score(batch, parts, store, others))
+    got = swap_layers(score(batch, parts, turned, others, True))
     sums.append((*score(batch, parts, store, [0]), got))
     return finish(half, sums).T
 

time: 31.9 us -> 31.6 us (level)
  waiting for transfers between devices: 10.6 us -> 10 us
    pallas_call x1, Pallas kernels: 2.2 us -> 2.8 us  [fetch(): pl.pallas_call(functools.partial(fetch_kernel, shares), out_shape=[jax.Sh...]
    ppermute x8, waiting for transfers between devices: 8.92 us -> 8.32 us  [hop(): lax.ppermute(piece, RING, [(a, ring[(i + steps) % len(ring)]) for i, a in...]
  transfers between devices with their start and end apart: 10 -> 10, of which waited for: 5 -> 5; matrix products, arithmetic and copies ran while one was open for 0% -> 0% of each run, Pallas kernels for 17% -> 18%
where the time goes in v6:
time: 31.6 us; the launch traced here: 31.5 us
  starting transfers between devices  13.1 us (41%)
  waiting for transfers between devices  10 us (32%)
  Pallas kernels  8.28 us (26%)
    ppermute x8, starting transfers between devices, hop(): lax.ppermute(piece, RING, [(a, ring[(i + steps) % len(ring)]) for i, a in...  10.1 us
    ppermute x8, waiting for transfers between devices, hop(): lax.ppermute(piece, RING, [(a, ring[(i + steps) % len(ring)]) for i, a in...  8.32 us
    ppermute x2, starting transfers between devices, swap_layers(): lax.ppermute(send, 'lay', [(i, (i + k + 1) % shares) for i in range(share...  3.02 us
    pallas_call x1, Pallas kernels, fetch(): pl.pallas_call(functools.partial(fetch_kernel, shares), out_shape=[jax.Sh...  2.8 us
    pallas_call x3, Pallas kernels, score(): pl.pallas_call(functools.partial(score_kernel, len(pieces), height, share...  2.77 us
    pallas_call x1, Pallas kernels, rotate(): pl.pallas_call(functools.partial(rotate_kernel, half, 1), out_shape=jax.S...  2 us
    ppermute x2, waiting for transfers between devices, swap_layers(): lax.ppermute(send, 'lay', [(i, (i + k + 1) % shares) for i in range(share...  1.68 us
    pallas_call x1, Pallas kernels, finish(): pl.pallas_call(functools.partial(finish_kernel, half, members, sizes), ou...  0.71 us
  transfers between devices with their start and end apart: 10, of which 5 were waited for; matrix products, arithmetic and copies ran while one was open for 0% of the time, Pallas kernels for 18%

profile of v6, /device:TPU:0, one launch (start us, length us, event | category | flops | bytes accessed | tf_op | source)
XLA Modules:
  0.0 31.5 jit_solution(1680151063693679061)
XLA Ops:
  0.0 2.0 %rotate.1.after_ref.refs_0_ = bf16[24,4096]{1,0:T(8,128)(2,1)S(1)} custom-call(bf16[1,48,4096]{2,1,0:T(8,128)(2,1)} %query_hbm.1, s32[384]{0:T(512)} %block_hbm.1, f32[4]{0:T(128)} %damping_hbm.1, s32[2]{0:T(128)} %slot_hbm.1, bf16[2,64,64]{2,1,0:T(8,128)(2,1)} %out_hbm.1, bf16[2,64,64]{2,1,0:T(8,128)(2,1)} %in_hbm.1, f32[2,64,64]{2,1,0:T(8,128)} %eigen_hbm.1), custom_call_target="tpu_custom_call" | custom-call | flops 201326592 | bytes 1048576 | tf_op jit(solution)/shard_map/rotate/pallas_call | solution.py:123
  2.0 3.1 %collective-permute-start = (bf16[24,4096]{1,0:T(8,128)(2,1)S(1)}, bf16[24,4096]{1,0:T(8,128)(2,1)S(1)}, u32[]{:S(2)}, u32[]{:S(2)}) collective-permute-start(bf16[24,4096]{1,0:T(8,128)(2,1)S(1)} %rotate.1.after_ref.refs_0_), channel_id=1, source_target_pairs={{0,4},{4,8},{8,12},{12,28},{28,24},{24,20},{20,16},{16,0},{1,5},{5... | collective-permute-start | bytes 589832 | tf_op jit(solution)/shard_map/ppermute | solution.py:274
  5.1 0.0 collective-permute-start.1
  5.1 2.8 %fetch.1 = (bf16[1,512,4096]{2,1,0:T(8,128)(2,1)S(1)}, bf16[1,4096,256]{2,1,0:T(8,128)(2,1)S(1)}) custom-call(bf16[24,4096]{1,0:T(8,128)(2,1)S(1)} %rotate.1.after_ref.refs_0_, bf16[1,512,4096]{2,1,0:T(8,128)(2,1)} %store_hbm.1), custom_call_target="tpu_custom_call" | custom-call | bytes 8388608 | tf_op jit(solution)/shard_map/fetch/pallas_call | solution.py:165
  7.9 2.0 %collective-permute-done.refs_1_ = bf16[24,4096]{1,0:T(8,128)(2,1)S(1)} collective-permute-done((bf16[24,4096]{1,0:T(8,128)(2,1)S(1)}, bf16[24,4096]{1,0:T(8,128)(2,1)S(1)}, u32[]{:S(2)}, u32[]{:S(2)}) %collective-permute-start) | collective-permute-done | bytes 196640 | tf_op jit(solution)/shard_map/ppermute | solution.py:274
  9.9 1.8 %collective-permute-start.2 = (bf16[24,4096]{1,0:T(8,128)(2,1)S(1)}, bf16[24,4096]{1,0:T(8,128)(2,1)S(1)}, u32[]{:S(2)}, u32[]{:S(2)}) collective-permute-start(bf16[24,4096]{1,0:T(8,128)(2,1)S(1)} %collective-permute-done.refs_1_), channel_id=1, source_target_pairs={{0,4},{4,8},{8,12},{12,28},{28,24},{24,20},{20,16},{16,0},{1,5},{5... | collective-permute-start | bytes 589832 | tf_op jit(solution)/shard_map/ppermute | solution.py:274
  11.7 0.0 collective-permute-done.1.refs_2_
  11.7 0.2 collective-permute-start.3
  12.0 4.1 %collective-permute-done.2.refs_3_ = bf16[24,4096]{1,0:T(8,128)(2,1)S(1)} collective-permute-done((bf16[24,4096]{1,0:T(8,128)(2,1)S(1)}, bf16[24,4096]{1,0:T(8,128)(2,1)S(1)}, u32[]{:S(2)}, u32[]{:S(2)}) %collective-permute-start.2) | collective-permute-done | bytes 196640 | tf_op jit(solution)/shard_map/ppermute | solution.py:274
  16.0 1.5 %collective-permute-start.5 = (bf16[24,4096]{1,0:T(8,128)(2,1)S(1)}, bf16[24,4096]{1,0:T(8,128)(2,1)S(1)}, u32[]{:S(2)}, u32[]{:S(2)}) collective-permute-start(bf16[24,4096]{1,0:T(8,128)(2,1)S(1)} %collective-permute-done.2.refs_3_), channel_id=1, source_target_pairs={{0,4},{4,8},{8,12},{12,28},{28,24},{24,20},{20,16},{16,0},{1,5},{5... | collective-permute-start | bytes 589832 | tf_op jit(solution)/shard_map/ppermute | solution.py:274
  17.5 0.0 collective-permute-done.3.refs_4_
  17.5 0.6 %collective-permute-start.6 = (bf16[24,4096]{1,0:T(8,128)(2,1)S(1)}, bf16[24,4096]{1,0:T(8,128)(2,1)S(1)}, u32[]{:S(2)}, u32[]{:S(2)}) collective-permute-start(bf16[24,4096]{1,0:T(8,128)(2,1)S(1)} %collective-permute-done.3.refs_4_), channel_id=1, source_target_pairs={{0,16},{4,0},{8,4},{12,8},{28,12},{24,28},{20,24},{16,20},{1,17},{... | collective-permute-start | bytes 589832 | tf_op jit(solution)/shard_map/ppermute | solution.py:274
  18.1 2.5 %collective-permute-start.7 = (bf16[24,2560]{1,0:T(8,128)(2,1)S(1)}, bf16[24,2560]{1,0:T(8,128)(2,1)S(1)}, u32[]{:S(2)}, u32[]{:S(2)}) collective-permute-start(bf16[24,2560]{1,0:T(8,128)(2,1)S(1)} %slice.8), channel_id=1, source_target_pairs={{0,8},{4,12},{8,28},{12,24},{28,20},{24,16},{20,0},{16,4},{1,9},{5... | collective-permute-start | bytes 368648 | tf_op jit(solution)/shard_map/ppermute | solution.py:274
  20.6 0.4 %collective-permute-start.8 = (bf16[24,1536]{1,0:T(8,128)(2,1)S(1)}, bf16[24,1536]{1,0:T(8,128)(2,1)S(1)}, u32[]{:S(2)}, u32[]{:S(2)}) collective-permute-start(bf16[24,1536]{1,0:T(8,128)(2,1)S(1)} %slice.9), channel_id=1, source_target_pairs={{0,20},{4,16},{8,0},{12,4},{28,8},{24,12},{20,28},{16,24},{1,21},{... | collective-permute-start | bytes 221192 | tf_op jit(solution)/shard_map/ppermute | solution.py:274
  21.1 1.5 %score.3 = (f32[120,256]{1,0:T(8,128)S(1)}, bf16[120,256]{1,0:T(8,128)(2,1)S(1)}) custom-call(bf16[24,4096]{1,0:T(8,128)(2,1)S(1)} %rotate.1.after_ref.refs_0_, bf16[24,4096]{1,0:T(8,128)(2,1)S(1)} %collective-permute-done.refs_1_, bf16[24,4096]{1,0:T(8,128)(2,1)S(1)} %collective-permute-done.1.refs_2_, bf16[24,4096]{1,0:T(8,128)(2,1)S(1)} %collective-permute-done.2.refs_3_, ...), custom_call_target="tpu_custom_call" | custom-call | flops 1073741824 | bytes 1048576 | tf_op jit(solution)/shard_map/score/pallas_call | solution.py:208
  22.6 1.5 %collective-permute-start.4 = (bf16[120,256]{1,0:T(8,128)(2,1)S(1)}, bf16[120,256]{1,0:T(8,128)(2,1)S(1)}, u32[]{:S(2)}, u32[]{:S(2)}) collective-permute-start(bf16[120,256]{1,0:T(8,128)(2,1)S(1)} %get-tuple-element.17), channel_id=1, source_target_pairs={{0,2},{2,0},{1,3},{3,1},{4,6},{6,4},{5,7},{7,5},{8,10},{10,8},{9,1... | collective-permute-start | bytes 184328 | tf_op jit(solution)/shard_map/ppermute | solution.py:225
  24.0 1.8 %collective-permute-done.8.refs_3_ = bf16[24,1536]{1,0:T(8,128)(2,1)S(1)} collective-permute-done((bf16[24,1536]{1,0:T(8,128)(2,1)S(1)}, bf16[24,1536]{1,0:T(8,128)(2,1)S(1)}, u32[]{:S(2)}, u32[]{:S(2)}) %collective-permute-start.8) | collective-permute-done | bytes 73760 | tf_op jit(solution)/shard_map/ppermute | solution.py:274
  25.9 0.4 %collective-permute-done.7.refs_2_ = bf16[24,2560]{1,0:T(8,128)(2,1)S(1)} collective-permute-done((bf16[24,2560]{1,0:T(8,128)(2,1)S(1)}, bf16[24,2560]{1,0:T(8,128)(2,1)S(1)}, u32[]{:S(2)}, u32[]{:S(2)}) %collective-permute-start.7) | collective-permute-done | bytes 122912 | tf_op jit(solution)/shard_map/ppermute | solution.py:274
  26.3 0.0 collective-permute-done.5.refs_0_
  26.3 0.0 collective-permute-done.6.refs_1_
  26.3 0.5 %score.5 = bf16[72,256]{1,0:T(8,128)(2,1)S(1)} custom-call(bf16[24,4096]{1,0:T(8,128)(2,1)S(1)} %collective-permute-done.5.refs_0_, bf16[24,4096]{1,0:T(8,128)(2,1)S(1)} %collective-permute-done.6.refs_1_, bf16[24,2560]{1,0:T(8,128)(2,1)S(1)} %collective-permute-done.7.refs_2_, bf16[24,1536]{1,0:T(8,128)(2,1)S(1)} %collective-permute-done.8.refs_3_, ...), custom_call_target="tpu_custom_call" | custom-call | flops 536870912 | bytes 1048576 | tf_op jit(solution)/shard_map/score/pallas_call | solution.py:208
  26.7 1.6 %collective-permute-start.9 = (bf16[72,256]{1,0:T(8,128)(2,1)S(1)}, bf16[72,256]{1,0:T(8,128)(2,1)S(1)}, u32[]{:S(2)}, u32[]{:S(2)}) collective-permute-start(bf16[72,256]{1,0:T(8,128)(2,1)S(1)} %score.5), channel_id=1, source_target_pairs={{0,2},{2,0},{1,3},{3,1},{4,6},{6,4},{5,7},{7,5},{8,10},{10,8},{9,1... | collective-permute-start | bytes 110600 | tf_op jit(solution)/shard_map/ppermute | solution.py:225
  28.3 0.8 %score.4.refs_2_ = f32[72,256]{1,0:T(8,128)S(1)} custom-call(bf16[24,4096]{1,0:T(8,128)(2,1)S(1)} %collective-permute-done.5.refs_0_, bf16[24,4096]{1,0:T(8,128)(2,1)S(1)} %collective-permute-done.6.refs_1_, bf16[24,2560]{1,0:T(8,128)(2,1)S(1)} %collective-permute-done.7.refs_2_, bf16[24,1536]{1,0:T(8,128)(2,1)S(1)} %collective-permute-done.8.refs_3_, ...), custom_call_target="tpu_custom_call" | custom-call | flops 536870912 | bytes 1048576 | tf_op jit(solution)/shard_map/score/pallas_call | solution.py:208
  29.1 0.0 collective-permute-done.4.refs_1_
  29.1 1.7 %collective-permute-done.9.refs_3_ = bf16[72,256]{1,0:T(8,128)(2,1)S(1)} collective-permute-done((bf16[72,256]{1,0:T(8,128)(2,1)S(1)}, bf16[72,256]{1,0:T(8,128)(2,1)S(1)}, u32[]{:S(2)}, u32[]{:S(2)}) %collective-permute-start.9) | collective-permute-done | bytes 36896 | tf_op jit(solution)/shard_map/ppermute | solution.py:225
  30.8 0.7 %finish.1 = f32[192,256]{1,0:T(8,128)} custom-call(f32[120,256]{1,0:T(8,128)S(1)} %get-tuple-element.16.refs_0_, bf16[120,256]{1,0:T(8,128)(2,1)S(1)} %collective-permute-done.4.refs_1_, f32[72,256]{1,0:T(8,128)S(1)} %score.4.refs_2_, bf16[72,256]{1,0:T(8,128)(2,1)S(1)} %collective-permute-done.9.refs_3_), custom_call_target="tpu_custom_call" | custom-call | tf_op jit(solution)/shard_map/finish/pallas_call | solution.py:258
  (2 shorter events, 0.0 us)
Async XLA Ops:
  2.0 7.9 %collective-permute-start = (bf16[24,4096]{1,0:T(8,128)(2,1)S(1)}, bf16[24,4096]{1,0:T(8,128)(2,1)S(1)}, u32[]{:S(2)}, u32[]{:S(2)}) collective-permute-start(bf16[24,4096]{1,0:T(8,128)(2,1)S(1)} %rotate.1.after_ref.refs_0_), channel_id=1, source_target_pairs={{0,4},{4,8},{8,12},{12,28},{28,24},{24,20},{20,16},{16,0},{1,5},{5... | collective-permute-start | bytes 589832 | tf_op jit(solution)/shard_map/ppermute | solution.py:274
  5.1 6.6 %collective-permute-start.1 = (bf16[24,4096]{1,0:T(8,128)(2,1)S(1)}, bf16[24,4096]{1,0:T(8,128)(2,1)S(1)}, u32[]{:S(2)}, u32[]{:S(2)}) collective-permute-start(bf16[24,4096]{1,0:T(8,128)(2,1)S(1)} %rotate.1.after_ref.refs_0_), channel_id=1, source_target_pairs={{0,16},{4,0},{8,4},{12,8},{28,12},{24,28},{20,24},{16,20},{1,17},{... | collective-permute-start | bytes 589832 | tf_op jit(solution)/shard_map/ppermute | solution.py:274
  9.9 6.1 %collective-permute-start.2 = (bf16[24,4096]{1,0:T(8,128)(2,1)S(1)}, bf16[24,4096]{1,0:T(8,128)(2,1)S(1)}, u32[]{:S(2)}, u32[]{:S(2)}) collective-permute-start(bf16[24,4096]{1,0:T(8,128)(2,1)S(1)} %collective-permute-done.refs_1_), channel_id=1, source_target_pairs={{0,4},{4,8},{8,12},{12,28},{28,24},{24,20},{20,16},{16,0},{1,5},{5... | collective-permute-start | bytes 589832 | tf_op jit(solution)/shard_map/ppermute | solution.py:274
  11.7 5.8 %collective-permute-start.3 = (bf16[24,4096]{1,0:T(8,128)(2,1)S(1)}, bf16[24,4096]{1,0:T(8,128)(2,1)S(1)}, u32[]{:S(2)}, u32[]{:S(2)}) collective-permute-start(bf16[24,4096]{1,0:T(8,128)(2,1)S(1)} %collective-permute-done.1.refs_2_), channel_id=1, source_target_pairs={{0,16},{4,0},{8,4},{12,8},{28,12},{24,28},{20,24},{16,20},{1,17},{... | collective-permute-start | bytes 589832 | tf_op jit(solution)/shard_map/ppermute | solution.py:274
  16.0 10.2 %collective-permute-start.5 = (bf16[24,4096]{1,0:T(8,128)(2,1)S(1)}, bf16[24,4096]{1,0:T(8,128)(2,1)S(1)}, u32[]{:S(2)}, u32[]{:S(2)}) collective-permute-start(bf16[24,4096]{1,0:T(8,128)(2,1)S(1)} %collective-permute-done.2.refs_3_), channel_id=1, source_target_pairs={{0,4},{4,8},{8,12},{12,28},{28,24},{24,20},{20,16},{16,0},{1,5},{5... | collective-permute-start | bytes 589832 | tf_op jit(solution)/shard_map/ppermute | solution.py:274
  17.5 8.8 %collective-permute-start.6 = (bf16[24,4096]{1,0:T(8,128)(2,1)S(1)}, bf16[24,4096]{1,0:T(8,128)(2,1)S(1)}, u32[]{:S(2)}, u32[]{:S(2)}) collective-permute-start(bf16[24,4096]{1,0:T(8,128)(2,1)S(1)} %collective-permute-done.3.refs_4_), channel_id=1, source_target_pairs={{0,16},{4,0},{8,4},{12,8},{28,12},{24,28},{20,24},{16,20},{1,17},{... | collective-permute-start | bytes 589832 | tf_op jit(solution)/shard_map/ppermute | solution.py:274
  18.1 8.2 %collective-permute-start.7 = (bf16[24,2560]{1,0:T(8,128)(2,1)S(1)}, bf16[24,2560]{1,0:T(8,128)(2,1)S(1)}, u32[]{:S(2)}, u32[]{:S(2)}) collective-permute-start(bf16[24,2560]{1,0:T(8,128)(2,1)S(1)} %slice.8), channel_id=1, source_target_pairs={{0,8},{4,12},{8,28},{12,24},{28,20},{24,16},{20,0},{16,4},{1,9},{5... | collective-permute-start | bytes 368648 | tf_op jit(solution)/shard_map/ppermute | solution.py:274
  20.6 5.3 %collective-permute-start.8 = (bf16[24,1536]{1,0:T(8,128)(2,1)S(1)}, bf16[24,1536]{1,0:T(8,128)(2,1)S(1)}, u32[]{:S(2)}, u32[]{:S(2)}) collective-permute-start(bf16[24,1536]{1,0:T(8,128)(2,1)S(1)} %slice.9), channel_id=1, source_target_pairs={{0,20},{4,16},{8,0},{12,4},{28,8},{24,12},{20,28},{16,24},{1,21},{... | collective-permute-start | bytes 221192 | tf_op jit(solution)/shard_map/ppermute | solution.py:274
  22.6 6.5 %collective-permute-start.4 = (bf16[120,256]{1,0:T(8,128)(2,1)S(1)}, bf16[120,256]{1,0:T(8,128)(2,1)S(1)}, u32[]{:S(2)}, u32[]{:S(2)}) collective-permute-start(bf16[120,256]{1,0:T(8,128)(2,1)S(1)} %get-tuple-element.17), channel_id=1, source_target_pairs={{0,2},{2,0},{1,3},{3,1},{4,6},{6,4},{5,7},{7,5},{8,10},{10,8},{9,1... | collective-permute-start | bytes 184328 | tf_op jit(solution)/shard_map/ppermute | solution.py:225
  26.7 4.0 %collective-permute-start.9 = (bf16[72,256]{1,0:T(8,128)(2,1)S(1)}, bf16[72,256]{1,0:T(8,128)(2,1)S(1)}, u32[]{:S(2)}, u32[]{:S(2)}) collective-permute-start(bf16[72,256]{1,0:T(8,128)(2,1)S(1)} %score.5), channel_id=1, source_target_pairs={{0,2},{2,0},{1,3},{3,1},{4,6},{6,4},{5,7},{7,5},{8,10},{10,8},{9,1... | collective-permute-start | bytes 110600 | tf_op jit(solution)/shard_map/ppermute | solution.py:225

commit v7 on v6

--- a/solution.py
+++ b/solution.py
@@ -54,7 +54,7 @@
         block = query_ref[0, :, pair * 128:(pair + 1) * 128].astype(F32)
         rows_ref[pair * half:(pair + 1) * half, :] = jnp.where(slab == 0, block[:half], block[half:2 * half])
 
-    basis_ref[:, :RANK] = out_ref[model_layer].astype(F32)
+    basis_ref[:RANK, :RANK] = out_ref[model_layer].astype(F32)
     out_rows = jnp.concatenate(
         [basis_ref[pl.ds(0, RANK // 2, stride=2), :], basis_ref[pl.ds(1, RANK // 2, stride=2), :]], axis=0
     )
@@ -126,9 +126,9 @@
         in_specs=[pl.BlockSpec(memory_space=pltpu.HBM)] * len(operands),
         out_specs=pl.BlockSpec(memory_space=pltpu.VMEM),
         scratch_shapes=[home(x.shape, x.dtype) for home, x in zip(homes, operands)] + [
-            pltpu.VMEM((half * dim // 128, 128), F32),
-            pltpu.VMEM((RANK, 128), F32),
-            pltpu.VMEM((half * dim // 128, 128), F32),
+            pltpu.VMEM((half * (dim // 128 + 1), 128), F32),
+            pltpu.VMEM((RANK + 8, 128), F32),
+            pltpu.VMEM((half * (dim // 128 + 1), 128), F32),
             pltpu.SemaphoreType.DMA((len(operands),)),
         ],
         compiler_params=pltpu.CompilerParams(vmem_limit_bytes=16 << 20),
@@ -199,7 +199,8 @@
 
 
 def score(pieces, parts, store, owners, turned=False):
-    half, dim = pieces[0].shape
+    half = (pieces + parts)[0].shape[0]
+    dim = pieces[0].shape[1] if pieces else sum(part.shape[1] for part in parts)
     shares = lax.axis_size("lay")
     share = store.shape[2] if turned else store.shape[1] // shares
     whole = len(pieces) + (1 if parts else 0)
@@ -270,6 +271,7 @@
 ):
     members = lax.axis_size("ex")
     ring = list(range(members)) + [members + i for i in reversed(range(members))]
+
     def hop(piece, steps):
         return lax.ppermute(piece, RING, [(a, ring[(i + steps) % len(ring)]) for i, a in enumerate(ring)])
 
@@ -298,8 +300,13 @@
         if len(batch) >= 5 and step < members - 1:
             hidden = score(batch, [], store, [0, *others])
             batch = []
-    got = swap_layers(score(batch, parts, turned, others, True))
-    sums.append((*score(batch, parts, store, [0]), got))
+    sends = score(batch, [], turned, others, True)
+    near = swap_layers(sends)
+    parts, _ = lax.optimization_barrier((parts, sends))
+    far = swap_layers(score([], parts, turned, others, True))
+    (keep,) = score(batch, parts, store, [0])
+    rows = len(batch) * half
+    sums += [(keep[:rows], near), (keep[rows:], far)]
     return finish(half, sums).T
 
 

time: 31.6 us -> 31.3 us (level)
  waiting for transfers between devices: 10 us -> 7.75 us
  starting transfers between devices: 13.1 us -> 14.6 us
  Pallas kernels: 8.28 us -> 8.75 us
    ppermute x8, waiting for transfers between devices: 8.32 us -> 6.34 us  [hop(): lax.ppermute(piece, RING, [(a, ring[(i + steps) % len(ring)]) for i, a in...]
    ppermute x2 -> x3, starting transfers between devices: 3.02 us -> 4.45 us  [swap_layers(): lax.ppermute(send, 'lay', [(i, (i + k + 1) % shares) for i in range(share...]
    pallas_call x3 -> x4, Pallas kernels: 2.77 us -> 3.23 us  [score(): pl.pallas_call(functools.partial(score_kernel, len(pieces), height, share...]
    ppermute x2 -> x3, waiting for transfers between devices: 1.68 us -> 1.41 us  [swap_layers(): lax.ppermute(send, 'lay', [(i, (i + k + 1) % shares) for i in range(share...]
  transfers between devices with their start and end apart: 10 -> 11, of which waited for: 5 -> 4; matrix products, arithmetic and copies ran while one was open for 0% -> 0% of each run, Pallas kernels for 18% -> 19%
where the time goes in v7:
time: 31.3 us; the launch traced here: 31.2 us
  starting transfers between devices  14.6 us (47%)
  Pallas kernels  8.75 us (28%)
  waiting for transfers between devices  7.75 us (25%)
    ppermute x8, starting transfers between devices, hop(): lax.ppermute(piece, RING, [(a, ring[(i + steps) % len(ring)]) for i, a in...  10.1 us
    ppermute x8, waiting for transfers between devices, hop(): lax.ppermute(piece, RING, [(a, ring[(i + steps) % len(ring)]) for i, a in...  6.34 us
    ppermute x3, starting transfers between devices, swap_layers(): lax.ppermute(send, 'lay', [(i, (i + k + 1) % shares) for i in range(share...  4.45 us
    pallas_call x4, Pallas kernels, score(): pl.pallas_call(functools.partial(score_kernel, len(pieces), height, share...  3.23 us
    pallas_call x1, Pallas kernels, fetch(): pl.pallas_call(functools.partial(fetch_kernel, shares), out_shape=[jax.Sh...  2.8 us
    pallas_call x1, Pallas kernels, rotate(): pl.pallas_call(functools.partial(rotate_kernel, half, 1), out_shape=jax.S...  2 us
    ppermute x3, waiting for transfers between devices, swap_layers(): lax.ppermute(send, 'lay', [(i, (i + k + 1) % shares) for i in range(share...  1.41 us
    pallas_call x1, Pallas kernels, finish(): pl.pallas_call(functools.partial(finish_kernel, half, members, sizes), ou...  0.71 us
  transfers between devices with their start and end apart: 11, of which 4 were waited for; matrix products, arithmetic and copies ran while one was open for 0% of the time, Pallas kernels for 19%

profile of v7, /device:TPU:0, one launch (start us, length us, event | category | flops | bytes accessed | tf_op | source)
XLA Modules:
  0.0 31.2 jit_solution(14448443208636460502)
XLA Ops:
  0.0 2.0 %rotate.1.after_ref.refs_0_ = bf16[24,4096]{1,0:T(8,128)(2,1)S(1)} custom-call(bf16[1,48,4096]{2,1,0:T(8,128)(2,1)} %query_hbm.1, s32[384]{0:T(512)} %block_hbm.1, f32[4]{0:T(128)} %damping_hbm.1, s32[2]{0:T(128)} %slot_hbm.1, bf16[2,64,64]{2,1,0:T(8,128)(2,1)} %out_hbm.1, bf16[2,64,64]{2,1,0:T(8,128)(2,1)} %in_hbm.1, f32[2,64,64]{2,1,0:T(8,128)} %eigen_hbm.1), custom_call_target="tpu_custom_call" | custom-call | flops 201326592 | bytes 1048576 | tf_op jit(solution)/shard_map/rotate/pallas_call | solution.py:123
  2.0 3.1 %collective-permute-start = (bf16[24,4096]{1,0:T(8,128)(2,1)S(1)}, bf16[24,4096]{1,0:T(8,128)(2,1)S(1)}, u32[]{:S(2)}, u32[]{:S(2)}) collective-permute-start(bf16[24,4096]{1,0:T(8,128)(2,1)S(1)} %rotate.1.after_ref.refs_0_), channel_id=1, source_target_pairs={{0,4},{4,8},{8,12},{12,28},{28,24},{24,20},{20,16},{16,0},{1,5},{5... | collective-permute-start | bytes 589832 | tf_op jit(solution)/shard_map/ppermute | solution.py:276
  5.1 0.0 collective-permute-start.1
  5.1 2.8 %fetch.1 = (bf16[1,512,4096]{2,1,0:T(8,128)(2,1)S(1)}, bf16[1,4096,256]{2,1,0:T(8,128)(2,1)S(1)}) custom-call(bf16[24,4096]{1,0:T(8,128)(2,1)S(1)} %rotate.1.after_ref.refs_0_, bf16[1,512,4096]{2,1,0:T(8,128)(2,1)} %store_hbm.1), custom_call_target="tpu_custom_call" | custom-call | bytes 8388608 | tf_op jit(solution)/shard_map/fetch/pallas_call | solution.py:165
  7.9 2.0 %collective-permute-done.refs_1_ = bf16[24,4096]{1,0:T(8,128)(2,1)S(1)} collective-permute-done((bf16[24,4096]{1,0:T(8,128)(2,1)S(1)}, bf16[24,4096]{1,0:T(8,128)(2,1)S(1)}, u32[]{:S(2)}, u32[]{:S(2)}) %collective-permute-start) | collective-permute-done | bytes 196640 | tf_op jit(solution)/shard_map/ppermute | solution.py:276
  9.9 1.8 %collective-permute-start.2 = (bf16[24,4096]{1,0:T(8,128)(2,1)S(1)}, bf16[24,4096]{1,0:T(8,128)(2,1)S(1)}, u32[]{:S(2)}, u32[]{:S(2)}) collective-permute-start(bf16[24,4096]{1,0:T(8,128)(2,1)S(1)} %collective-permute-done.refs_1_), channel_id=1, source_target_pairs={{0,4},{4,8},{8,12},{12,28},{28,24},{24,20},{20,16},{16,0},{1,5},{5... | collective-permute-start | bytes 589832 | tf_op jit(solution)/shard_map/ppermute | solution.py:276
  11.7 0.0 collective-permute-done.1.refs_2_
  11.7 0.2 collective-permute-start.3
  12.0 4.1 %collective-permute-done.2.refs_3_ = bf16[24,4096]{1,0:T(8,128)(2,1)S(1)} collective-permute-done((bf16[24,4096]{1,0:T(8,128)(2,1)S(1)}, bf16[24,4096]{1,0:T(8,128)(2,1)S(1)}, u32[]{:S(2)}, u32[]{:S(2)}) %collective-permute-start.2) | collective-permute-done | bytes 196640 | tf_op jit(solution)/shard_map/ppermute | solution.py:276
  16.0 1.5 %collective-permute-start.5 = (bf16[24,4096]{1,0:T(8,128)(2,1)S(1)}, bf16[24,4096]{1,0:T(8,128)(2,1)S(1)}, u32[]{:S(2)}, u32[]{:S(2)}) collective-permute-start(bf16[24,4096]{1,0:T(8,128)(2,1)S(1)} %collective-permute-done.2.refs_3_), channel_id=1, source_target_pairs={{0,4},{4,8},{8,12},{12,28},{28,24},{24,20},{20,16},{16,0},{1,5},{5... | collective-permute-start | bytes 589832 | tf_op jit(solution)/shard_map/ppermute | solution.py:276
  17.5 0.0 collective-permute-done.3.refs_4_
  17.5 0.5 %collective-permute-start.6 = (bf16[24,4096]{1,0:T(8,128)(2,1)S(1)}, bf16[24,4096]{1,0:T(8,128)(2,1)S(1)}, u32[]{:S(2)}, u32[]{:S(2)}) collective-permute-start(bf16[24,4096]{1,0:T(8,128)(2,1)S(1)} %collective-permute-done.3.refs_4_), channel_id=1, source_target_pairs={{0,16},{4,0},{8,4},{12,8},{28,12},{24,28},{20,24},{16,20},{1,17},{... | collective-permute-start | bytes 589832 | tf_op jit(solution)/shard_map/ppermute | solution.py:276
  18.1 2.5 %collective-permute-start.7 = (bf16[24,2560]{1,0:T(8,128)(2,1)S(1)}, bf16[24,2560]{1,0:T(8,128)(2,1)S(1)}, u32[]{:S(2)}, u32[]{:S(2)}) collective-permute-start(bf16[24,2560]{1,0:T(8,128)(2,1)S(1)} %slice.16), channel_id=1, source_target_pairs={{0,8},{4,12},{8,28},{12,24},{28,20},{24,16},{20,0},{16,4},{1,9},{5... | collective-permute-start | bytes 368648 | tf_op jit(solution)/shard_map/ppermute | solution.py:276
  20.6 0.4 %collective-permute-start.8 = (bf16[24,1536]{1,0:T(8,128)(2,1)S(1)}, bf16[24,1536]{1,0:T(8,128)(2,1)S(1)}, u32[]{:S(2)}, u32[]{:S(2)}) collective-permute-start(bf16[24,1536]{1,0:T(8,128)(2,1)S(1)} %slice.17), channel_id=1, source_target_pairs={{0,20},{4,16},{8,0},{12,4},{28,8},{24,12},{20,28},{16,24},{1,21},{... | collective-permute-start | bytes 221192 | tf_op jit(solution)/shard_map/ppermute | solution.py:276
  21.1 1.5 %score.4 = (f32[120,256]{1,0:T(8,128)S(1)}, bf16[120,256]{1,0:T(8,128)(2,1)S(1)}) custom-call(bf16[24,4096]{1,0:T(8,128)(2,1)S(1)} %rotate.1.after_ref.refs_0_, bf16[24,4096]{1,0:T(8,128)(2,1)S(1)} %collective-permute-done.refs_1_, bf16[24,4096]{1,0:T(8,128)(2,1)S(1)} %collective-permute-done.1.refs_2_, bf16[24,4096]{1,0:T(8,128)(2,1)S(1)} %collective-permute-done.2.refs_3_, ...), custom_call_target="tpu_custom_call" | custom-call | flops 1073741824 | bytes 1048576 | tf_op jit(solution)/shard_map/score/pallas_call | solution.py:209
  22.6 1.5 %collective-permute-start.4 = (bf16[120,256]{1,0:T(8,128)(2,1)S(1)}, bf16[120,256]{1,0:T(8,128)(2,1)S(1)}, u32[]{:S(2)}, u32[]{:S(2)}) collective-permute-start(bf16[120,256]{1,0:T(8,128)(2,1)S(1)} %get-tuple-element.19), channel_id=1, source_target_pairs={{0,2},{2,0},{1,3},{3,1},{4,6},{6,4},{5,7},{7,5},{8,10},{10,8},{9,1... | collective-permute-start | bytes 184328 | tf_op jit(solution)/shard_map/ppermute | solution.py:226
  24.0 0.0 collective-permute-done.5.refs_0_
  24.0 0.0 collective-permute-done.6.refs_1_
  24.0 0.5 %score.5 = bf16[48,256]{1,0:T(8,128)(2,1)S(1)} custom-call(bf16[24,4096]{1,0:T(8,128)(2,1)S(1)} %collective-permute-done.5.refs_0_, bf16[24,4096]{1,0:T(8,128)(2,1)S(1)} %collective-permute-done.6.refs_1_, bf16[1,4096,256]{2,1,0:T(8,128)(2,1)S(1)} %get-tuple-element.20.refs_2_), custom_call_target="tpu_custom_call" | custom-call | flops 536870912 | bytes 1048576 | tf_op jit(solution)/shard_map/score/pallas_call | solution.py:209
  24.5 1.5 %collective-permute-start.9 = (bf16[48,256]{1,0:T(8,128)(2,1)S(1)}, bf16[48,256]{1,0:T(8,128)(2,1)S(1)}, u32[]{:S(2)}, u32[]{:S(2)}) collective-permute-start(bf16[48,256]{1,0:T(8,128)(2,1)S(1)} %score.5), channel_id=1, source_target_pairs={{0,2},{2,0},{1,3},{3,1},{4,6},{6,4},{5,7},{7,5},{8,10},{10,8},{9,1... | collective-permute-start | bytes 73736 | tf_op jit(solution)/shard_map/ppermute | solution.py:226
  26.0 0.0 collective-permute-done.8.refs_3_.refs_1_
  26.0 0.2 collective-permute-done.7.refs_2_.refs_0_
  26.3 0.5 %score.7 = bf16[24,256]{1,0:T(8,128)(2,1)S(1)} custom-call(bf16[24,2560]{1,0:T(8,128)(2,1)S(1)} %collective-permute-done.7.refs_2_.refs_0_, bf16[24,1536]{1,0:T(8,128)(2,1)S(1)} %collective-permute-done.8.refs_3_.refs_1_, bf16[1,4096,256]{2,1,0:T(8,128)(2,1)S(1)} %get-tuple-element.20.refs_2_), custom_call_target="tpu_custom_call" | custom-call | flops 536870912 | bytes 1048576 | tf_op jit(solution)/shard_map/score/pallas_call | solution.py:209
  26.7 1.5 %collective-permute-start.10 = (bf16[24,256]{1,0:T(8,128)(2,1)S(1)}, bf16[24,256]{1,0:T(8,128)(2,1)S(1)}, u32[]{:S(2)}, u32[]{:S(2)}) collective-permute-start(bf16[24,256]{1,0:T(8,128)(2,1)S(1)} %score.7), channel_id=1, source_target_pairs={{0,2},{2,0},{1,3},{3,1},{4,6},{6,4},{5,7},{7,5},{8,10},{10,8},{9,1... | collective-permute-start | bytes 36872 | tf_op jit(solution)/shard_map/ppermute | solution.py:226
  28.2 0.8 %score.6 = f32[72,256]{1,0:T(8,128)S(1)} custom-call(bf16[24,4096]{1,0:T(8,128)(2,1)S(1)} %collective-permute-done.5.refs_0_, bf16[24,4096]{1,0:T(8,128)(2,1)S(1)} %collective-permute-done.6.refs_1_, bf16[24,2560]{1,0:T(8,128)(2,1)S(1)} %collective-permute-done.7.refs_2_.refs_0_, bf16[24,1536]{1,0:T(8,128)(2,1)S(1)} %collective-permute-done.8.refs_3_.refs_1_, ...), custom_call_target="tpu_custom_call" | custom-call | flops 536870912 | bytes 1048576 | tf_op jit(solution)/shard_map/score/pallas_call | solution.py:209
  29.0 0.0 collective-permute-done.4.refs_1_
  29.0 1.4 %collective-permute-done.10.refs_5_ = bf16[24,256]{1,0:T(8,128)(2,1)S(1)} collective-permute-done((bf16[24,256]{1,0:T(8,128)(2,1)S(1)}, bf16[24,256]{1,0:T(8,128)(2,1)S(1)}, u32[]{:S(2)}, u32[]{:S(2)}) %collective-permute-start.10) | collective-permute-done | bytes 12320 | tf_op jit(solution)/shard_map/ppermute | solution.py:226
  30.4 0.0 collective-permute-done.9.refs_3_
  30.4 0.7 %finish.1 = f32[192,256]{1,0:T(8,128)} custom-call(f32[120,256]{1,0:T(8,128)S(1)} %get-tuple-element.18.refs_0_, bf16[120,256]{1,0:T(8,128)(2,1)S(1)} %collective-permute-done.4.refs_1_, f32[48,256]{1,0:T(8,128)S(1)} %slice.18.refs_2_, bf16[48,256]{1,0:T(8,128)(2,1)S(1)} %collective-permute-done.9.refs_3_, f32[24,256]{1,0:T(8,128)S(1)} %slice.19.refs_4_, ...), custom_call_target="tpu_custom_call" | custom-call | tf_op jit(solution)/shard_map/finish/pallas_call | solution.py:259
  (4 shorter events, 0.0 us)
Async XLA Ops:
  2.0 7.9 %collective-permute-start = (bf16[24,4096]{1,0:T(8,128)(2,1)S(1)}, bf16[24,4096]{1,0:T(8,128)(2,1)S(1)}, u32[]{:S(2)}, u32[]{:S(2)}) collective-permute-start(bf16[24,4096]{1,0:T(8,128)(2,1)S(1)} %rotate.1.after_ref.refs_0_), channel_id=1, source_target_pairs={{0,4},{4,8},{8,12},{12,28},{28,24},{24,20},{20,16},{16,0},{1,5},{5... | collective-permute-start | bytes 589832 | tf_op jit(solution)/shard_map/ppermute | solution.py:276
  5.1 6.6 %collective-permute-start.1 = (bf16[24,4096]{1,0:T(8,128)(2,1)S(1)}, bf16[24,4096]{1,0:T(8,128)(2,1)S(1)}, u32[]{:S(2)}, u32[]{:S(2)}) collective-permute-start(bf16[24,4096]{1,0:T(8,128)(2,1)S(1)} %rotate.1.after_ref.refs_0_), channel_id=1, source_target_pairs={{0,16},{4,0},{8,4},{12,8},{28,12},{24,28},{20,24},{16,20},{1,17},{... | collective-permute-start | bytes 589832 | tf_op jit(solution)/shard_map/ppermute | solution.py:276
  9.9 6.1 %collective-permute-start.2 = (bf16[24,4096]{1,0:T(8,128)(2,1)S(1)}, bf16[24,4096]{1,0:T(8,128)(2,1)S(1)}, u32[]{:S(2)}, u32[]{:S(2)}) collective-permute-start(bf16[24,4096]{1,0:T(8,128)(2,1)S(1)} %collective-permute-done.refs_1_), channel_id=1, source_target_pairs={{0,4},{4,8},{8,12},{12,28},{28,24},{24,20},{20,16},{16,0},{1,5},{5... | collective-permute-start | bytes 589832 | tf_op jit(solution)/shard_map/ppermute | solution.py:276
  11.7 5.8 %collective-permute-start.3 = (bf16[24,4096]{1,0:T(8,128)(2,1)S(1)}, bf16[24,4096]{1,0:T(8,128)(2,1)S(1)}, u32[]{:S(2)}, u32[]{:S(2)}) collective-permute-start(bf16[24,4096]{1,0:T(8,128)(2,1)S(1)} %collective-permute-done.1.refs_2_), channel_id=1, source_target_pairs={{0,16},{4,0},{8,4},{12,8},{28,12},{24,28},{20,24},{16,20},{1,17},{... | collective-permute-start | bytes 589832 | tf_op jit(solution)/shard_map/ppermute | solution.py:276
  16.0 8.0 %collective-permute-start.5 = (bf16[24,4096]{1,0:T(8,128)(2,1)S(1)}, bf16[24,4096]{1,0:T(8,128)(2,1)S(1)}, u32[]{:S(2)}, u32[]{:S(2)}) collective-permute-start(bf16[24,4096]{1,0:T(8,128)(2,1)S(1)} %collective-permute-done.2.refs_3_), channel_id=1, source_target_pairs={{0,4},{4,8},{8,12},{12,28},{28,24},{24,20},{20,16},{16,0},{1,5},{5... | collective-permute-start | bytes 589832 | tf_op jit(solution)/shard_map/ppermute | solution.py:276
  17.5 6.5 %collective-permute-start.6 = (bf16[24,4096]{1,0:T(8,128)(2,1)S(1)}, bf16[24,4096]{1,0:T(8,128)(2,1)S(1)}, u32[]{:S(2)}, u32[]{:S(2)}) collective-permute-start(bf16[24,4096]{1,0:T(8,128)(2,1)S(1)} %collective-permute-done.3.refs_4_), channel_id=1, source_target_pairs={{0,16},{4,0},{8,4},{12,8},{28,12},{24,28},{20,24},{16,20},{1,17},{... | collective-permute-start | bytes 589832 | tf_op jit(solution)/shard_map/ppermute | solution.py:276
  18.1 8.2 %collective-permute-start.7 = (bf16[24,2560]{1,0:T(8,128)(2,1)S(1)}, bf16[24,2560]{1,0:T(8,128)(2,1)S(1)}, u32[]{:S(2)}, u32[]{:S(2)}) collective-permute-start(bf16[24,2560]{1,0:T(8,128)(2,1)S(1)} %slice.16), channel_id=1, source_target_pairs={{0,8},{4,12},{8,28},{12,24},{28,20},{24,16},{20,0},{16,4},{1,9},{5... | collective-permute-start | bytes 368648 | tf_op jit(solution)/shard_map/ppermute | solution.py:276
  20.6 5.4 %collective-permute-start.8 = (bf16[24,1536]{1,0:T(8,128)(2,1)S(1)}, bf16[24,1536]{1,0:T(8,128)(2,1)S(1)}, u32[]{:S(2)}, u32[]{:S(2)}) collective-permute-start(bf16[24,1536]{1,0:T(8,128)(2,1)S(1)} %slice.17), channel_id=1, source_target_pairs={{0,20},{4,16},{8,0},{12,4},{28,8},{24,12},{20,28},{16,24},{1,21},{... | collective-permute-start | bytes 221192 | tf_op jit(solution)/shard_map/ppermute | solution.py:276
  22.6 6.5 %collective-permute-start.4 = (bf16[120,256]{1,0:T(8,128)(2,1)S(1)}, bf16[120,256]{1,0:T(8,128)(2,1)S(1)}, u32[]{:S(2)}, u32[]{:S(2)}) collective-permute-start(bf16[120,256]{1,0:T(8,128)(2,1)S(1)} %get-tuple-element.19), channel_id=1, source_target_pairs={{0,2},{2,0},{1,3},{3,1},{4,6},{6,4},{5,7},{7,5},{8,10},{10,8},{9,1... | collective-permute-start | bytes 184328 | tf_op jit(solution)/shard_map/ppermute | solution.py:226
  24.5 5.9 %collective-permute-start.9 = (bf16[48,256]{1,0:T(8,128)(2,1)S(1)}, bf16[48,256]{1,0:T(8,128)(2,1)S(1)}, u32[]{:S(2)}, u32[]{:S(2)}) collective-permute-start(bf16[48,256]{1,0:T(8,128)(2,1)S(1)} %score.5), channel_id=1, source_target_pairs={{0,2},{2,0},{1,3},{3,1},{4,6},{6,4},{5,7},{7,5},{8,10},{10,8},{9,1... | collective-permute-start | bytes 73736 | tf_op jit(solution)/shard_map/ppermute | solution.py:226
  26.7 3.7 %collective-permute-start.10 = (bf16[24,256]{1,0:T(8,128)(2,1)S(1)}, bf16[24,256]{1,0:T(8,128)(2,1)S(1)}, u32[]{:S(2)}, u32[]{:S(2)}) collective-permute-start(bf16[24,256]{1,0:T(8,128)(2,1)S(1)} %score.7), channel_id=1, source_target_pairs={{0,2},{2,0},{1,3},{3,1},{4,6},{6,4},{5,7},{7,5},{8,10},{10,8},{9,1... | collective-permute-start | bytes 36872 | tf_op jit(solution)/shard_map/ppermute | solution.py:226

commit v8 on v7

--- a/solution.py
+++ b/solution.py
@@ -66,6 +66,7 @@
     in_wide = jnp.concatenate([in_ref[model_layer].astype(F32)] * 4, axis=1)
     in_tall = jnp.concatenate([in_wide] * 4, axis=0)
     in_diag = jnp.where(row == col, in_tall, F32(0.0)).astype(BF16)
+    in_diag_t = jnp.where(row == col, in_tall.T, F32(0.0)).astype(BF16)
     eigen = jnp.concatenate([eigen_ref[model_layer]] * 4, axis=1)
 
     quads = range(half // 4)
@@ -101,8 +102,8 @@
         jnp.dot(out_twice, jnp.concatenate(split(block), axis=0), preferred_element_type=F32) for block in scaled
     ]
     hi, lo = split(jnp.concatenate(turned, axis=0))
-    result = lax.dot_general(hi, in_diag, NT, preferred_element_type=F32)
-    result = result + lax.dot_general(lo, in_diag, NT, preferred_element_type=F32)
+    result = jnp.dot(hi, in_diag_t, preferred_element_type=F32)
+    result = result + jnp.dot(lo, in_diag_t, preferred_element_type=F32)
     for quad in quads:
         for two in range(2):
             at = quad * 4 + two * 2
@@ -280,7 +281,7 @@
     half, dim = own.shape
     others = range(1, lax.axis_size("lay"))
     one = two = own
-    batch, sums, hidden = [own], [], [store, turned]
+    batch, sums = [own], []
     for step in range(1, members):
         if step == members - 1:
             cut = dim // 8 * 5 // 128 * 128
@@ -288,18 +289,16 @@
         one, two = hop(one, 1), hop(two, -1)
         if step == members - 1:
             parts = [hop(parts[0], 2), hop(parts[1], -2)]
-        if step < members - 1:
-            one, hidden = lax.optimization_barrier((one, hidden))
         if step == 1:
-            store, turned = hidden
-        elif hidden:
-            keep, *sends = hidden
-            sums.append((keep, swap_layers(sends)))
-        hidden = []
+            one, store, turned = lax.optimization_barrier((one, store, turned))
+        elif len(batch) >= 7:
+            keep, *sends = score(batch, [], store, [0, *others])
+            got = swap_layers(sends)
+            if step < members - 1:
+                one, _ = lax.optimization_barrier((one, sends))
+            sums.append((keep, got))
+            batch = []
         batch += [one, two]
-        if len(batch) >= 5 and step < members - 1:
-            hidden = score(batch, [], store, [0, *others])
-            batch = []
     sends = score(batch, [], turned, others, True)
     near = swap_layers(sends)
     parts, _ = lax.optimization_barrier((parts, sends))

time: 31.3 us -> 31.3 us (level)
  waiting for transfers between devices: 7.75 us -> 10.5 us
  Pallas kernels: 8.75 us -> 7.35 us
  starting transfers between devices: 14.6 us -> 13.2 us
    ppermute x8, waiting for transfers between devices: 6.34 us -> 9.09 us  [hop(): lax.ppermute(piece, RING, [(a, ring[(i + steps) % len(ring)]) for i, a in...]
    ppermute x3 -> x2, starting transfers between devices: 4.45 us -> 3.06 us  [swap_layers(): lax.ppermute(send, 'lay', [(i, (i + k + 1) % shares) for i in range(share...]
    pallas_call x4 -> x3, Pallas kernels: 3.23 us -> 1.86 us  [score(): pl.pallas_call(functools.partial(score_kernel, len(pieces), height, share...]
    ppermute x3 -> x2, waiting for transfers between devices: 1.41 us -> 1.4 us  [swap_layers(): lax.ppermute(send, 'lay', [(i, (i + k + 1) % shares) for i in range(share...]
  transfers between devices with their start and end apart: 11 -> 10, of which waited for: 4 -> 6; matrix products, arithmetic and copies ran while one was open for 0% -> 0% of each run, Pallas kernels for 19% -> 15%
where the time goes in v8:
time: 31.3 us; the launch traced here: 31.1 us
  starting transfers between devices  13.2 us (42%)
  waiting for transfers between devices  10.5 us (34%)
  Pallas kernels  7.35 us (23%)
    ppermute x8, starting transfers between devices, hop(): lax.ppermute(piece, RING, [(a, ring[(i + steps) % len(ring)]) for i, a in...  10.1 us
    ppermute x8, waiting for transfers between devices, hop(): lax.ppermute(piece, RING, [(a, ring[(i + steps) % len(ring)]) for i, a in...  9.09 us
    ppermute x2, starting transfers between devices, swap_layers(): lax.ppermute(send, 'lay', [(i, (i + k + 1) % shares) for i in range(share...  3.06 us
    pallas_call x1, Pallas kernels, fetch(): pl.pallas_call(functools.partial(fetch_kernel, shares), out_shape=[jax.Sh...  2.8 us
    pallas_call x1, Pallas kernels, rotate(): pl.pallas_call(functools.partial(rotate_kernel, half, 1), out_shape=jax.S...  1.99 us
    pallas_call x3, Pallas kernels, score(): pl.pallas_call(functools.partial(score_kernel, len(pieces), height, share...  1.86 us
    ppermute x2, waiting for transfers between devices, swap_layers(): lax.ppermute(send, 'lay', [(i, (i + k + 1) % shares) for i in range(share...  1.4 us
    pallas_call x1, Pallas kernels, finish(): pl.pallas_call(functools.partial(finish_kernel, half, members, sizes), ou...  0.71 us
  transfers between devices with their start and end apart: 10, of which 6 were waited for; matrix products, arithmetic and copies ran while one was open for 0% of the time, Pallas kernels for 15%

profile of v8, /device:TPU:0, one launch (start us, length us, event | category | flops | bytes accessed | tf_op | source)
XLA Modules:
  0.0 31.1 jit_solution(16909377893409754699)
XLA Ops:
  0.0 2.0 %rotate.1.after_ref.refs_0_ = bf16[24,4096]{1,0:T(8,128)(2,1)S(1)} custom-call(bf16[1,48,4096]{2,1,0:T(8,128)(2,1)} %query_hbm.1, s32[384]{0:T(512)} %block_hbm.1, f32[4]{0:T(128)} %damping_hbm.1, s32[2]{0:T(128)} %slot_hbm.1, bf16[2,64,64]{2,1,0:T(8,128)(2,1)} %out_hbm.1, bf16[2,64,64]{2,1,0:T(8,128)(2,1)} %in_hbm.1, f32[2,64,64]{2,1,0:T(8,128)} %eigen_hbm.1), custom_call_target="tpu_custom_call" | custom-call | flops 201326592 | bytes 1048576 | tf_op jit(solution)/shard_map/rotate/pallas_call | solution.py:124
  2.0 3.1 %collective-permute-start = (bf16[24,4096]{1,0:T(8,128)(2,1)S(1)}, bf16[24,4096]{1,0:T(8,128)(2,1)S(1)}, u32[]{:S(2)}, u32[]{:S(2)}) collective-permute-start(bf16[24,4096]{1,0:T(8,128)(2,1)S(1)} %rotate.1.after_ref.refs_0_), channel_id=1, source_target_pairs={{0,4},{4,8},{8,12},{12,28},{28,24},{24,20},{20,16},{16,0},{1,5},{5... | collective-permute-start | bytes 589832 | tf_op jit(solution)/shard_map/ppermute | solution.py:277
  5.1 0.0 collective-permute-start.1
  5.1 2.8 %fetch.1 = (bf16[1,512,4096]{2,1,0:T(8,128)(2,1)S(1)}, bf16[1,4096,256]{2,1,0:T(8,128)(2,1)S(1)}) custom-call(bf16[24,4096]{1,0:T(8,128)(2,1)S(1)} %rotate.1.after_ref.refs_0_, bf16[1,512,4096]{2,1,0:T(8,128)(2,1)} %store_hbm.1), custom_call_target="tpu_custom_call" | custom-call | bytes 8388608 | tf_op jit(solution)/shard_map/fetch/pallas_call | solution.py:166
  7.9 2.0 %collective-permute-done.refs_1_ = bf16[24,4096]{1,0:T(8,128)(2,1)S(1)} collective-permute-done((bf16[24,4096]{1,0:T(8,128)(2,1)S(1)}, bf16[24,4096]{1,0:T(8,128)(2,1)S(1)}, u32[]{:S(2)}, u32[]{:S(2)}) %collective-permute-start) | collective-permute-done | bytes 196640 | tf_op jit(solution)/shard_map/ppermute | solution.py:277
  9.9 1.8 %collective-permute-start.2 = (bf16[24,4096]{1,0:T(8,128)(2,1)S(1)}, bf16[24,4096]{1,0:T(8,128)(2,1)S(1)}, u32[]{:S(2)}, u32[]{:S(2)}) collective-permute-start(bf16[24,4096]{1,0:T(8,128)(2,1)S(1)} %collective-permute-done.refs_1_), channel_id=1, source_target_pairs={{0,4},{4,8},{8,12},{12,28},{28,24},{24,20},{20,16},{16,0},{1,5},{5... | collective-permute-start | bytes 589832 | tf_op jit(solution)/shard_map/ppermute | solution.py:277
  11.7 0.0 collective-permute-done.1.refs_2_
  11.7 0.2 collective-permute-start.3
  11.9 4.1 %collective-permute-done.2.refs_3_ = bf16[24,4096]{1,0:T(8,128)(2,1)S(1)} collective-permute-done((bf16[24,4096]{1,0:T(8,128)(2,1)S(1)}, bf16[24,4096]{1,0:T(8,128)(2,1)S(1)}, u32[]{:S(2)}, u32[]{:S(2)}) %collective-permute-start.2) | collective-permute-done | bytes 196640 | tf_op jit(solution)/shard_map/ppermute | solution.py:277
  16.0 1.5 %collective-permute-start.4 = (bf16[24,4096]{1,0:T(8,128)(2,1)S(1)}, bf16[24,4096]{1,0:T(8,128)(2,1)S(1)}, u32[]{:S(2)}, u32[]{:S(2)}) collective-permute-start(bf16[24,4096]{1,0:T(8,128)(2,1)S(1)} %collective-permute-done.2.refs_3_), channel_id=1, source_target_pairs={{0,4},{4,8},{8,12},{12,28},{28,24},{24,20},{20,16},{16,0},{1,5},{5... | collective-permute-start | bytes 589832 | tf_op jit(solution)/shard_map/ppermute | solution.py:277
  17.5 0.0 collective-permute-done.3.refs_4_
  17.5 0.5 %collective-permute-start.5 = (bf16[24,4096]{1,0:T(8,128)(2,1)S(1)}, bf16[24,4096]{1,0:T(8,128)(2,1)S(1)}, u32[]{:S(2)}, u32[]{:S(2)}) collective-permute-start(bf16[24,4096]{1,0:T(8,128)(2,1)S(1)} %collective-permute-done.3.refs_4_), channel_id=1, source_target_pairs={{0,16},{4,0},{8,4},{12,8},{28,12},{24,28},{20,24},{16,20},{1,17},{... | collective-permute-start | bytes 589832 | tf_op jit(solution)/shard_map/ppermute | solution.py:277
  18.0 2.6 %collective-permute-start.6 = (bf16[24,2560]{1,0:T(8,128)(2,1)S(1)}, bf16[24,2560]{1,0:T(8,128)(2,1)S(1)}, u32[]{:S(2)}, u32[]{:S(2)}) collective-permute-start(bf16[24,2560]{1,0:T(8,128)(2,1)S(1)} %slice.16), channel_id=1, source_target_pairs={{0,8},{4,12},{8,28},{12,24},{28,20},{24,16},{20,0},{16,4},{1,9},{5... | collective-permute-start | bytes 368648 | tf_op jit(solution)/shard_map/ppermute | solution.py:277
  20.6 0.4 %collective-permute-start.7 = (bf16[24,1536]{1,0:T(8,128)(2,1)S(1)}, bf16[24,1536]{1,0:T(8,128)(2,1)S(1)}, u32[]{:S(2)}, u32[]{:S(2)}) collective-permute-start(bf16[24,1536]{1,0:T(8,128)(2,1)S(1)} %slice.17), channel_id=1, source_target_pairs={{0,20},{4,16},{8,0},{12,4},{28,8},{24,12},{20,28},{16,24},{1,21},{... | collective-permute-start | bytes 221192 | tf_op jit(solution)/shard_map/ppermute | solution.py:277
  21.0 2.0 %collective-permute-done.4.refs_5_ = bf16[24,4096]{1,0:T(8,128)(2,1)S(1)} collective-permute-done((bf16[24,4096]{1,0:T(8,128)(2,1)S(1)}, bf16[24,4096]{1,0:T(8,128)(2,1)S(1)}, u32[]{:S(2)}, u32[]{:S(2)}) %collective-permute-start.4) | collective-permute-done | bytes 196640 | tf_op jit(solution)/shard_map/ppermute | solution.py:277
  23.0 1.0 %collective-permute-done.5.refs_6_ = bf16[24,4096]{1,0:T(8,128)(2,1)S(1)} collective-permute-done((bf16[24,4096]{1,0:T(8,128)(2,1)S(1)}, bf16[24,4096]{1,0:T(8,128)(2,1)S(1)}, u32[]{:S(2)}, u32[]{:S(2)}) %collective-permute-start.5) | collective-permute-done | bytes 196640 | tf_op jit(solution)/shard_map/ppermute | solution.py:277
  24.0 0.6 %score.3 = bf16[168,256]{1,0:T(8,128)(2,1)S(1)} custom-call(bf16[24,4096]{1,0:T(8,128)(2,1)S(1)} %rotate.1.after_ref.refs_0_, bf16[24,4096]{1,0:T(8,128)(2,1)S(1)} %collective-permute-done.refs_1_, bf16[24,4096]{1,0:T(8,128)(2,1)S(1)} %collective-permute-done.1.refs_2_, bf16[24,4096]{1,0:T(8,128)(2,1)S(1)} %collective-permute-done.2.refs_3_, ...), custom_call_target="tpu_custom_call" | custom-call | flops 536870912 | bytes 1048576 | tf_op jit(solution)/shard_map/score/pallas_call | solution.py:210
  24.6 1.5 %collective-permute-start.8 = (bf16[168,256]{1,0:T(8,128)(2,1)S(1)}, bf16[168,256]{1,0:T(8,128)(2,1)S(1)}, u32[]{:S(2)}, u32[]{:S(2)}) collective-permute-start(bf16[168,256]{1,0:T(8,128)(2,1)S(1)} %score.3), channel_id=1, source_target_pairs={{0,2},{2,0},{1,3},{3,1},{4,6},{6,4},{5,7},{7,5},{8,10},{10,8},{9,1... | collective-permute-start | bytes 258056 | tf_op jit(solution)/shard_map/ppermute | solution.py:227
  26.2 0.0 collective-permute-done.7.refs_8_.refs_1_
  26.2 0.1 collective-permute-done.6.refs_7_.refs_0_
  26.2 0.5 %score.5 = bf16[24,256]{1,0:T(8,128)(2,1)S(1)} custom-call(bf16[24,2560]{1,0:T(8,128)(2,1)S(1)} %collective-permute-done.6.refs_7_.refs_0_, bf16[24,1536]{1,0:T(8,128)(2,1)S(1)} %collective-permute-done.7.refs_8_.refs_1_, bf16[1,4096,256]{2,1,0:T(8,128)(2,1)S(1)} %get-tuple-element.15.refs_7_.refs_2_), custom_call_target="tpu_custom_call" | custom-call | flops 536870912 | bytes 1048576 | tf_op jit(solution)/shard_map/score/pallas_call | solution.py:210
  26.7 1.5 %collective-permute-start.9 = (bf16[24,256]{1,0:T(8,128)(2,1)S(1)}, bf16[24,256]{1,0:T(8,128)(2,1)S(1)}, u32[]{:S(2)}, u32[]{:S(2)}) collective-permute-start(bf16[24,256]{1,0:T(8,128)(2,1)S(1)} %score.5), channel_id=1, source_target_pairs={{0,2},{2,0},{1,3},{3,1},{4,6},{6,4},{5,7},{7,5},{8,10},{10,8},{9,1... | collective-permute-start | bytes 36872 | tf_op jit(solution)/shard_map/ppermute | solution.py:227
  28.2 0.7 %score.4 = f32[192,256]{1,0:T(8,128)S(1)} custom-call(bf16[24,4096]{1,0:T(8,128)(2,1)S(1)} %rotate.1.after_ref.refs_0_, bf16[24,4096]{1,0:T(8,128)(2,1)S(1)} %collective-permute-done.refs_1_, bf16[24,4096]{1,0:T(8,128)(2,1)S(1)} %collective-permute-done.1.refs_2_, bf16[24,4096]{1,0:T(8,128)(2,1)S(1)} %collective-permute-done.2.refs_3_, ...), custom_call_target="tpu_custom_call" | custom-call | flops 536870912 | bytes 1048576 | tf_op jit(solution)/shard_map/score/pallas_call | solution.py:210
  29.0 1.4 %collective-permute-done.9.refs_3_ = bf16[24,256]{1,0:T(8,128)(2,1)S(1)} collective-permute-done((bf16[24,256]{1,0:T(8,128)(2,1)S(1)}, bf16[24,256]{1,0:T(8,128)(2,1)S(1)}, u32[]{:S(2)}, u32[]{:S(2)}) %collective-permute-start.9) | collective-permute-done | bytes 12320 | tf_op jit(solution)/shard_map/ppermute | solution.py:227
  30.4 0.0 collective-permute-done.8.refs_1_
  30.4 0.7 %finish.1 = f32[192,256]{1,0:T(8,128)} custom-call(f32[168,256]{1,0:T(8,128)S(1)} %slice.18.refs_0_, bf16[168,256]{1,0:T(8,128)(2,1)S(1)} %collective-permute-done.8.refs_1_, f32[24,256]{1,0:T(8,128)S(1)} %slice.19.refs_2_, bf16[24,256]{1,0:T(8,128)(2,1)S(1)} %collective-permute-done.9.refs_3_), custom_call_target="tpu_custom_call" | custom-call | tf_op jit(solution)/shard_map/finish/pallas_call | solution.py:260
  (4 shorter events, 0.0 us)
Async XLA Ops:
  2.0 7.9 %collective-permute-start = (bf16[24,4096]{1,0:T(8,128)(2,1)S(1)}, bf16[24,4096]{1,0:T(8,128)(2,1)S(1)}, u32[]{:S(2)}, u32[]{:S(2)}) collective-permute-start(bf16[24,4096]{1,0:T(8,128)(2,1)S(1)} %rotate.1.after_ref.refs_0_), channel_id=1, source_target_pairs={{0,4},{4,8},{8,12},{12,28},{28,24},{24,20},{20,16},{16,0},{1,5},{5... | collective-permute-start | bytes 589832 | tf_op jit(solution)/shard_map/ppermute | solution.py:277
  5.1 6.6 %collective-permute-start.1 = (bf16[24,4096]{1,0:T(8,128)(2,1)S(1)}, bf16[24,4096]{1,0:T(8,128)(2,1)S(1)}, u32[]{:S(2)}, u32[]{:S(2)}) collective-permute-start(bf16[24,4096]{1,0:T(8,128)(2,1)S(1)} %rotate.1.after_ref.refs_0_), channel_id=1, source_target_pairs={{0,16},{4,0},{8,4},{12,8},{28,12},{24,28},{20,24},{16,20},{1,17},{... | collective-permute-start | bytes 589832 | tf_op jit(solution)/shard_map/ppermute | solution.py:277
  9.9 6.1 %collective-permute-start.2 = (bf16[24,4096]{1,0:T(8,128)(2,1)S(1)}, bf16[24,4096]{1,0:T(8,128)(2,1)S(1)}, u32[]{:S(2)}, u32[]{:S(2)}) collective-permute-start(bf16[24,4096]{1,0:T(8,128)(2,1)S(1)} %collective-permute-done.refs_1_), channel_id=1, source_target_pairs={{0,4},{4,8},{8,12},{12,28},{28,24},{24,20},{20,16},{16,0},{1,5},{5... | collective-permute-start | bytes 589832 | tf_op jit(solution)/shard_map/ppermute | solution.py:277
  11.7 5.8 %collective-permute-start.3 = (bf16[24,4096]{1,0:T(8,128)(2,1)S(1)}, bf16[24,4096]{1,0:T(8,128)(2,1)S(1)}, u32[]{:S(2)}, u32[]{:S(2)}) collective-permute-start(bf16[24,4096]{1,0:T(8,128)(2,1)S(1)} %collective-permute-done.1.refs_2_), channel_id=1, source_target_pairs={{0,16},{4,0},{8,4},{12,8},{28,12},{24,28},{20,24},{16,20},{1,17},{... | collective-permute-start | bytes 589832 | tf_op jit(solution)/shard_map/ppermute | solution.py:277
  16.0 7.0 %collective-permute-start.4 = (bf16[24,4096]{1,0:T(8,128)(2,1)S(1)}, bf16[24,4096]{1,0:T(8,128)(2,1)S(1)}, u32[]{:S(2)}, u32[]{:S(2)}) collective-permute-start(bf16[24,4096]{1,0:T(8,128)(2,1)S(1)} %collective-permute-done.2.refs_3_), channel_id=1, source_target_pairs={{0,4},{4,8},{8,12},{12,28},{28,24},{24,20},{20,16},{16,0},{1,5},{5... | collective-permute-start | bytes 589832 | tf_op jit(solution)/shard_map/ppermute | solution.py:277
  17.5 6.5 %collective-permute-start.5 = (bf16[24,4096]{1,0:T(8,128)(2,1)S(1)}, bf16[24,4096]{1,0:T(8,128)(2,1)S(1)}, u32[]{:S(2)}, u32[]{:S(2)}) collective-permute-start(bf16[24,4096]{1,0:T(8,128)(2,1)S(1)} %collective-permute-done.3.refs_4_), channel_id=1, source_target_pairs={{0,16},{4,0},{8,4},{12,8},{28,12},{24,28},{20,24},{16,20},{1,17},{... | collective-permute-start | bytes 589832 | tf_op jit(solution)/shard_map/ppermute | solution.py:277
  18.0 8.2 %collective-permute-start.6 = (bf16[24,2560]{1,0:T(8,128)(2,1)S(1)}, bf16[24,2560]{1,0:T(8,128)(2,1)S(1)}, u32[]{:S(2)}, u32[]{:S(2)}) collective-permute-start(bf16[24,2560]{1,0:T(8,128)(2,1)S(1)} %slice.16), channel_id=1, source_target_pairs={{0,8},{4,12},{8,28},{12,24},{28,20},{24,16},{20,0},{16,4},{1,9},{5... | collective-permute-start | bytes 368648 | tf_op jit(solution)/shard_map/ppermute | solution.py:277
  20.6 5.6 %collective-permute-start.7 = (bf16[24,1536]{1,0:T(8,128)(2,1)S(1)}, bf16[24,1536]{1,0:T(8,128)(2,1)S(1)}, u32[]{:S(2)}, u32[]{:S(2)}) collective-permute-start(bf16[24,1536]{1,0:T(8,128)(2,1)S(1)} %slice.17), channel_id=1, source_target_pairs={{0,20},{4,16},{8,0},{12,4},{28,8},{24,12},{20,28},{16,24},{1,21},{... | collective-permute-start | bytes 221192 | tf_op jit(solution)/shard_map/ppermute | solution.py:277
  24.6 5.8 %collective-permute-start.8 = (bf16[168,256]{1,0:T(8,128)(2,1)S(1)}, bf16[168,256]{1,0:T(8,128)(2,1)S(1)}, u32[]{:S(2)}, u32[]{:S(2)}) collective-permute-start(bf16[168,256]{1,0:T(8,128)(2,1)S(1)} %score.3), channel_id=1, source_target_pairs={{0,2},{2,0},{1,3},{3,1},{4,6},{6,4},{5,7},{7,5},{8,10},{10,8},{9,1... | collective-permute-start | bytes 258056 | tf_op jit(solution)/shard_map/ppermute | solution.py:227
  26.7 3.7 %collective-permute-start.9 = (bf16[24,256]{1,0:T(8,128)(2,1)S(1)}, bf16[24,256]{1,0:T(8,128)(2,1)S(1)}, u32[]{:S(2)}, u32[]{:S(2)}) collective-permute-start(bf16[24,256]{1,0:T(8,128)(2,1)S(1)} %score.5), channel_id=1, source_target_pairs={{0,2},{2,0},{1,3},{3,1},{4,6},{6,4},{5,7},{7,5},{8,10},{10,8},{9,1... | collective-permute-start | bytes 36872 | tf_op jit(solution)/shard_map/ppermute | solution.py:227

commit v9 on v8

--- a/solution.py
+++ b/solution.py
@@ -229,14 +229,12 @@
     ]
 
 
-def finish_kernel(half, members, sizes, *refs):
-    out_ref = refs[-1]
-    refs = refs[:-1]
+def finish_kernel(half, members, sizes, first, rows_ref, sems, out_hbm, *refs):
     count = len(sizes)
     each = len(refs) // count
     slab, ex = lax.axis_index("slab"), lax.axis_index("ex")
     place = jnp.where(slab == 0, ex, 2 * members - 1 - ex)
-    at = 0
+    at, copies = first, []
     for k, size in enumerate(sizes):
         keep, got = refs[k * each], refs[k * each + 1:(k + 1) * each]
         for j in range(size):
@@ -248,23 +246,40 @@
             hops = 2 * members - distance if at % 2 == 1 else distance
             source = lax.rem(place + hops, 2 * members)
             block = jnp.where(source < members, 2 * source, 2 * (2 * members - 1 - source) + 1)
-            out_ref[pl.ds(pl.multiple_of(block * half, 8), half), :] = total
+            here = slice((at - first) * half, (at - first + 1) * half)
+            rows_ref[here, :] = total
+            copies.append(pltpu.make_async_copy(
+                rows_ref.at[here, :], out_hbm.at[pl.ds(pl.multiple_of(block * half, 8), half), :], sems.at[at - first]
+            ))
+            copies[-1].start()
             at += 1
-
-
-def finish(half, parts):
+    for copy in copies:
+        copy.wait()
+
+
+def finish(half, sums, first=0, before=None):
     members = lax.axis_size("ex")
-    vmem = pl.BlockSpec(memory_space=pltpu.VMEM)
-    flat = [array for keep, got in parts for array in [keep, *got]]
-    sizes = [keep.shape[0] // half for keep, _ in parts]
+    vmem, hbm = pl.BlockSpec(memory_space=pltpu.VMEM), pl.BlockSpec(memory_space=pltpu.HBM)
+    flat = [array for keep, got in sums for array in [keep, *got]]
+    sizes = [keep.shape[0] // half for keep, _ in sums]
+    share = flat[0].shape[1]
+    ahead = [] if before is None else [before]
+
+    def kernel(*refs):
+        out_hbm, rows_ref, sems = refs[-3:]
+        finish_kernel(half, members, sizes, first, rows_ref, sems, out_hbm, *refs[len(ahead):-3])
+
     return pl.pallas_call(
-        functools.partial(finish_kernel, half, members, sizes),
-        out_shape=jax.ShapeDtypeStruct((2 * members * half, flat[0].shape[1]), F32),
-        in_specs=[vmem] * len(flat),
-        out_specs=vmem,
+        kernel,
+        out_shape=jax.ShapeDtypeStruct((2 * members * half, share), F32),
+        in_specs=[hbm] * len(ahead) + [vmem] * len(flat),
+        out_specs=hbm,
+        input_output_aliases={0: 0} if ahead else {},
+        scratch_shapes=[pltpu.VMEM((sum(sizes) * half, share), F32), pltpu.SemaphoreType.DMA((sum(sizes),))],
         compiler_params=pltpu.CompilerParams(vmem_limit_bytes=16 << 20),
+        cost_estimate=pl.CostEstimate(flops=0, bytes_accessed=1 << 20, transcendentals=0),
         name="finish",
-    )(*flat)
+    )(*ahead, *flat)
 
 
 def local(
@@ -305,8 +320,9 @@
     far = swap_layers(score([], parts, turned, others, True))
     (keep,) = score(batch, parts, store, [0])
     rows = len(batch) * half
-    sums += [(keep[:rows], near), (keep[rows:], far)]
-    return finish(half, sums).T
+    sums.append((keep[:rows], near))
+    scores = finish(half, sums)
+    return finish(half, [(keep[rows:], far)], 2 * members - 1, scores).T
 
 
 def solution(mesh):

time: 31.3 us -> 31.2 us (level)
  waiting for transfers between devices: 10.5 us -> 9.73 us
  Pallas kernels: 7.35 us -> 8.01 us
    ppermute x2, waiting for transfers between devices: 1.4 us -> 0.65 us  [swap_layers(): lax.ppermute(send, 'lay', [(i, (i + k + 1) % shares) for i in range(share...]
    pallas_call x1 -> x2, Pallas kernels: 0.71 us -> 1.37 us  [finish(): pl.pallas_call(kernel, out_shape=jax.ShapeDtypeStruct((2 * members * half...]
  transfers between devices with their start and end apart: 10 -> 10, of which waited for: 6 -> 7; matrix products, arithmetic and copies ran while one was open for 0% -> 0% of each run, Pallas kernels for 15% -> 17%
where the time goes in v9:
time: 31.2 us; the launch traced here: 31 us
  starting transfers between devices  13.2 us (42%)
  waiting for transfers between devices  9.73 us (31%)
  Pallas kernels  8.01 us (26%)
    ppermute x8, starting transfers between devices, hop(): lax.ppermute(piece, RING, [(a, ring[(i + steps) % len(ring)]) for i, a in...  10.1 us
    ppermute x8, waiting for transfers between devices, hop(): lax.ppermute(piece, RING, [(a, ring[(i + steps) % len(ring)]) for i, a in...  9.09 us
    ppermute x2, starting transfers between devices, swap_layers(): lax.ppermute(send, 'lay', [(i, (i + k + 1) % shares) for i in range(share...  3.06 us
    pallas_call x1, Pallas kernels, fetch(): pl.pallas_call(functools.partial(fetch_kernel, shares), out_shape=[jax.Sh...  2.8 us
    pallas_call x1, Pallas kernels, rotate(): pl.pallas_call(functools.partial(rotate_kernel, half, 1), out_shape=jax.S...  1.99 us
    pallas_call x3, Pallas kernels, score(): pl.pallas_call(functools.partial(score_kernel, len(pieces), height, share...  1.86 us
    pallas_call x2, Pallas kernels, finish(): pl.pallas_call(kernel, out_shape=jax.ShapeDtypeStruct((2 * members * half...  1.37 us
    ppermute x2, waiting for transfers between devices, swap_layers(): lax.ppermute(send, 'lay', [(i, (i + k + 1) % shares) for i in range(share...  0.65 us
  transfers between devices with their start and end apart: 10, of which 7 were waited for; matrix products, arithmetic and copies ran while one was open for 0% of the time, Pallas kernels for 17%

profile of v9, /device:TPU:0, one launch (start us, length us, event | category | flops | bytes accessed | tf_op | source)
XLA Modules:
  0.0 31.0 jit_solution(14568733586077188712)
XLA Ops:
  0.0 2.0 %rotate.1.after_ref.refs_0_ = bf16[24,4096]{1,0:T(8,128)(2,1)S(1)} custom-call(bf16[1,48,4096]{2,1,0:T(8,128)(2,1)} %query_hbm.1, s32[384]{0:T(512)} %block_hbm.1, f32[4]{0:T(128)} %damping_hbm.1, s32[2]{0:T(128)} %slot_hbm.1, bf16[2,64,64]{2,1,0:T(8,128)(2,1)} %out_hbm.1, bf16[2,64,64]{2,1,0:T(8,128)(2,1)} %in_hbm.1, f32[2,64,64]{2,1,0:T(8,128)} %eigen_hbm.1), custom_call_target="tpu_custom_call" | custom-call | flops 201326592 | bytes 1048576 | tf_op jit(solution)/shard_map/rotate/pallas_call | solution.py:124
  2.0 3.1 %collective-permute-start = (bf16[24,4096]{1,0:T(8,128)(2,1)S(1)}, bf16[24,4096]{1,0:T(8,128)(2,1)S(1)}, u32[]{:S(2)}, u32[]{:S(2)}) collective-permute-start(bf16[24,4096]{1,0:T(8,128)(2,1)S(1)} %rotate.1.after_ref.refs_0_), channel_id=1, source_target_pairs={{0,4},{4,8},{8,12},{12,28},{28,24},{24,20},{20,16},{16,0},{1,5},{5... | collective-permute-start | bytes 589832 | tf_op jit(solution)/shard_map/ppermute | solution.py:292
  5.1 0.0 collective-permute-start.1
  5.1 2.8 %fetch.1 = (bf16[1,512,4096]{2,1,0:T(8,128)(2,1)S(1)}, bf16[1,4096,256]{2,1,0:T(8,128)(2,1)S(1)}) custom-call(bf16[24,4096]{1,0:T(8,128)(2,1)S(1)} %rotate.1.after_ref.refs_0_, bf16[1,512,4096]{2,1,0:T(8,128)(2,1)} %store_hbm.1), custom_call_target="tpu_custom_call" | custom-call | bytes 8388608 | tf_op jit(solution)/shard_map/fetch/pallas_call | solution.py:166
  7.9 2.0 %collective-permute-done.refs_1_ = bf16[24,4096]{1,0:T(8,128)(2,1)S(1)} collective-permute-done((bf16[24,4096]{1,0:T(8,128)(2,1)S(1)}, bf16[24,4096]{1,0:T(8,128)(2,1)S(1)}, u32[]{:S(2)}, u32[]{:S(2)}) %collective-permute-start) | collective-permute-done | bytes 196640 | tf_op jit(solution)/shard_map/ppermute | solution.py:292
  9.9 1.8 %collective-permute-start.2 = (bf16[24,4096]{1,0:T(8,128)(2,1)S(1)}, bf16[24,4096]{1,0:T(8,128)(2,1)S(1)}, u32[]{:S(2)}, u32[]{:S(2)}) collective-permute-start(bf16[24,4096]{1,0:T(8,128)(2,1)S(1)} %collective-permute-done.refs_1_), channel_id=1, source_target_pairs={{0,4},{4,8},{8,12},{12,28},{28,24},{24,20},{20,16},{16,0},{1,5},{5... | collective-permute-start | bytes 589832 | tf_op jit(solution)/shard_map/ppermute | solution.py:292
  11.7 0.0 collective-permute-done.1.refs_2_
  11.7 0.2 collective-permute-start.3
  11.9 4.1 %collective-permute-done.2.refs_3_ = bf16[24,4096]{1,0:T(8,128)(2,1)S(1)} collective-permute-done((bf16[24,4096]{1,0:T(8,128)(2,1)S(1)}, bf16[24,4096]{1,0:T(8,128)(2,1)S(1)}, u32[]{:S(2)}, u32[]{:S(2)}) %collective-permute-start.2) | collective-permute-done | bytes 196640 | tf_op jit(solution)/shard_map/ppermute | solution.py:292
  16.0 1.5 %collective-permute-start.4 = (bf16[24,4096]{1,0:T(8,128)(2,1)S(1)}, bf16[24,4096]{1,0:T(8,128)(2,1)S(1)}, u32[]{:S(2)}, u32[]{:S(2)}) collective-permute-start(bf16[24,4096]{1,0:T(8,128)(2,1)S(1)} %collective-permute-done.2.refs_3_), channel_id=1, source_target_pairs={{0,4},{4,8},{8,12},{12,28},{28,24},{24,20},{20,16},{16,0},{1,5},{5... | collective-permute-start | bytes 589832 | tf_op jit(solution)/shard_map/ppermute | solution.py:292
  17.5 0.0 collective-permute-done.3.refs_4_
  17.5 0.5 %collective-permute-start.5 = (bf16[24,4096]{1,0:T(8,128)(2,1)S(1)}, bf16[24,4096]{1,0:T(8,128)(2,1)S(1)}, u32[]{:S(2)}, u32[]{:S(2)}) collective-permute-start(bf16[24,4096]{1,0:T(8,128)(2,1)S(1)} %collective-permute-done.3.refs_4_), channel_id=1, source_target_pairs={{0,16},{4,0},{8,4},{12,8},{28,12},{24,28},{20,24},{16,20},{1,17},{... | collective-permute-start | bytes 589832 | tf_op jit(solution)/shard_map/ppermute | solution.py:292
  18.0 2.6 %collective-permute-start.6 = (bf16[24,2560]{1,0:T(8,128)(2,1)S(1)}, bf16[24,2560]{1,0:T(8,128)(2,1)S(1)}, u32[]{:S(2)}, u32[]{:S(2)}) collective-permute-start(bf16[24,2560]{1,0:T(8,128)(2,1)S(1)} %slice.16), channel_id=1, source_target_pairs={{0,8},{4,12},{8,28},{12,24},{28,20},{24,16},{20,0},{16,4},{1,9},{5... | collective-permute-start | bytes 368648 | tf_op jit(solution)/shard_map/ppermute | solution.py:292
  20.6 0.4 %collective-permute-start.7 = (bf16[24,1536]{1,0:T(8,128)(2,1)S(1)}, bf16[24,1536]{1,0:T(8,128)(2,1)S(1)}, u32[]{:S(2)}, u32[]{:S(2)}) collective-permute-start(bf16[24,1536]{1,0:T(8,128)(2,1)S(1)} %slice.17), channel_id=1, source_target_pairs={{0,20},{4,16},{8,0},{12,4},{28,8},{24,12},{20,28},{16,24},{1,21},{... | collective-permute-start | bytes 221192 | tf_op jit(solution)/shard_map/ppermute | solution.py:292
  21.0 2.0 %collective-permute-done.4.refs_5_ = bf16[24,4096]{1,0:T(8,128)(2,1)S(1)} collective-permute-done((bf16[24,4096]{1,0:T(8,128)(2,1)S(1)}, bf16[24,4096]{1,0:T(8,128)(2,1)S(1)}, u32[]{:S(2)}, u32[]{:S(2)}) %collective-permute-start.4) | collective-permute-done | bytes 196640 | tf_op jit(solution)/shard_map/ppermute | solution.py:292
  23.0 1.0 %collective-permute-done.5.refs_6_ = bf16[24,4096]{1,0:T(8,128)(2,1)S(1)} collective-permute-done((bf16[24,4096]{1,0:T(8,128)(2,1)S(1)}, bf16[24,4096]{1,0:T(8,128)(2,1)S(1)}, u32[]{:S(2)}, u32[]{:S(2)}) %collective-permute-start.5) | collective-permute-done | bytes 196640 | tf_op jit(solution)/shard_map/ppermute | solution.py:292
  24.0 0.6 %score.3 = bf16[168,256]{1,0:T(8,128)(2,1)S(1)} custom-call(bf16[24,4096]{1,0:T(8,128)(2,1)S(1)} %rotate.1.after_ref.refs_0_, bf16[24,4096]{1,0:T(8,128)(2,1)S(1)} %collective-permute-done.refs_1_, bf16[24,4096]{1,0:T(8,128)(2,1)S(1)} %collective-permute-done.1.refs_2_, bf16[24,4096]{1,0:T(8,128)(2,1)S(1)} %collective-permute-done.2.refs_3_, ...), custom_call_target="tpu_custom_call" | custom-call | flops 536870912 | bytes 1048576 | tf_op jit(solution)/shard_map/score/pallas_call | solution.py:210
  24.6 1.5 %collective-permute-start.8 = (bf16[168,256]{1,0:T(8,128)(2,1)S(1)}, bf16[168,256]{1,0:T(8,128)(2,1)S(1)}, u32[]{:S(2)}, u32[]{:S(2)}) collective-permute-start(bf16[168,256]{1,0:T(8,128)(2,1)S(1)} %score.3), channel_id=1, source_target_pairs={{0,2},{2,0},{1,3},{3,1},{4,6},{6,4},{5,7},{7,5},{8,10},{10,8},{9,1... | collective-permute-start | bytes 258056 | tf_op jit(solution)/shard_map/ppermute | solution.py:227
  26.2 0.0 collective-permute-done.7.refs_8_.refs_1_
  26.2 0.1 collective-permute-done.6.refs_7_.refs_0_
  26.2 0.5 %score.5 = bf16[24,256]{1,0:T(8,128)(2,1)S(1)} custom-call(bf16[24,2560]{1,0:T(8,128)(2,1)S(1)} %collective-permute-done.6.refs_7_.refs_0_, bf16[24,1536]{1,0:T(8,128)(2,1)S(1)} %collective-permute-done.7.refs_8_.refs_1_, bf16[1,4096,256]{2,1,0:T(8,128)(2,1)S(1)} %get-tuple-element.15.refs_7_.refs_2_), custom_call_target="tpu_custom_call" | custom-call | flops 536870912 | bytes 1048576 | tf_op jit(solution)/shard_map/score/pallas_call | solution.py:210
  26.7 1.5 %collective-permute-start.9 = (bf16[24,256]{1,0:T(8,128)(2,1)S(1)}, bf16[24,256]{1,0:T(8,128)(2,1)S(1)}, u32[]{:S(2)}, u32[]{:S(2)}) collective-permute-start(bf16[24,256]{1,0:T(8,128)(2,1)S(1)} %score.5), channel_id=1, source_target_pairs={{0,2},{2,0},{1,3},{3,1},{4,6},{6,4},{5,7},{7,5},{8,10},{10,8},{9,1... | collective-permute-start | bytes 36872 | tf_op jit(solution)/shard_map/ppermute | solution.py:227
  28.2 0.7 %score.4 = f32[192,256]{1,0:T(8,128)S(1)} custom-call(bf16[24,4096]{1,0:T(8,128)(2,1)S(1)} %rotate.1.after_ref.refs_0_, bf16[24,4096]{1,0:T(8,128)(2,1)S(1)} %collective-permute-done.refs_1_, bf16[24,4096]{1,0:T(8,128)(2,1)S(1)} %collective-permute-done.1.refs_2_, bf16[24,4096]{1,0:T(8,128)(2,1)S(1)} %collective-permute-done.2.refs_3_, ...), custom_call_target="tpu_custom_call" | custom-call | flops 536870912 | bytes 1048576 | tf_op jit(solution)/shard_map/score/pallas_call | solution.py:210
  29.0 0.2 collective-permute-done.8.refs_1_
  29.2 0.7 %finish.2.refs_0_ = f32[192,256]{1,0:T(8,128)} custom-call(f32[168,256]{1,0:T(8,128)S(1)} %slice.18.refs_0_, bf16[168,256]{1,0:T(8,128)(2,1)S(1)} %collective-permute-done.8.refs_1_), custom_call_target="tpu_custom_call" | custom-call | bytes 1048576 | tf_op jit(solution)/shard_map/finish/pallas_call | solution.py:272
  29.9 0.5 %collective-permute-done.9.refs_2_ = bf16[24,256]{1,0:T(8,128)(2,1)S(1)} collective-permute-done((bf16[24,256]{1,0:T(8,128)(2,1)S(1)}, bf16[24,256]{1,0:T(8,128)(2,1)S(1)}, u32[]{:S(2)}, u32[]{:S(2)}) %collective-permute-start.9) | collective-permute-done | bytes 12320 | tf_op jit(solution)/shard_map/ppermute | solution.py:227
  30.4 0.6 %finish.3 = f32[192,256]{1,0:T(8,128)} custom-call(f32[192,256]{1,0:T(8,128)} %finish.2.refs_0_, f32[24,256]{1,0:T(8,128)S(1)} %slice.19.refs_1_, bf16[24,256]{1,0:T(8,128)(2,1)S(1)} %collective-permute-done.9.refs_2_), custom_call_target="tpu_custom_call", output_to_operand_aliasing={{}: (0, {})} | custom-call | bytes 1048576 | tf_op jit(solution)/shard_map/finish/pallas_call | solution.py:272
  (4 shorter events, 0.0 us)
Async XLA Ops:
  2.0 7.9 %collective-permute-start = (bf16[24,4096]{1,0:T(8,128)(2,1)S(1)}, bf16[24,4096]{1,0:T(8,128)(2,1)S(1)}, u32[]{:S(2)}, u32[]{:S(2)}) collective-permute-start(bf16[24,4096]{1,0:T(8,128)(2,1)S(1)} %rotate.1.after_ref.refs_0_), channel_id=1, source_target_pairs={{0,4},{4,8},{8,12},{12,28},{28,24},{24,20},{20,16},{16,0},{1,5},{5... | collective-permute-start | bytes 589832 | tf_op jit(solution)/shard_map/ppermute | solution.py:292
  5.1 6.6 %collective-permute-start.1 = (bf16[24,4096]{1,0:T(8,128)(2,1)S(1)}, bf16[24,4096]{1,0:T(8,128)(2,1)S(1)}, u32[]{:S(2)}, u32[]{:S(2)}) collective-permute-start(bf16[24,4096]{1,0:T(8,128)(2,1)S(1)} %rotate.1.after_ref.refs_0_), channel_id=1, source_target_pairs={{0,16},{4,0},{8,4},{12,8},{28,12},{24,28},{20,24},{16,20},{1,17},{... | collective-permute-start | bytes 589832 | tf_op jit(solution)/shard_map/ppermute | solution.py:292
  9.9 6.1 %collective-permute-start.2 = (bf16[24,4096]{1,0:T(8,128)(2,1)S(1)}, bf16[24,4096]{1,0:T(8,128)(2,1)S(1)}, u32[]{:S(2)}, u32[]{:S(2)}) collective-permute-start(bf16[24,4096]{1,0:T(8,128)(2,1)S(1)} %collective-permute-done.refs_1_), channel_id=1, source_target_pairs={{0,4},{4,8},{8,12},{12,28},{28,24},{24,20},{20,16},{16,0},{1,5},{5... | collective-permute-start | bytes 589832 | tf_op jit(solution)/shard_map/ppermute | solution.py:292
  11.7 5.8 %collective-permute-start.3 = (bf16[24,4096]{1,0:T(8,128)(2,1)S(1)}, bf16[24,4096]{1,0:T(8,128)(2,1)S(1)}, u32[]{:S(2)}, u32[]{:S(2)}) collective-permute-start(bf16[24,4096]{1,0:T(8,128)(2,1)S(1)} %collective-permute-done.1.refs_2_), channel_id=1, source_target_pairs={{0,16},{4,0},{8,4},{12,8},{28,12},{24,28},{20,24},{16,20},{1,17},{... | collective-permute-start | bytes 589832 | tf_op jit(solution)/shard_map/ppermute | solution.py:292
  16.0 7.0 %collective-permute-start.4 = (bf16[24,4096]{1,0:T(8,128)(2,1)S(1)}, bf16[24,4096]{1,0:T(8,128)(2,1)S(1)}, u32[]{:S(2)}, u32[]{:S(2)}) collective-permute-start(bf16[24,4096]{1,0:T(8,128)(2,1)S(1)} %collective-permute-done.2.refs_3_), channel_id=1, source_target_pairs={{0,4},{4,8},{8,12},{12,28},{28,24},{24,20},{20,16},{16,0},{1,5},{5... | collective-permute-start | bytes 589832 | tf_op jit(solution)/shard_map/ppermute | solution.py:292
  17.5 6.5 %collective-permute-start.5 = (bf16[24,4096]{1,0:T(8,128)(2,1)S(1)}, bf16[24,4096]{1,0:T(8,128)(2,1)S(1)}, u32[]{:S(2)}, u32[]{:S(2)}) collective-permute-start(bf16[24,4096]{1,0:T(8,128)(2,1)S(1)} %collective-permute-done.3.refs_4_), channel_id=1, source_target_pairs={{0,16},{4,0},{8,4},{12,8},{28,12},{24,28},{20,24},{16,20},{1,17},{... | collective-permute-start | bytes 589832 | tf_op jit(solution)/shard_map/ppermute | solution.py:292
  18.0 8.2 %collective-permute-start.6 = (bf16[24,2560]{1,0:T(8,128)(2,1)S(1)}, bf16[24,2560]{1,0:T(8,128)(2,1)S(1)}, u32[]{:S(2)}, u32[]{:S(2)}) collective-permute-start(bf16[24,2560]{1,0:T(8,128)(2,1)S(1)} %slice.16), channel_id=1, source_target_pairs={{0,8},{4,12},{8,28},{12,24},{28,20},{24,16},{20,0},{16,4},{1,9},{5... | collective-permute-start | bytes 368648 | tf_op jit(solution)/shard_map/ppermute | solution.py:292
  20.6 5.6 %collective-permute-start.7 = (bf16[24,1536]{1,0:T(8,128)(2,1)S(1)}, bf16[24,1536]{1,0:T(8,128)(2,1)S(1)}, u32[]{:S(2)}, u32[]{:S(2)}) collective-permute-start(bf16[24,1536]{1,0:T(8,128)(2,1)S(1)} %slice.17), channel_id=1, source_target_pairs={{0,20},{4,16},{8,0},{12,4},{28,8},{24,12},{20,28},{16,24},{1,21},{... | collective-permute-start | bytes 221192 | tf_op jit(solution)/shard_map/ppermute | solution.py:292
  24.6 4.6 %collective-permute-start.8 = (bf16[168,256]{1,0:T(8,128)(2,1)S(1)}, bf16[168,256]{1,0:T(8,128)(2,1)S(1)}, u32[]{:S(2)}, u32[]{:S(2)}) collective-permute-start(bf16[168,256]{1,0:T(8,128)(2,1)S(1)} %score.3), channel_id=1, source_target_pairs={{0,2},{2,0},{1,3},{3,1},{4,6},{6,4},{5,7},{7,5},{8,10},{10,8},{9,1... | collective-permute-start | bytes 258056 | tf_op jit(solution)/shard_map/ppermute | solution.py:227
  26.7 3.7 %collective-permute-start.9 = (bf16[24,256]{1,0:T(8,128)(2,1)S(1)}, bf16[24,256]{1,0:T(8,128)(2,1)S(1)}, u32[]{:S(2)}, u32[]{:S(2)}) collective-permute-start(bf16[24,256]{1,0:T(8,128)(2,1)S(1)} %score.5), channel_id=1, source_target_pairs={{0,2},{2,0},{1,3},{3,1},{4,6},{6,4},{5,7},{7,5},{8,10},{10,8},{9,1... | collective-permute-start | bytes 36872 | tf_op jit(solution)/shard_map/ppermute | solution.py:227

commit v10 on v9

--- a/solution.py
+++ b/solution.py
@@ -30,17 +30,19 @@
     rows_ref, basis_ref, turned_ref, sems,
 ):
     pairs = RANK * RANK // 128
-    local = query_ref.shape[1]
+    local, span = query_hbm.shape[1], query_ref.shape[1]
+    slab = lax.axis_index("slab")
+    begin = pl.multiple_of(slab * (local - span), 16)
+    later = half - (local - span)
     copies = [
         pltpu.make_async_copy(source, target, sems.at[k])
         for k, (source, target) in enumerate([
-            (slot_hbm, slot_ref), (query_hbm, query_ref), (block_hbm, block_ref), (damping_hbm, damping_ref),
+            (slot_hbm, slot_ref), (query_hbm.at[:, pl.ds(begin, span), :], query_ref), (block_hbm, block_ref), (damping_hbm, damping_ref),
             (out_hbm, out_ref), (in_hbm, in_ref), (eigen_hbm, eigen_ref),
         ])
     ]
     for copy in copies:
         copy.start()
-    slab = lax.axis_index("slab")
     first = (lax.axis_index("pb") * lax.axis_size("ex") + lax.axis_index("ex")) * local + slab * half
     low_lanes = lax.broadcasted_iota(jnp.int32, (RANK // 2, 128), 1) < RANK
     row = lax.broadcasted_iota(jnp.int32, (4 * RANK, 4 * RANK), 0) // RANK
@@ -52,7 +54,7 @@
 
     for pair in range(pairs):
         block = query_ref[0, :, pair * 128:(pair + 1) * 128].astype(F32)
-        rows_ref[pair * half:(pair + 1) * half, :] = jnp.where(slab == 0, block[:half], block[half:2 * half])
+        rows_ref[pair * half:(pair + 1) * half, :] = jnp.where(slab == 0, block[:half], block[later:later + half])
 
     basis_ref[:RANK, :RANK] = out_ref[model_layer].astype(F32)
     out_rows = jnp.concatenate(
@@ -120,13 +122,15 @@
     half = query_grads.shape[1] // lax.axis_size("slab")
     dim = query_grads.shape[2]
     operands = (query_grads, query_block, damping, layer_slot, out_basis, in_basis, eigen_values)
+    span = -(-half // 16) * 16
+    held = ((1, span, dim), *(x.shape for x in operands[1:]))
     homes = (pltpu.VMEM, pltpu.SMEM, pltpu.SMEM, pltpu.SMEM, pltpu.VMEM, pltpu.VMEM, pltpu.VMEM)
     return pl.pallas_call(
         functools.partial(rotate_kernel, half, 1),
         out_shape=jax.ShapeDtypeStruct((half, dim), BF16),
         in_specs=[pl.BlockSpec(memory_space=pltpu.HBM)] * len(operands),
         out_specs=pl.BlockSpec(memory_space=pltpu.VMEM),
-        scratch_shapes=[home(x.shape, x.dtype) for home, x in zip(homes, operands)] + [
+        scratch_shapes=[home(shape, x.dtype) for home, shape, x in zip(homes, held, operands)] + [
             pltpu.VMEM((half * (dim // 128 + 1), 128), F32),
             pltpu.VMEM((RANK + 8, 128), F32),
             pltpu.VMEM((half * (dim // 128 + 1), 128), F32),

time: 31.2 us -> 31.2 us (level)
  no operation moved by 1% of the time
where the time goes in v10:
time: 31.2 us; the launch traced here: 31 us
  starting transfers between devices  13.2 us (42%)
  waiting for transfers between devices  9.76 us (31%)
  Pallas kernels  7.98 us (26%)
    ppermute x8, starting transfers between devices, hop(): lax.ppermute(piece, RING, [(a, ring[(i + steps) % len(ring)]) for i, a in...  10.1 us
    ppermute x8, waiting for transfers between devices, hop(): lax.ppermute(piece, RING, [(a, ring[(i + steps) % len(ring)]) for i, a in...  9.09 us
    ppermute x2, starting transfers between devices, swap_layers(): lax.ppermute(send, 'lay', [(i, (i + k + 1) % shares) for i in range(share...  3.05 us
    pallas_call x1, Pallas kernels, fetch(): pl.pallas_call(functools.partial(fetch_kernel, shares), out_shape=[jax.Sh...  2.8 us
    pallas_call x1, Pallas kernels, rotate(): pl.pallas_call(functools.partial(rotate_kernel, half, 1), out_shape=jax.S...  1.95 us
    pallas_call x3, Pallas kernels, score(): pl.pallas_call(functools.partial(score_kernel, len(pieces), height, share...  1.86 us
    pallas_call x2, Pallas kernels, finish(): pl.pallas_call(kernel, out_shape=jax.ShapeDtypeStruct((2 * members * half...  1.37 us
    ppermute x2, waiting for transfers between devices, swap_layers(): lax.ppermute(send, 'lay', [(i, (i + k + 1) % shares) for i in range(share...  0.66 us
  transfers between devices with their start and end apart: 10, of which 7 were waited for; matrix products, arithmetic and copies ran while one was open for 0% of the time, Pallas kernels for 17%

profile of v10, /device:TPU:0, one launch (start us, length us, event | category | flops | bytes accessed | tf_op | source)
XLA Modules:
  0.0 31.0 jit_solution(7626068937687885642)
XLA Ops:
  0.0 2.0 %rotate.1.after_ref.refs_0_ = bf16[24,4096]{1,0:T(8,128)(2,1)S(1)} custom-call(bf16[1,48,4096]{2,1,0:T(8,128)(2,1)} %query_hbm.1, s32[384]{0:T(512)} %block_hbm.1, f32[4]{0:T(128)} %damping_hbm.1, s32[2]{0:T(128)} %slot_hbm.1, bf16[2,64,64]{2,1,0:T(8,128)(2,1)} %out_hbm.1, bf16[2,64,64]{2,1,0:T(8,128)(2,1)} %in_hbm.1, f32[2,64,64]{2,1,0:T(8,128)} %eigen_hbm.1), custom_call_target="tpu_custom_call" | custom-call | flops 201326592 | bytes 1048576 | tf_op jit(solution)/shard_map/rotate/pallas_call | solution.py:128
  2.0 3.1 %collective-permute-start = (bf16[24,4096]{1,0:T(8,128)(2,1)S(1)}, bf16[24,4096]{1,0:T(8,128)(2,1)S(1)}, u32[]{:S(2)}, u32[]{:S(2)}) collective-permute-start(bf16[24,4096]{1,0:T(8,128)(2,1)S(1)} %rotate.1.after_ref.refs_0_), channel_id=1, source_target_pairs={{0,4},{4,8},{8,12},{12,28},{28,24},{24,20},{20,16},{16,0},{1,5},{5... | collective-permute-start | bytes 589832 | tf_op jit(solution)/shard_map/ppermute | solution.py:296
  5.0 0.0 collective-permute-start.1
  5.0 2.8 %fetch.1 = (bf16[1,512,4096]{2,1,0:T(8,128)(2,1)S(1)}, bf16[1,4096,256]{2,1,0:T(8,128)(2,1)S(1)}) custom-call(bf16[24,4096]{1,0:T(8,128)(2,1)S(1)} %rotate.1.after_ref.refs_0_, bf16[1,512,4096]{2,1,0:T(8,128)(2,1)} %store_hbm.1), custom_call_target="tpu_custom_call" | custom-call | bytes 8388608 | tf_op jit(solution)/shard_map/fetch/pallas_call | solution.py:170
  7.9 2.0 %collective-permute-done.refs_1_ = bf16[24,4096]{1,0:T(8,128)(2,1)S(1)} collective-permute-done((bf16[24,4096]{1,0:T(8,128)(2,1)S(1)}, bf16[24,4096]{1,0:T(8,128)(2,1)S(1)}, u32[]{:S(2)}, u32[]{:S(2)}) %collective-permute-start) | collective-permute-done | bytes 196640 | tf_op jit(solution)/shard_map/ppermute | solution.py:296
  9.9 1.8 %collective-permute-start.2 = (bf16[24,4096]{1,0:T(8,128)(2,1)S(1)}, bf16[24,4096]{1,0:T(8,128)(2,1)S(1)}, u32[]{:S(2)}, u32[]{:S(2)}) collective-permute-start(bf16[24,4096]{1,0:T(8,128)(2,1)S(1)} %collective-permute-done.refs_1_), channel_id=1, source_target_pairs={{0,4},{4,8},{8,12},{12,28},{28,24},{24,20},{20,16},{16,0},{1,5},{5... | collective-permute-start | bytes 589832 | tf_op jit(solution)/shard_map/ppermute | solution.py:296
  11.7 0.0 collective-permute-done.1.refs_2_
  11.7 0.2 collective-permute-start.3
  11.9 4.1 %collective-permute-done.2.refs_3_ = bf16[24,4096]{1,0:T(8,128)(2,1)S(1)} collective-permute-done((bf16[24,4096]{1,0:T(8,128)(2,1)S(1)}, bf16[24,4096]{1,0:T(8,128)(2,1)S(1)}, u32[]{:S(2)}, u32[]{:S(2)}) %collective-permute-start.2) | collective-permute-done | bytes 196640 | tf_op jit(solution)/shard_map/ppermute | solution.py:296
  16.0 1.5 %collective-permute-start.4 = (bf16[24,4096]{1,0:T(8,128)(2,1)S(1)}, bf16[24,4096]{1,0:T(8,128)(2,1)S(1)}, u32[]{:S(2)}, u32[]{:S(2)}) collective-permute-start(bf16[24,4096]{1,0:T(8,128)(2,1)S(1)} %collective-permute-done.2.refs_3_), channel_id=1, source_target_pairs={{0,4},{4,8},{8,12},{12,28},{28,24},{24,20},{20,16},{16,0},{1,5},{5... | collective-permute-start | bytes 589832 | tf_op jit(solution)/shard_map/ppermute | solution.py:296
  17.5 0.0 collective-permute-done.3.refs_4_
  17.5 0.5 %collective-permute-start.5 = (bf16[24,4096]{1,0:T(8,128)(2,1)S(1)}, bf16[24,4096]{1,0:T(8,128)(2,1)S(1)}, u32[]{:S(2)}, u32[]{:S(2)}) collective-permute-start(bf16[24,4096]{1,0:T(8,128)(2,1)S(1)} %collective-permute-done.3.refs_4_), channel_id=1, source_target_pairs={{0,16},{4,0},{8,4},{12,8},{28,12},{24,28},{20,24},{16,20},{1,17},{... | collective-permute-start | bytes 589832 | tf_op jit(solution)/shard_map/ppermute | solution.py:296
  18.0 2.5 %collective-permute-start.6 = (bf16[24,2560]{1,0:T(8,128)(2,1)S(1)}, bf16[24,2560]{1,0:T(8,128)(2,1)S(1)}, u32[]{:S(2)}, u32[]{:S(2)}) collective-permute-start(bf16[24,2560]{1,0:T(8,128)(2,1)S(1)} %slice.16), channel_id=1, source_target_pairs={{0,8},{4,12},{8,28},{12,24},{28,20},{24,16},{20,0},{16,4},{1,9},{5... | collective-permute-start | bytes 368648 | tf_op jit(solution)/shard_map/ppermute | solution.py:296
  20.6 0.4 %collective-permute-start.7 = (bf16[24,1536]{1,0:T(8,128)(2,1)S(1)}, bf16[24,1536]{1,0:T(8,128)(2,1)S(1)}, u32[]{:S(2)}, u32[]{:S(2)}) collective-permute-start(bf16[24,1536]{1,0:T(8,128)(2,1)S(1)} %slice.17), channel_id=1, source_target_pairs={{0,20},{4,16},{8,0},{12,4},{28,8},{24,12},{20,28},{16,24},{1,21},{... | collective-permute-start | bytes 221192 | tf_op jit(solution)/shard_map/ppermute | solution.py:296
  21.0 2.0 %collective-permute-done.4.refs_5_ = bf16[24,4096]{1,0:T(8,128)(2,1)S(1)} collective-permute-done((bf16[24,4096]{1,0:T(8,128)(2,1)S(1)}, bf16[24,4096]{1,0:T(8,128)(2,1)S(1)}, u32[]{:S(2)}, u32[]{:S(2)}) %collective-permute-start.4) | collective-permute-done | bytes 196640 | tf_op jit(solution)/shard_map/ppermute | solution.py:296
  23.0 1.0 %collective-permute-done.5.refs_6_ = bf16[24,4096]{1,0:T(8,128)(2,1)S(1)} collective-permute-done((bf16[24,4096]{1,0:T(8,128)(2,1)S(1)}, bf16[24,4096]{1,0:T(8,128)(2,1)S(1)}, u32[]{:S(2)}, u32[]{:S(2)}) %collective-permute-start.5) | collective-permute-done | bytes 196640 | tf_op jit(solution)/shard_map/ppermute | solution.py:296
  23.9 0.7 %score.3 = bf16[168,256]{1,0:T(8,128)(2,1)S(1)} custom-call(bf16[24,4096]{1,0:T(8,128)(2,1)S(1)} %rotate.1.after_ref.refs_0_, bf16[24,4096]{1,0:T(8,128)(2,1)S(1)} %collective-permute-done.refs_1_, bf16[24,4096]{1,0:T(8,128)(2,1)S(1)} %collective-permute-done.1.refs_2_, bf16[24,4096]{1,0:T(8,128)(2,1)S(1)} %collective-permute-done.2.refs_3_, ...), custom_call_target="tpu_custom_call" | custom-call | flops 536870912 | bytes 1048576 | tf_op jit(solution)/shard_map/score/pallas_call | solution.py:214
  24.6 1.6 %collective-permute-start.8 = (bf16[168,256]{1,0:T(8,128)(2,1)S(1)}, bf16[168,256]{1,0:T(8,128)(2,1)S(1)}, u32[]{:S(2)}, u32[]{:S(2)}) collective-permute-start(bf16[168,256]{1,0:T(8,128)(2,1)S(1)} %score.3), channel_id=1, source_target_pairs={{0,2},{2,0},{1,3},{3,1},{4,6},{6,4},{5,7},{7,5},{8,10},{10,8},{9,1... | collective-permute-start | bytes 258056 | tf_op jit(solution)/shard_map/ppermute | solution.py:231
  26.1 0.0 collective-permute-done.7.refs_8_.refs_1_
  26.1 0.1 collective-permute-done.6.refs_7_.refs_0_
  26.2 0.5 %score.5 = bf16[24,256]{1,0:T(8,128)(2,1)S(1)} custom-call(bf16[24,2560]{1,0:T(8,128)(2,1)S(1)} %collective-permute-done.6.refs_7_.refs_0_, bf16[24,1536]{1,0:T(8,128)(2,1)S(1)} %collective-permute-done.7.refs_8_.refs_1_, bf16[1,4096,256]{2,1,0:T(8,128)(2,1)S(1)} %get-tuple-element.15.refs_7_.refs_2_), custom_call_target="tpu_custom_call" | custom-call | flops 536870912 | bytes 1048576 | tf_op jit(solution)/shard_map/score/pallas_call | solution.py:214
  26.7 1.5 %collective-permute-start.9 = (bf16[24,256]{1,0:T(8,128)(2,1)S(1)}, bf16[24,256]{1,0:T(8,128)(2,1)S(1)}, u32[]{:S(2)}, u32[]{:S(2)}) collective-permute-start(bf16[24,256]{1,0:T(8,128)(2,1)S(1)} %score.5), channel_id=1, source_target_pairs={{0,2},{2,0},{1,3},{3,1},{4,6},{6,4},{5,7},{7,5},{8,10},{10,8},{9,1... | collective-permute-start | bytes 36872 | tf_op jit(solution)/shard_map/ppermute | solution.py:231
  28.2 0.7 %score.4 = f32[192,256]{1,0:T(8,128)S(1)} custom-call(bf16[24,4096]{1,0:T(8,128)(2,1)S(1)} %rotate.1.after_ref.refs_0_, bf16[24,4096]{1,0:T(8,128)(2,1)S(1)} %collective-permute-done.refs_1_, bf16[24,4096]{1,0:T(8,128)(2,1)S(1)} %collective-permute-done.1.refs_2_, bf16[24,4096]{1,0:T(8,128)(2,1)S(1)} %collective-permute-done.2.refs_3_, ...), custom_call_target="tpu_custom_call" | custom-call | flops 536870912 | bytes 1048576 | tf_op jit(solution)/shard_map/score/pallas_call | solution.py:214
  29.0 0.2 collective-permute-done.8.refs_1_
  29.1 0.7 %finish.2.refs_0_ = f32[192,256]{1,0:T(8,128)} custom-call(f32[168,256]{1,0:T(8,128)S(1)} %slice.18.refs_0_, bf16[168,256]{1,0:T(8,128)(2,1)S(1)} %collective-permute-done.8.refs_1_), custom_call_target="tpu_custom_call" | custom-call | bytes 1048576 | tf_op jit(solution)/shard_map/finish/pallas_call | solution.py:276
  29.9 0.5 %collective-permute-done.9.refs_2_ = bf16[24,256]{1,0:T(8,128)(2,1)S(1)} collective-permute-done((bf16[24,256]{1,0:T(8,128)(2,1)S(1)}, bf16[24,256]{1,0:T(8,128)(2,1)S(1)}, u32[]{:S(2)}, u32[]{:S(2)}) %collective-permute-start.9) | collective-permute-done | bytes 12320 | tf_op jit(solution)/shard_map/ppermute | solution.py:231
  30.4 0.6 %finish.3 = f32[192,256]{1,0:T(8,128)} custom-call(f32[192,256]{1,0:T(8,128)} %finish.2.refs_0_, f32[24,256]{1,0:T(8,128)S(1)} %slice.19.refs_1_, bf16[24,256]{1,0:T(8,128)(2,1)S(1)} %collective-permute-done.9.refs_2_), custom_call_target="tpu_custom_call", output_to_operand_aliasing={{}: (0, {})} | custom-call | bytes 1048576 | tf_op jit(solution)/shard_map/finish/pallas_call | solution.py:276
  (4 shorter events, 0.0 us)
Async XLA Ops:
  2.0 7.9 %collective-permute-start = (bf16[24,4096]{1,0:T(8,128)(2,1)S(1)}, bf16[24,4096]{1,0:T(8,128)(2,1)S(1)}, u32[]{:S(2)}, u32[]{:S(2)}) collective-permute-start(bf16[24,4096]{1,0:T(8,128)(2,1)S(1)} %rotate.1.after_ref.refs_0_), channel_id=1, source_target_pairs={{0,4},{4,8},{8,12},{12,28},{28,24},{24,20},{20,16},{16,0},{1,5},{5... | collective-permute-start | bytes 589832 | tf_op jit(solution)/shard_map/ppermute | solution.py:296
  5.0 6.6 %collective-permute-start.1 = (bf16[24,4096]{1,0:T(8,128)(2,1)S(1)}, bf16[24,4096]{1,0:T(8,128)(2,1)S(1)}, u32[]{:S(2)}, u32[]{:S(2)}) collective-permute-start(bf16[24,4096]{1,0:T(8,128)(2,1)S(1)} %rotate.1.after_ref.refs_0_), channel_id=1, source_target_pairs={{0,16},{4,0},{8,4},{12,8},{28,12},{24,28},{20,24},{16,20},{1,17},{... | collective-permute-start | bytes 589832 | tf_op jit(solution)/shard_map/ppermute | solution.py:296
  9.9 6.1 %collective-permute-start.2 = (bf16[24,4096]{1,0:T(8,128)(2,1)S(1)}, bf16[24,4096]{1,0:T(8,128)(2,1)S(1)}, u32[]{:S(2)}, u32[]{:S(2)}) collective-permute-start(bf16[24,4096]{1,0:T(8,128)(2,1)S(1)} %collective-permute-done.refs_1_), channel_id=1, source_target_pairs={{0,4},{4,8},{8,12},{12,28},{28,24},{24,20},{20,16},{16,0},{1,5},{5... | collective-permute-start | bytes 589832 | tf_op jit(solution)/shard_map/ppermute | solution.py:296
  11.7 5.8 %collective-permute-start.3 = (bf16[24,4096]{1,0:T(8,128)(2,1)S(1)}, bf16[24,4096]{1,0:T(8,128)(2,1)S(1)}, u32[]{:S(2)}, u32[]{:S(2)}) collective-permute-start(bf16[24,4096]{1,0:T(8,128)(2,1)S(1)} %collective-permute-done.1.refs_2_), channel_id=1, source_target_pairs={{0,16},{4,0},{8,4},{12,8},{28,12},{24,28},{20,24},{16,20},{1,17},{... | collective-permute-start | bytes 589832 | tf_op jit(solution)/shard_map/ppermute | solution.py:296
  16.0 7.0 %collective-permute-start.4 = (bf16[24,4096]{1,0:T(8,128)(2,1)S(1)}, bf16[24,4096]{1,0:T(8,128)(2,1)S(1)}, u32[]{:S(2)}, u32[]{:S(2)}) collective-permute-start(bf16[24,4096]{1,0:T(8,128)(2,1)S(1)} %collective-permute-done.2.refs_3_), channel_id=1, source_target_pairs={{0,4},{4,8},{8,12},{12,28},{28,24},{24,20},{20,16},{16,0},{1,5},{5... | collective-permute-start | bytes 589832 | tf_op jit(solution)/shard_map/ppermute | solution.py:296
  17.5 6.5 %collective-permute-start.5 = (bf16[24,4096]{1,0:T(8,128)(2,1)S(1)}, bf16[24,4096]{1,0:T(8,128)(2,1)S(1)}, u32[]{:S(2)}, u32[]{:S(2)}) collective-permute-start(bf16[24,4096]{1,0:T(8,128)(2,1)S(1)} %collective-permute-done.3.refs_4_), channel_id=1, source_target_pairs={{0,16},{4,0},{8,4},{12,8},{28,12},{24,28},{20,24},{16,20},{1,17},{... | collective-permute-start | bytes 589832 | tf_op jit(solution)/shard_map/ppermute | solution.py:296
  18.0 8.2 %collective-permute-start.6 = (bf16[24,2560]{1,0:T(8,128)(2,1)S(1)}, bf16[24,2560]{1,0:T(8,128)(2,1)S(1)}, u32[]{:S(2)}, u32[]{:S(2)}) collective-permute-start(bf16[24,2560]{1,0:T(8,128)(2,1)S(1)} %slice.16), channel_id=1, source_target_pairs={{0,8},{4,12},{8,28},{12,24},{28,20},{24,16},{20,0},{16,4},{1,9},{5... | collective-permute-start | bytes 368648 | tf_op jit(solution)/shard_map/ppermute | solution.py:296
  20.6 5.6 %collective-permute-start.7 = (bf16[24,1536]{1,0:T(8,128)(2,1)S(1)}, bf16[24,1536]{1,0:T(8,128)(2,1)S(1)}, u32[]{:S(2)}, u32[]{:S(2)}) collective-permute-start(bf16[24,1536]{1,0:T(8,128)(2,1)S(1)} %slice.17), channel_id=1, source_target_pairs={{0,20},{4,16},{8,0},{12,4},{28,8},{24,12},{20,28},{16,24},{1,21},{... | collective-permute-start | bytes 221192 | tf_op jit(solution)/shard_map/ppermute | solution.py:296
  24.6 4.6 %collective-permute-start.8 = (bf16[168,256]{1,0:T(8,128)(2,1)S(1)}, bf16[168,256]{1,0:T(8,128)(2,1)S(1)}, u32[]{:S(2)}, u32[]{:S(2)}) collective-permute-start(bf16[168,256]{1,0:T(8,128)(2,1)S(1)} %score.3), channel_id=1, source_target_pairs={{0,2},{2,0},{1,3},{3,1},{4,6},{6,4},{5,7},{7,5},{8,10},{10,8},{9,1... | collective-permute-start | bytes 258056 | tf_op jit(solution)/shard_map/ppermute | solution.py:231
  26.7 3.7 %collective-permute-start.9 = (bf16[24,256]{1,0:T(8,128)(2,1)S(1)}, bf16[24,256]{1,0:T(8,128)(2,1)S(1)}, u32[]{:S(2)}, u32[]{:S(2)}) collective-permute-start(bf16[24,256]{1,0:T(8,128)(2,1)S(1)} %score.5), channel_id=1, source_target_pairs={{0,2},{2,0},{1,3},{3,1},{4,6},{6,4},{5,7},{7,5},{8,10},{10,8},{9,1... | collective-permute-start | bytes 36872 | tf_op jit(solution)/shard_map/ppermute | solution.py:231

commit v11 on v10

--- a/solution.py
+++ b/solution.py
@@ -52,9 +52,12 @@
         copy.wait()
     model_layer = slot_ref[lax.axis_index("lay") * lay_slots]
 
-    for pair in range(pairs):
-        block = query_ref[0, :, pair * 128:(pair + 1) * 128].astype(F32)
-        rows_ref[pair * half:(pair + 1) * half, :] = jnp.where(slab == 0, block[:half], block[later:later + half])
+    for number, start in ((0, 0), (1, later)):
+        @pl.when(slab == number)
+        def _(start=start):
+            for pair in range(pairs):
+                block = query_ref[0, :, pair * 128:(pair + 1) * 128].astype(F32)
+                rows_ref[pair * half:(pair + 1) * half, :] = block[start:start + half]
 
     basis_ref[:RANK, :RANK] = out_ref[model_layer].astype(F32)
     out_rows = jnp.concatenate(

time: 31.2 us -> 31.2 us (level)
  no operation moved by 1% of the time
where the time goes in v11:
time: 31.2 us; the launch traced here: 31 us
  starting transfers between devices  13.2 us (42%)
  waiting for transfers between devices  9.75 us (31%)
  Pallas kernels  7.99 us (26%)
    ppermute x8, starting transfers between devices, hop(): lax.ppermute(piece, RING, [(a, ring[(i + steps) % len(ring)]) for i, a in...  10.1 us
    ppermute x8, waiting for transfers between devices, hop(): lax.ppermute(piece, RING, [(a, ring[(i + steps) % len(ring)]) for i, a in...  9.09 us
    ppermute x2, starting transfers between devices, swap_layers(): lax.ppermute(send, 'lay', [(i, (i + k + 1) % shares) for i in range(share...  3.06 us
    pallas_call x1, Pallas kernels, fetch(): pl.pallas_call(functools.partial(fetch_kernel, shares), out_shape=[jax.Sh...  2.8 us
    pallas_call x1, Pallas kernels, rotate(): pl.pallas_call(functools.partial(rotate_kernel, half, 1), out_shape=jax.S...  1.96 us
    pallas_call x3, Pallas kernels, score(): pl.pallas_call(functools.partial(score_kernel, len(pieces), height, share...  1.86 us
    pallas_call x2, Pallas kernels, finish(): pl.pallas_call(kernel, out_shape=jax.ShapeDtypeStruct((2 * members * half...  1.37 us
    ppermute x2, waiting for transfers between devices, swap_layers(): lax.ppermute(send, 'lay', [(i, (i + k + 1) % shares) for i in range(share...  0.66 us
  transfers between devices with their start and end apart: 10, of which 7 were waited for; matrix products, arithmetic and copies ran while one was open for 0% of the time, Pallas kernels for 17%

profile of v11, /device:TPU:0, one launch (start us, length us, event | category | flops | bytes accessed | tf_op | source)
XLA Modules:
  0.0 31.0 jit_solution(6752756430284749989)
XLA Ops:
  0.0 2.0 %rotate.1.after_ref.refs_0_ = bf16[24,4096]{1,0:T(8,128)(2,1)S(1)} custom-call(bf16[1,48,4096]{2,1,0:T(8,128)(2,1)} %query_hbm.1, s32[384]{0:T(512)} %block_hbm.1, f32[4]{0:T(128)} %damping_hbm.1, s32[2]{0:T(128)} %slot_hbm.1, bf16[2,64,64]{2,1,0:T(8,128)(2,1)} %out_hbm.1, bf16[2,64,64]{2,1,0:T(8,128)(2,1)} %in_hbm.1, f32[2,64,64]{2,1,0:T(8,128)} %eigen_hbm.1), custom_call_target="tpu_custom_call" | custom-call | flops 201326592 | bytes 1048576 | tf_op jit(solution)/shard_map/rotate/pallas_call | solution.py:131
  2.0 3.1 %collective-permute-start = (bf16[24,4096]{1,0:T(8,128)(2,1)S(1)}, bf16[24,4096]{1,0:T(8,128)(2,1)S(1)}, u32[]{:S(2)}, u32[]{:S(2)}) collective-permute-start(bf16[24,4096]{1,0:T(8,128)(2,1)S(1)} %rotate.1.after_ref.refs_0_), channel_id=1, source_target_pairs={{0,4},{4,8},{8,12},{12,28},{28,24},{24,20},{20,16},{16,0},{1,5},{5... | collective-permute-start | bytes 589832 | tf_op jit(solution)/shard_map/ppermute | solution.py:299
  5.0 0.0 collective-permute-start.1
  5.1 2.8 %fetch.1 = (bf16[1,512,4096]{2,1,0:T(8,128)(2,1)S(1)}, bf16[1,4096,256]{2,1,0:T(8,128)(2,1)S(1)}) custom-call(bf16[24,4096]{1,0:T(8,128)(2,1)S(1)} %rotate.1.after_ref.refs_0_, bf16[1,512,4096]{2,1,0:T(8,128)(2,1)} %store_hbm.1), custom_call_target="tpu_custom_call" | custom-call | bytes 8388608 | tf_op jit(solution)/shard_map/fetch/pallas_call | solution.py:173
  7.9 2.0 %collective-permute-done.refs_1_ = bf16[24,4096]{1,0:T(8,128)(2,1)S(1)} collective-permute-done((bf16[24,4096]{1,0:T(8,128)(2,1)S(1)}, bf16[24,4096]{1,0:T(8,128)(2,1)S(1)}, u32[]{:S(2)}, u32[]{:S(2)}) %collective-permute-start) | collective-permute-done | bytes 196640 | tf_op jit(solution)/shard_map/ppermute | solution.py:299
  9.9 1.8 %collective-permute-start.2 = (bf16[24,4096]{1,0:T(8,128)(2,1)S(1)}, bf16[24,4096]{1,0:T(8,128)(2,1)S(1)}, u32[]{:S(2)}, u32[]{:S(2)}) collective-permute-start(bf16[24,4096]{1,0:T(8,128)(2,1)S(1)} %collective-permute-done.refs_1_), channel_id=1, source_target_pairs={{0,4},{4,8},{8,12},{12,28},{28,24},{24,20},{20,16},{16,0},{1,5},{5... | collective-permute-start | bytes 589832 | tf_op jit(solution)/shard_map/ppermute | solution.py:299
  11.7 0.0 collective-permute-done.1.refs_2_
  11.7 0.2 collective-permute-start.3
  11.9 4.1 %collective-permute-done.2.refs_3_ = bf16[24,4096]{1,0:T(8,128)(2,1)S(1)} collective-permute-done((bf16[24,4096]{1,0:T(8,128)(2,1)S(1)}, bf16[24,4096]{1,0:T(8,128)(2,1)S(1)}, u32[]{:S(2)}, u32[]{:S(2)}) %collective-permute-start.2) | collective-permute-done | bytes 196640 | tf_op jit(solution)/shard_map/ppermute | solution.py:299
  16.0 1.5 %collective-permute-start.4 = (bf16[24,4096]{1,0:T(8,128)(2,1)S(1)}, bf16[24,4096]{1,0:T(8,128)(2,1)S(1)}, u32[]{:S(2)}, u32[]{:S(2)}) collective-permute-start(bf16[24,4096]{1,0:T(8,128)(2,1)S(1)} %collective-permute-done.2.refs_3_), channel_id=1, source_target_pairs={{0,4},{4,8},{8,12},{12,28},{28,24},{24,20},{20,16},{16,0},{1,5},{5... | collective-permute-start | bytes 589832 | tf_op jit(solution)/shard_map/ppermute | solution.py:299
  17.5 0.0 collective-permute-done.3.refs_4_
  17.5 0.5 %collective-permute-start.5 = (bf16[24,4096]{1,0:T(8,128)(2,1)S(1)}, bf16[24,4096]{1,0:T(8,128)(2,1)S(1)}, u32[]{:S(2)}, u32[]{:S(2)}) collective-permute-start(bf16[24,4096]{1,0:T(8,128)(2,1)S(1)} %collective-permute-done.3.refs_4_), channel_id=1, source_target_pairs={{0,16},{4,0},{8,4},{12,8},{28,12},{24,28},{20,24},{16,20},{1,17},{... | collective-permute-start | bytes 589832 | tf_op jit(solution)/shard_map/ppermute | solution.py:299
  18.0 2.5 %collective-permute-start.6 = (bf16[24,2560]{1,0:T(8,128)(2,1)S(1)}, bf16[24,2560]{1,0:T(8,128)(2,1)S(1)}, u32[]{:S(2)}, u32[]{:S(2)}) collective-permute-start(bf16[24,2560]{1,0:T(8,128)(2,1)S(1)} %slice.16), channel_id=1, source_target_pairs={{0,8},{4,12},{8,28},{12,24},{28,20},{24,16},{20,0},{16,4},{1,9},{5... | collective-permute-start | bytes 368648 | tf_op jit(solution)/shard_map/ppermute | solution.py:299
  20.6 0.4 %collective-permute-start.7 = (bf16[24,1536]{1,0:T(8,128)(2,1)S(1)}, bf16[24,1536]{1,0:T(8,128)(2,1)S(1)}, u32[]{:S(2)}, u32[]{:S(2)}) collective-permute-start(bf16[24,1536]{1,0:T(8,128)(2,1)S(1)} %slice.17), channel_id=1, source_target_pairs={{0,20},{4,16},{8,0},{12,4},{28,8},{24,12},{20,28},{16,24},{1,21},{... | collective-permute-start | bytes 221192 | tf_op jit(solution)/shard_map/ppermute | solution.py:299
  21.0 2.0 %collective-permute-done.4.refs_5_ = bf16[24,4096]{1,0:T(8,128)(2,1)S(1)} collective-permute-done((bf16[24,4096]{1,0:T(8,128)(2,1)S(1)}, bf16[24,4096]{1,0:T(8,128)(2,1)S(1)}, u32[]{:S(2)}, u32[]{:S(2)}) %collective-permute-start.4) | collective-permute-done | bytes 196640 | tf_op jit(solution)/shard_map/ppermute | solution.py:299
  23.0 1.0 %collective-permute-done.5.refs_6_ = bf16[24,4096]{1,0:T(8,128)(2,1)S(1)} collective-permute-done((bf16[24,4096]{1,0:T(8,128)(2,1)S(1)}, bf16[24,4096]{1,0:T(8,128)(2,1)S(1)}, u32[]{:S(2)}, u32[]{:S(2)}) %collective-permute-start.5) | collective-permute-done | bytes 196640 | tf_op jit(solution)/shard_map/ppermute | solution.py:299
  23.9 0.7 %score.3 = bf16[168,256]{1,0:T(8,128)(2,1)S(1)} custom-call(bf16[24,4096]{1,0:T(8,128)(2,1)S(1)} %rotate.1.after_ref.refs_0_, bf16[24,4096]{1,0:T(8,128)(2,1)S(1)} %collective-permute-done.refs_1_, bf16[24,4096]{1,0:T(8,128)(2,1)S(1)} %collective-permute-done.1.refs_2_, bf16[24,4096]{1,0:T(8,128)(2,1)S(1)} %collective-permute-done.2.refs_3_, ...), custom_call_target="tpu_custom_call" | custom-call | flops 536870912 | bytes 1048576 | tf_op jit(solution)/shard_map/score/pallas_call | solution.py:217
  24.6 1.6 %collective-permute-start.8 = (bf16[168,256]{1,0:T(8,128)(2,1)S(1)}, bf16[168,256]{1,0:T(8,128)(2,1)S(1)}, u32[]{:S(2)}, u32[]{:S(2)}) collective-permute-start(bf16[168,256]{1,0:T(8,128)(2,1)S(1)} %score.3), channel_id=1, source_target_pairs={{0,2},{2,0},{1,3},{3,1},{4,6},{6,4},{5,7},{7,5},{8,10},{10,8},{9,1... | collective-permute-start | bytes 258056 | tf_op jit(solution)/shard_map/ppermute | solution.py:234
  26.2 0.0 collective-permute-done.7.refs_8_.refs_1_
  26.2 0.1 collective-permute-done.6.refs_7_.refs_0_
  26.2 0.5 %score.5 = bf16[24,256]{1,0:T(8,128)(2,1)S(1)} custom-call(bf16[24,2560]{1,0:T(8,128)(2,1)S(1)} %collective-permute-done.6.refs_7_.refs_0_, bf16[24,1536]{1,0:T(8,128)(2,1)S(1)} %collective-permute-done.7.refs_8_.refs_1_, bf16[1,4096,256]{2,1,0:T(8,128)(2,1)S(1)} %get-tuple-element.15.refs_7_.refs_2_), custom_call_target="tpu_custom_call" | custom-call | flops 536870912 | bytes 1048576 | tf_op jit(solution)/shard_map/score/pallas_call | solution.py:217
  26.7 1.5 %collective-permute-start.9 = (bf16[24,256]{1,0:T(8,128)(2,1)S(1)}, bf16[24,256]{1,0:T(8,128)(2,1)S(1)}, u32[]{:S(2)}, u32[]{:S(2)}) collective-permute-start(bf16[24,256]{1,0:T(8,128)(2,1)S(1)} %score.5), channel_id=1, source_target_pairs={{0,2},{2,0},{1,3},{3,1},{4,6},{6,4},{5,7},{7,5},{8,10},{10,8},{9,1... | collective-permute-start | bytes 36872 | tf_op jit(solution)/shard_map/ppermute | solution.py:234
  28.2 0.7 %score.4 = f32[192,256]{1,0:T(8,128)S(1)} custom-call(bf16[24,4096]{1,0:T(8,128)(2,1)S(1)} %rotate.1.after_ref.refs_0_, bf16[24,4096]{1,0:T(8,128)(2,1)S(1)} %collective-permute-done.refs_1_, bf16[24,4096]{1,0:T(8,128)(2,1)S(1)} %collective-permute-done.1.refs_2_, bf16[24,4096]{1,0:T(8,128)(2,1)S(1)} %collective-permute-done.2.refs_3_, ...), custom_call_target="tpu_custom_call" | custom-call | flops 536870912 | bytes 1048576 | tf_op jit(solution)/shard_map/score/pallas_call | solution.py:217
  29.0 0.2 collective-permute-done.8.refs_1_
  29.2 0.7 %finish.2.refs_0_ = f32[192,256]{1,0:T(8,128)} custom-call(f32[168,256]{1,0:T(8,128)S(1)} %slice.18.refs_0_, bf16[168,256]{1,0:T(8,128)(2,1)S(1)} %collective-permute-done.8.refs_1_), custom_call_target="tpu_custom_call" | custom-call | bytes 1048576 | tf_op jit(solution)/shard_map/finish/pallas_call | solution.py:279
  29.9 0.5 %collective-permute-done.9.refs_2_ = bf16[24,256]{1,0:T(8,128)(2,1)S(1)} collective-permute-done((bf16[24,256]{1,0:T(8,128)(2,1)S(1)}, bf16[24,256]{1,0:T(8,128)(2,1)S(1)}, u32[]{:S(2)}, u32[]{:S(2)}) %collective-permute-start.9) | collective-permute-done | bytes 12320 | tf_op jit(solution)/shard_map/ppermute | solution.py:234
  30.4 0.6 %finish.3 = f32[192,256]{1,0:T(8,128)} custom-call(f32[192,256]{1,0:T(8,128)} %finish.2.refs_0_, f32[24,256]{1,0:T(8,128)S(1)} %slice.19.refs_1_, bf16[24,256]{1,0:T(8,128)(2,1)S(1)} %collective-permute-done.9.refs_2_), custom_call_target="tpu_custom_call", output_to_operand_aliasing={{}: (0, {})} | custom-call | bytes 1048576 | tf_op jit(solution)/shard_map/finish/pallas_call | solution.py:279
  (4 shorter events, 0.0 us)
Async XLA Ops:
  2.0 7.9 %collective-permute-start = (bf16[24,4096]{1,0:T(8,128)(2,1)S(1)}, bf16[24,4096]{1,0:T(8,128)(2,1)S(1)}, u32[]{:S(2)}, u32[]{:S(2)}) collective-permute-start(bf16[24,4096]{1,0:T(8,128)(2,1)S(1)} %rotate.1.after_ref.refs_0_), channel_id=1, source_target_pairs={{0,4},{4,8},{8,12},{12,28},{28,24},{24,20},{20,16},{16,0},{1,5},{5... | collective-permute-start | bytes 589832 | tf_op jit(solution)/shard_map/ppermute | solution.py:299
  5.0 6.6 %collective-permute-start.1 = (bf16[24,4096]{1,0:T(8,128)(2,1)S(1)}, bf16[24,4096]{1,0:T(8,128)(2,1)S(1)}, u32[]{:S(2)}, u32[]{:S(2)}) collective-permute-start(bf16[24,4096]{1,0:T(8,128)(2,1)S(1)} %rotate.1.after_ref.refs_0_), channel_id=1, source_target_pairs={{0,16},{4,0},{8,4},{12,8},{28,12},{24,28},{20,24},{16,20},{1,17},{... | collective-permute-start | bytes 589832 | tf_op jit(solution)/shard_map/ppermute | solution.py:299
  9.9 6.1 %collective-permute-start.2 = (bf16[24,4096]{1,0:T(8,128)(2,1)S(1)}, bf16[24,4096]{1,0:T(8,128)(2,1)S(1)}, u32[]{:S(2)}, u32[]{:S(2)}) collective-permute-start(bf16[24,4096]{1,0:T(8,128)(2,1)S(1)} %collective-permute-done.refs_1_), channel_id=1, source_target_pairs={{0,4},{4,8},{8,12},{12,28},{28,24},{24,20},{20,16},{16,0},{1,5},{5... | collective-permute-start | bytes 589832 | tf_op jit(solution)/shard_map/ppermute | solution.py:299
  11.7 5.8 %collective-permute-start.3 = (bf16[24,4096]{1,0:T(8,128)(2,1)S(1)}, bf16[24,4096]{1,0:T(8,128)(2,1)S(1)}, u32[]{:S(2)}, u32[]{:S(2)}) collective-permute-start(bf16[24,4096]{1,0:T(8,128)(2,1)S(1)} %collective-permute-done.1.refs_2_), channel_id=1, source_target_pairs={{0,16},{4,0},{8,4},{12,8},{28,12},{24,28},{20,24},{16,20},{1,17},{... | collective-permute-start | bytes 589832 | tf_op jit(solution)/shard_map/ppermute | solution.py:299
  16.0 7.0 %collective-permute-start.4 = (bf16[24,4096]{1,0:T(8,128)(2,1)S(1)}, bf16[24,4096]{1,0:T(8,128)(2,1)S(1)}, u32[]{:S(2)}, u32[]{:S(2)}) collective-permute-start(bf16[24,4096]{1,0:T(8,128)(2,1)S(1)} %collective-permute-done.2.refs_3_), channel_id=1, source_target_pairs={{0,4},{4,8},{8,12},{12,28},{28,24},{24,20},{20,16},{16,0},{1,5},{5... | collective-permute-start | bytes 589832 | tf_op jit(solution)/shard_map/ppermute | solution.py:299
  17.5 6.5 %collective-permute-start.5 = (bf16[24,4096]{1,0:T(8,128)(2,1)S(1)}, bf16[24,4096]{1,0:T(8,128)(2,1)S(1)}, u32[]{:S(2)}, u32[]{:S(2)}) collective-permute-start(bf16[24,4096]{1,0:T(8,128)(2,1)S(1)} %collective-permute-done.3.refs_4_), channel_id=1, source_target_pairs={{0,16},{4,0},{8,4},{12,8},{28,12},{24,28},{20,24},{16,20},{1,17},{... | collective-permute-start | bytes 589832 | tf_op jit(solution)/shard_map/ppermute | solution.py:299
  18.0 8.2 %collective-permute-start.6 = (bf16[24,2560]{1,0:T(8,128)(2,1)S(1)}, bf16[24,2560]{1,0:T(8,128)(2,1)S(1)}, u32[]{:S(2)}, u32[]{:S(2)}) collective-permute-start(bf16[24,2560]{1,0:T(8,128)(2,1)S(1)} %slice.16), channel_id=1, source_target_pairs={{0,8},{4,12},{8,28},{12,24},{28,20},{24,16},{20,0},{16,4},{1,9},{5... | collective-permute-start | bytes 368648 | tf_op jit(solution)/shard_map/ppermute | solution.py:299
  20.6 5.6 %collective-permute-start.7 = (bf16[24,1536]{1,0:T(8,128)(2,1)S(1)}, bf16[24,1536]{1,0:T(8,128)(2,1)S(1)}, u32[]{:S(2)}, u32[]{:S(2)}) collective-permute-start(bf16[24,1536]{1,0:T(8,128)(2,1)S(1)} %slice.17), channel_id=1, source_target_pairs={{0,20},{4,16},{8,0},{12,4},{28,8},{24,12},{20,28},{16,24},{1,21},{... | collective-permute-start | bytes 221192 | tf_op jit(solution)/shard_map/ppermute | solution.py:299
  24.6 4.6 %collective-permute-start.8 = (bf16[168,256]{1,0:T(8,128)(2,1)S(1)}, bf16[168,256]{1,0:T(8,128)(2,1)S(1)}, u32[]{:S(2)}, u32[]{:S(2)}) collective-permute-start(bf16[168,256]{1,0:T(8,128)(2,1)S(1)} %score.3), channel_id=1, source_target_pairs={{0,2},{2,0},{1,3},{3,1},{4,6},{6,4},{5,7},{7,5},{8,10},{10,8},{9,1... | collective-permute-start | bytes 258056 | tf_op jit(solution)/shard_map/ppermute | solution.py:234
  26.7 3.7 %collective-permute-start.9 = (bf16[24,256]{1,0:T(8,128)(2,1)S(1)}, bf16[24,256]{1,0:T(8,128)(2,1)S(1)}, u32[]{:S(2)}, u32[]{:S(2)}) collective-permute-start(bf16[24,256]{1,0:T(8,128)(2,1)S(1)} %score.5), channel_id=1, source_target_pairs={{0,2},{2,0},{1,3},{3,1},{4,6},{6,4},{5,7},{7,5},{8,10},{10,8},{9,1... | collective-permute-start | bytes 36872 | tf_op jit(solution)/shard_map/ppermute | solution.py:234
